TPU v7x, 256 devices: a whole 4x4x8 slice. The times are simulated.
256 devices in a mesh: feat: 64 (over y, z, core), ex: 4 (over x).
Axes of the slice: x: 4, y: 4, z: 8, core: 2. Of those that a mesh axis runs over, the one named last changes fastest.
Arguments:
- examples: bfloat16 [4096, 262144], P('ex', 'feat'), may hold values from -6 to 6
- weights: bfloat16 [262144], P('feat'), may hold values from -0.01171875 to 0.01171875
- labels: int32 [4096], P('ex'), may hold values from 0 to 1
- split: int32 [4096], P('ex'), may hold values 0 or 1
- val_weight: float32 [32, 4096], P(None, 'ex'), may hold values from 0.1 to 10
- strengths: float32 [256], replicated, may hold values from 0.05 to 1
- block_ids: int32 [262144], P('feat'), may hold values from 0 to 255
Outputs:
- solve: float32 [32, 262144], P(None, ('feat', 'ex'))
- hypergrad: float32 [32, 256], P(None, ('feat', 'ex'))
All inputs are finite; a program needn't handle non-finite values. No bound on the sum of `split` on one device may be relied on, other than what follows from the above.
Results may differ from a plain program's by a relative error of at most 0.0029.
Values may be sent and summed in bfloat16 or wider, within the bound.
No kernel may reach another device: no remote copies, remote signals or barrier semaphores. Data moves between devices by JAX's collectives and lax.ppermute only.
A program may use at most 64 MiB of HBM per device.

v0:
```python
import jax
import jax.numpy as jnp
from jax import lax
from jax.sharding import PartitionSpec as P


def from_everyone(array, axis):
    length = lax.axis_size(axis)
    return lax.all_to_all(
        jnp.broadcast_to(array[None], (length, *array.shape)), axis, 0, 0, tiled=True
    )


def over_copies(array, axis):
    everything = from_everyone(array, axis)
    return jnp.sum(everything, axis=0)


def split_up(array, dim, length):
    lengths = array.shape
    parts = array.reshape(*lengths[:dim], length, lengths[dim] // length, *lengths[dim + 1 :])
    return jnp.moveaxis(parts, dim, 0)


def sum_at_owner(array, axis, dim):
    parts = split_up(array, dim, lax.axis_size(axis))
    arrived = lax.all_to_all(parts, axis, split_axis=0, concat_axis=0, tiled=True)
    return arrived.sum(axis=0)


def rows_for(lines, length):
    spare = -len(lines) % length
    return jnp.pad(lines, [(0, spare)] + [(0, 0)] * (lines.ndim - 1))


def in_order(parts, dim):
    parts = jnp.moveaxis(parts, 0, dim)
    lengths = parts.shape
    return parts.reshape(*lengths[:dim], lengths[dim] * lengths[dim + 1], *lengths[dim + 2 :])


def gathered_copies(array, axis, dim):
    parts = from_everyone(array, axis)
    return in_order(parts, dim)


def total_of(array, axes):
    lines = array.reshape(-1)
    own = sum_at_owner(rows_for(lines, lax.axis_size(axes)), axes, 0)
    whole = gathered_copies(own, axes, 0)
    return whole[: len(lines)].reshape(array.shape)


def shards(examples, weights, labels, split, val_weight, strengths, block_ids):
    n_ex = lax.axis_size("ex")
    n_feat = lax.axis_size("feat")
    ex_pos = lax.axis_index("ex")
    feat_pos = lax.axis_index("feat")
    total = examples.shape[0] * n_ex
    width = examples.shape[1]
    share = width // n_ex
    blocks = strengths.shape[0]
    nb_local = blocks // (n_feat * n_ex)
    margin = over_copies(jnp.dot(examples, weights, preferred_element_type=jnp.float32), "feat")
    prob = 1.0 / (1.0 + jnp.exp(-margin))
    train = split.astype(jnp.float32)
    curvew = train * prob * (1.0 - prob)
    err = (1.0 - train) * (prob - labels.astype(jnp.float32))
    gradw = (val_weight * err[None, :] / jnp.sqrt(jnp.float32(total))).astype(jnp.bfloat16)
    grad_part = jnp.dot(gradw, examples, preferred_element_type=jnp.float32)
    onehot = (block_ids[:, None] == jnp.arange(blocks, dtype=jnp.int32)[None, :]).astype(
        jnp.float32
    )
    lamf = jnp.dot(onehot, strengths, precision=lax.Precision.HIGHEST)
    wfloat = weights.astype(jnp.float32)
    rhs = over_copies(grad_part, "ex")

    def norm_sum(vec):
        return over_copies(jnp.sum(vec * vec, axis=1), "feat")

    solve = jnp.zeros_like(rhs)
    resid = rhs
    direc = rhs
    norm_now = norm_sum(resid)
    for step in range(2):
        tang = lax.dot_general(
            direc.astype(jnp.bfloat16),
            examples,
            (((1,), (1,)), ((), ())),
            preferred_element_type=jnp.float32,
        )
        tang = total_of(tang, "feat")
        wtang = (curvew[None, :] * tang).astype(jnp.bfloat16)
        prod = over_copies(jnp.dot(wtang, examples, preferred_element_type=jnp.float32), "ex")
        image = prod / jnp.float32(total) + lamf[None, :] * direc
        alpha = norm_now / over_copies(jnp.sum(direc * image, axis=1), "feat")
        solve = solve + alpha[:, None] * direc
        resid = resid - alpha[:, None] * image
        if step == 0:
            norm_next = norm_sum(resid)
            direc = resid + (norm_next / norm_now)[:, None] * direc
            norm_now = norm_next
    partial_blocks = jnp.dot(solve * wfloat[None, :], onehot, precision=lax.Precision.HIGHEST)
    feat_sums = sum_at_owner(partial_blocks, "feat", 1)
    block_sums = lax.dynamic_slice_in_dim(feat_sums, ex_pos * nb_local, nb_local, 1)
    solve_out = lax.dynamic_slice_in_dim(solve, ex_pos * share, share, 1)
    own = lax.dynamic_slice_in_dim(strengths, (feat_pos * n_ex + ex_pos) * nb_local, nb_local, 0)
    return (solve_out, -own[None, :] * block_sums)


def solution(mesh):
    placed = (P("ex", "feat"), P("feat"), P("ex"), P("ex"), P(None, "ex"), P(), P("feat"))
    return jax.shard_map(
        shards,
        mesh=mesh,
        in_specs=placed,
        out_specs=(P(None, ("feat", "ex")), P(None, ("feat", "ex"))),
        check_vma=False,
    )
```

profile of v0, /device:TPU:1, one launch (start us, length us, event | category | flops | bytes accessed | tf_op | source)
XLA Modules:
  0.0 294.6 jit_solution(6493765755535580545)
XLA Ops:
  0.7 0.7 reshape.91
  1.4 5.6 %fusion.18 = f32[1,1024]{1,0:T(1,128)S(1)} fusion(bf16[1024,4096]{1,0:T(8,128)(2,1)} %param.7, bf16[4096,1]{0,1:T(2,128)(2,1)S(1)} %reshape.91), kind=kOutput, calls=%fused_computation.36 | convolution fusion | flops 8388608 | bytes 8400896 | tf_op jit(solution)/shard_map/dot_general | solution.py:64
  7.1 0.1 broadcast_in_dim.20
  7.2 25.0 %all_to_all.82 = f32[64,1,1024]{2,1,0:T(1,128)S(1)} all-to-all(f32[64,1,1024]{2,1,0:T(1,128)S(1)} %broadcast_in_dim.20), channel_id=1, replica_groups=mesh['feat'=64,'ex'=4] {'feat'}, dimensions={0} | all-to-all | bytes 524288 | tf_op jit(solution)/shard_map/all_to_all | solution.py:9
  32.2 0.2 reduce_sum.135
  32.4 4.9 %fusion.10 = f32[32,4096]{1,0:T(8,128)S(1)} fusion(bf16[1024,4096]{1,0:T(8,128)(2,1)} %param.7, f32[32,1024]{1,0:T(8,128)S(1)} %copy-done, f32[1024]{0:T(1024)S(1)} %get-tuple-element.5), kind=kOutput, calls=%fused_computation.22 | convolution fusion | flops 268533760 | bytes 9048064 | tf_op jit(solution)/shard_map/dot_general | solution.py:70
  37.3 0.2 broadcast_in_dim.21
  37.5 29.2 %all_to_all.83 = f32[4,32,4096]{2,1,0:T(8,128)S(1)} all-to-all(f32[4,32,4096]{2,1,0:T(8,128)S(1)} %broadcast_in_dim.21), channel_id=1, replica_groups=mesh['feat'=64,'ex'=4] {'ex'}, dimensions={0} | all-to-all | bytes 4194304 | tf_op jit(solution)/shard_map/all_to_all | solution.py:9
  66.9 6.0 %fusion.8 = f32[32,1024]{1,0:T(8,128)S(1)} fusion(bf16[1024,4096]{1,0:T(8,128)(2,1)} %param.7, f32[32,4096]{1,0:T(8,128)S(1)} %reduce_sum.136), kind=kOutput, calls=%fused_computation.17 | convolution fusion | flops 268566528 | bytes 9043968 | tf_op jit(solution)/shard_map/dot_general | solution.py:86
  72.8 0.2 all_to_all.67
  73.0 17.5 %all_to_all.84 = f32[64,1,512]{2,1,0:T(1,128)S(1)} all-to-all(f32[64,1,512]{2,1,0:T(1,128)S(1)} %all_to_all.67), channel_id=1, replica_groups=mesh['feat'=64,'ex'=4] {'feat'}, dimensions={0} | all-to-all | bytes 262144 | tf_op jit(solution)/shard_map/all_to_all | solution.py:27
  90.7 15.0 %all_to_all.85 = f32[64,1,512]{2,1,0:T(1,128)S(1)} all-to-all(f32[64,1,512]{2,1,0:T(1,128)S(1)} %broadcast_in_dim.23), channel_id=1, replica_groups=mesh['feat'=64,'ex'=4] {'feat'}, dimensions={0} | all-to-all | bytes 262144 | tf_op jit(solution)/shard_map/all_to_all | solution.py:9
  105.8 0.3 reduce.7
  106.2 4.9 %fusion.11 = f32[32,4096]{1,0:T(8,128)S(1)} fusion(bf16[1024,4096]{1,0:T(8,128)(2,1)} %param.7, f32[32,1024]{1,0:T(8,128)S(1)} %reshape_reshape.6, f32[1024]{0:T(1024)S(1)} %get-tuple-element.4), kind=kOutput, calls=%fused_computation.23 | convolution fusion | flops 268500992 | bytes 9048064 | tf_op jit(solution)/shard_map/dot_general | solution.py:94
  111.1 1.6 broadcast_in_dim.24
  112.7 3.6 %all-to-all-start.5 = ((f32[4,32,4096]{2,1,0:T(8,128)}), f32[4,32,4096]{2,1,0:T(8,128)S(1)}, u32[]{:S(2)}, u32[]{:S(2)}) async-start(f32[4,32,4096]{2,1,0:T(8,128)} %broadcast_in_dim.24), calls=%async_computation.5 | async-start | bytes 4194304 | tf_op jit(solution)/shard_map/all_to_all | solution.py:9
  116.3 2.1 fusion.1
  118.4 23.9 %all-to-all-done.5 = f32[4,32,4096]{2,1,0:T(8,128)S(1)} async-done(((f32[4,32,4096]{2,1,0:T(8,128)}), f32[4,32,4096]{2,1,0:T(8,128)S(1)}, u32[]{:S(2)}, u32[]{:S(2)}) %all-to-all-start.5) | async-done | bytes 2097184 | tf_op jit(solution)/shard_map/all_to_all | solution.py:9
  142.4 0.3 multiply_reduce_fusion.2
  142.7 14.7 %all_to_all.86 = f32[64,1,32]{2,1,0:T(1,128)S(1)} all-to-all(f32[64,1,32]{2,1,0:T(1,128)S(1)} %broadcast_in_dim.22), channel_id=1, replica_groups=mesh['feat'=64,'ex'=4] {'feat'}, dimensions={0} | all-to-all | bytes 16384 | tf_op jit(solution)/shard_map/all_to_all | solution.py:9
  157.4 0.6 broadcast_in_dim.25
  158.1 4.7 %all-to-all-start.6 = ((f32[64,1,32]{2,1,0:T(1,128)}), f32[64,1,32]{2,1,0:T(1,128)S(1)}, u32[]{:S(2)}, u32[]{:S(2)}) async-start(f32[64,1,32]{2,1,0:T(1,128)} %broadcast_in_dim.25), calls=%async_computation.6 | async-start | bytes 65536 | tf_op jit(solution)/shard_map/all_to_all | solution.py:9
  162.8 9.2 %all-to-all-done.6 = f32[64,1,32]{2,1,0:T(1,128)S(1)} async-done(((f32[64,1,32]{2,1,0:T(1,128)}), f32[64,1,32]{2,1,0:T(1,128)S(1)}, u32[]{:S(2)}, u32[]{:S(2)}) %all-to-all-start.6) | async-done | bytes 8224 | tf_op jit(solution)/shard_map/all_to_all | solution.py:9
  172.2 0.3 multiply_reduce_fusion.1
  172.5 13.3 %all_to_all.87 = f32[64,1,32]{2,1,0:T(1,128)S(1)} all-to-all(f32[64,1,32]{2,1,0:T(1,128)S(1)} %broadcast_in_dim.26), channel_id=1, replica_groups=mesh['feat'=64,'ex'=4] {'feat'}, dimensions={0} | all-to-all | bytes 16384 | tf_op jit(solution)/shard_map/all_to_all | solution.py:9
  185.9 6.0 %fusion.6 = f32[32,1024]{1,0:T(8,128)S(1)} fusion(bf16[1024,4096]{1,0:T(8,128)(2,1)} %param.7, f32[32,4096]{1,0:T(8,128)S(1)} %reduce_sum.136, f32[32,4096]{1,0:T(8,128)S(1)} %reduce_sum.140, f32[32]{0:T(128)S(1)} %div.41, f32[32]{0:T(128)S(1)} %div.40, f32[4096]{0:T(1024)S(1)} %bitcast.20), kind=kOutput, calls=%fused_computation.15 | convolution fusion | flops 269484032 | bytes 9584896 | tf_op jit(solution)/shard_map/dot_general | solution.py:86
  191.8 0.2 all_to_all.68
  192.0 14.4 %all_to_all.88 = f32[64,1,512]{2,1,0:T(1,128)S(1)} all-to-all(f32[64,1,512]{2,1,0:T(1,128)S(1)} %all_to_all.68), channel_id=1, replica_groups=mesh['feat'=64,'ex'=4] {'feat'}, dimensions={0} | all-to-all | bytes 262144 | tf_op jit(solution)/shard_map/all_to_all | solution.py:27
  206.6 15.0 %all_to_all.89 = f32[64,1,512]{2,1,0:T(1,128)S(1)} all-to-all(f32[64,1,512]{2,1,0:T(1,128)S(1)} %broadcast_in_dim.27), channel_id=1, replica_groups=mesh['feat'=64,'ex'=4] {'feat'}, dimensions={0} | all-to-all | bytes 262144 | tf_op jit(solution)/shard_map/all_to_all | solution.py:9
  221.6 0.3 reduce.8
  222.0 4.9 %fusion.12 = f32[32,4096]{1,0:T(8,128)S(1)} fusion(bf16[1024,4096]{1,0:T(8,128)(2,1)} %param.7, f32[32,1024]{1,0:T(8,128)S(1)} %reshape_reshape.7, f32[1024]{0:T(1024)S(1)} %get-tuple-element.4), kind=kOutput, calls=%fused_computation.24 | convolution fusion | flops 268500992 | bytes 9048064 | tf_op jit(solution)/shard_map/dot_general | solution.py:94
  226.9 0.2 broadcast_in_dim.28
  227.1 28.5 %all_to_all.90 = f32[4,32,4096]{2,1,0:T(8,128)S(1)} all-to-all(f32[4,32,4096]{2,1,0:T(8,128)S(1)} %broadcast_in_dim.28), channel_id=1, replica_groups=mesh['feat'=64,'ex'=4] {'ex'}, dimensions={0} | all-to-all | bytes 4194304 | tf_op jit(solution)/shard_map/all_to_all | solution.py:9
  255.6 0.9 reduce_sum.146
  256.6 1.4 multiply_reduce_fusion
  258.0 0.6 broadcast_in_dim.29
  258.6 5.6 %all-to-all-start.11 = ((f32[64,1,32]{2,1,0:T(1,128)}), f32[64,1,32]{2,1,0:T(1,128)S(1)}, u32[]{:S(2)}, u32[]{:S(2)}) async-start(f32[64,1,32]{2,1,0:T(1,128)} %broadcast_in_dim.29), calls=%async_computation.11 | async-start | bytes 65536 | tf_op jit(solution)/shard_map/all_to_all | solution.py:9
  264.3 0.6 dynamic_slice.10
  265.5 7.9 %all-to-all-done.11 = f32[64,1,32]{2,1,0:T(1,128)S(1)} async-done(((f32[64,1,32]{2,1,0:T(1,128)}), f32[64,1,32]{2,1,0:T(1,128)S(1)}, u32[]{:S(2)}, u32[]{:S(2)}) %all-to-all-start.11) | async-done | bytes 8224 | tf_op jit(solution)/shard_map/all_to_all | solution.py:9
  273.5 0.2 multiply_add_fusion
  273.8 4.0 %fusion = f32[32,256]{0,1:T(8,128)S(1)} fusion(s32[4096]{0:T(1024)S(1)} %copy-done.4, f32[32,4096]{1,0:T(8,128)S(1)} %multiply_add_fusion, f32[4096]{0:T(1024)S(1)} %convert_element_type.32), kind=kOutput, calls=%fused_computation.1 | convolution fusion | flops 403832832 | bytes 589824 | tf_op jit(solution)/shard_map/dot_general | solution.py:103
  277.7 0.7 reshape.97
  278.5 4.7 %all-to-all-start.12 = ((f32[64,1,128]{2,1,0:T(1,128)}), f32[64,1,128]{2,1,0:T(1,128)S(1)}, u32[]{:S(2)}, u32[]{:S(2)}) async-start(f32[64,1,128]{2,1,0:T(1,128)} %reshape.97), calls=%async_computation.12 | async-start | bytes 65536 | tf_op jit(solution)/shard_map/all_to_all | solution.py:27
  283.2 0.7 constant_dynamic-slice_fusion
  283.9 8.7 %all-to-all-done.12 = f32[64,1,128]{2,1,0:T(1,128)S(1)} async-done(((f32[64,1,128]{2,1,0:T(1,128)}), f32[64,1,128]{2,1,0:T(1,128)S(1)}, u32[]{:S(2)}, u32[]{:S(2)}) %all-to-all-start.12) | async-done | bytes 32800 | tf_op jit(solution)/shard_map/all_to_all | solution.py:27
  292.6 0.5 broadcast.61
  293.1 0.7 reduce.9
  294.0 0.5 dynamic-slice_multiply_fusion
  (33 shorter events, 1.4 us)
Async XLA Ops:
  0.6 31.7 %copy-start.2 = (s32[1024]{0:T(1024)S(1)}, s32[1024]{0:T(1024)}, u32[]{:S(2)}) copy-start(s32[1024]{0:T(1024)} %param.10) | copy-start | bytes 12292
  0.6 31.7 %copy-start.3 = (s32[1024]{0:T(1024)S(1)}, s32[1024]{0:T(1024)}, u32[]{:S(2)}) copy-start(s32[1024]{0:T(1024)} %param.9) | copy-start | bytes 12292
  0.7 31.7 %copy-start = (f32[32,1024]{1,0:T(8,128)S(1)}, f32[32,1024]{1,0:T(8,128)}, u32[]{:S(2)}) copy-start(f32[32,1024]{1,0:T(8,128)} %param.11) | copy-start | bytes 393220
  106.1 10.1 %copy-start.4 = (s32[4096]{0:T(1024)S(1)}, s32[4096]{0:T(1024)}, u32[]{:S(2)}) copy-start(s32[4096]{0:T(1024)} %param.13) | copy-start | bytes 49156
  106.1 10.1 %copy-start.5 = (f32[256]{0:T(256)S(1)}, f32[256]{0:T(256)}, u32[]{:S(2)}) copy-start(f32[256]{0:T(256)} %param.12) | copy-start | bytes 3076
  112.7 29.6 %all-to-all-start.5 = ((f32[4,32,4096]{2,1,0:T(8,128)}), f32[4,32,4096]{2,1,0:T(8,128)S(1)}, u32[]{:S(2)}, u32[]{:S(2)}) async-start(f32[4,32,4096]{2,1,0:T(8,128)} %broadcast_in_dim.24), calls=%async_computation.5 | async-start | bytes 4194304 | tf_op jit(solution)/shard_map/all_to_all | solution.py:9
  158.1 14.0 %all-to-all-start.6 = ((f32[64,1,32]{2,1,0:T(1,128)}), f32[64,1,32]{2,1,0:T(1,128)S(1)}, u32[]{:S(2)}, u32[]{:S(2)}) async-start(f32[64,1,32]{2,1,0:T(1,128)} %broadcast_in_dim.25), calls=%async_computation.6 | async-start | bytes 65536 | tf_op jit(solution)/shard_map/all_to_all | solution.py:9
  226.9 37.3 %copy-start.1 = (bf16[4096]{0:T(1024)(128)(2,1)S(1)}, bf16[4096]{0:T(1024)(128)(2,1)}, u32[]{:S(2)}) copy-start(bf16[4096]{0:T(1024)(128)(2,1)} %param.8) | copy-start | bytes 24580
  258.6 14.8 %all-to-all-start.11 = ((f32[64,1,32]{2,1,0:T(1,128)}), f32[64,1,32]{2,1,0:T(1,128)S(1)}, u32[]{:S(2)}, u32[]{:S(2)}) async-start(f32[64,1,32]{2,1,0:T(1,128)} %broadcast_in_dim.29), calls=%async_computation.11 | async-start | bytes 65536 | tf_op jit(solution)/shard_map/all_to_all | solution.py:9
  278.5 14.1 %all-to-all-start.12 = ((f32[64,1,128]{2,1,0:T(1,128)}), f32[64,1,128]{2,1,0:T(1,128)S(1)}, u32[]{:S(2)}, u32[]{:S(2)}) async-start(f32[64,1,128]{2,1,0:T(1,128)} %reshape.97), calls=%async_computation.12 | async-start | bytes 65536 | tf_op jit(solution)/shard_map/all_to_all | solution.py:27
where the time goes:
time: 295 us
  blocking collectives  173 us (59%)
  waiting for transfers between devices  49.8 us (17%)
  matrix products  38.4 us (13%)
  starting transfers between devices  18.6 us (6%)
  local copies, waits for them, and re-layouts  7.42 us (3%)
  other arithmetic  6.07 us (2%)
    all_to_all x7, blocking collectives, from_everyone(): lax.all_to_all(jnp.broadcast_to(array[None], (length, *array.shape)), axi...  141 us
    all_to_all x3, waiting for transfers between devices, from_everyone(): lax.all_to_all(jnp.broadcast_to(array[None], (length, *array.shape)), axi...  41.1 us
    all_to_all x2, blocking collectives, sum_at_owner(): lax.all_to_all(parts, axis, split_axis=0, concat_axis=0, tiled=True)  31.9 us
    all_to_all x3, starting transfers between devices, from_everyone(): lax.all_to_all(jnp.broadcast_to(array[None], (length, *array.shape)), axi...  13.9 us
    dot_general x2, matrix products, shards(): lax.dot_general(direc.astype(jnp.bfloat16), examples, (((1,), (1,)), ((),...  11.9 us
    dot_general x2, matrix products, shards(): jnp.dot(wtang, examples, preferred_element_type=jnp.float32)  9.85 us
    all_to_all x1, waiting for transfers between devices, sum_at_owner(): lax.all_to_all(parts, axis, split_axis=0, concat_axis=0, tiled=True)  8.72 us
  transfers between devices with their start and end apart: 4, of which 4 were waited for; matrix products, arithmetic and copies ran while one was open for 1% of the time, Pallas kernels for 0%

commit v1 on v0

v1 whole, which is shorter than its diff:
```python
import functools

import jax
import jax.numpy as jnp
from jax import lax
from jax.experimental import pallas as pl
from jax.experimental.pallas import tpu as pltpu
from jax.sharding import Mesh
from jax.sharding import PartitionSpec as P

F32 = jnp.float32
BF16 = jnp.bfloat16
NT = (((1,), (1,)), ((), ()))
NY, NZ, NC, NX = 4, 8, 2, 4
R = 32
N = 1024
HALF = N // NC
W = 4096
OWN = W // NX
NB = 256
TOTAL = float(N * NX)
LANES = 128
VMEM = pl.BlockSpec(memory_space=pltpu.VMEM)
SMEM = pl.BlockSpec(memory_space=pltpu.SMEM)


def call(body, outs, *arrays, scratch=(), limit=16, smem=()):
    return pl.pallas_call(
        body,
        out_shape=outs,
        in_specs=[SMEM if i in smem else VMEM for i in range(len(arrays))],
        out_specs=jax.tree.map(lambda _: VMEM, outs),
        scratch_shapes=scratch,
        compiler_params=pltpu.CompilerParams(vmem_limit_bytes=limit << 20),
    )(*arrays)


def shape(*dims, dtype=F32):
    return jax.ShapeDtypeStruct(dims, dtype)


def lane_ids(lanes=LANES):
    return lax.broadcasted_iota(jnp.int32, (R, lanes), 1)


def column(tile, lane):
    return jnp.sum(jnp.where(lane_ids(tile.shape[1]) == lane, tile, 0.0), axis=1, keepdims=True)


def columns(values, first=0):
    lanes = lane_ids()
    tile = jnp.zeros((R, LANES), F32)
    for i, value in enumerate(values):
        tile = jnp.where(lanes == first + i, value, tile)
    return tile


def terms(value, count):
    found = []
    for _ in range(count):
        term = value.astype(BF16).astype(F32)
        found.append(term)
        value = value - term
    return found


def packed(values):
    return columns([term for value in values for term in terms(value, 3)])


def unpacked(tile, index):
    lanes = lane_ids()
    inside = (lanes >= 3 * index) & (lanes < 3 * index + 3)
    return jnp.sum(jnp.where(inside, tile, 0.0), axis=1, keepdims=True)


def chunk(index, size):
    return pl.ds(pl.multiple_of(index * size, size), size)


def block_sums(vec, weight, onehot):
    parts = jnp.concatenate(terms(vec * weight, 3), axis=0).astype(BF16)
    sums = lax.dot_general(parts, onehot, NT, preferred_element_type=F32)
    return sums[:R] + sums[R : 2 * R] + sums[2 * R :]


def prepare(ids, strengths, place, lamf, onehot):
    kinds = lax.broadcasted_iota(jnp.int32, (NB, OWN), 0)
    rows = lax.broadcasted_iota(jnp.int32, (16, NB), 0)
    value = strengths[...]
    split3 = jnp.zeros((16, NB), F32)
    for i, term in enumerate(terms(value, 3)):
        split3 = jnp.where(rows == i, term, split3)
    split3 = split3.astype(BF16)
    for j in range(NX):
        hot = (kinds == ids[:, j * OWN : (j + 1) * OWN]).astype(F32).astype(BF16)
        found = jnp.dot(split3, hot, preferred_element_type=F32)
        lamf[:, j * OWN : (j + 1) * OWN] = found[0:1] + found[1:2] + found[2:3]
    own = ids[:, chunk(place[3], OWN)]
    core = lax.shift_right_logical(own, 2) & 1
    moved = core * 128 + lax.shift_right_logical(own, 3) * 4 + (own & 3)
    onehot[...] = (kinds == moved).astype(F32).astype(BF16)


def margins(examples, weights, margin):
    for i in range(8):
        rows = lax.dot_general(
            weights[...], examples[i * 128 : (i + 1) * 128, :], NT, preferred_element_type=F32
        )
        margin[i : i + 1, :] = rows[0:1]


def gradients(margin_parts, labels, split, val_weight, examples, part, curvew):
    whole = jnp.sum(margin_parts[...], axis=0)
    margin = jnp.concatenate([whole[i : i + 1] for i in range(8)], axis=1)
    prob = 1.0 / (1.0 + jnp.exp(-margin))
    train = split[...].astype(F32)
    curvew[...] = train * prob * (1.0 - prob)
    err = (1.0 - train) * (prob - labels[...].astype(F32))
    gradw = (val_weight[...] * err / jnp.sqrt(F32(TOTAL))).astype(BF16)
    for j in range(NX):

        def step(i, _, j=j):
            at = chunk(i, 256)
            cols = pl.ds(pl.multiple_of(j * OWN + i * 256, 256), 256)
            part[j, :, at] = jnp.dot(gradw, examples[:, cols], preferred_element_type=F32)
            return 0

        lax.fori_loop(0, OWN // 256, step, 0)


def start_rhs(arrived, rhs, low):
    total = jnp.sum(arrived[...], axis=0)
    rhs[...] = total
    low[...] = total.astype(BF16)


def rhs_sums(rhs, lamf, wfloat, onehot, place, sums):
    own = chunk(place[3], OWN)
    vec = rhs[...]
    norm = jnp.sum(vec * vec, axis=1, keepdims=True)
    scaled = jnp.sum(lamf[:, own] * vec * vec, axis=1, keepdims=True)
    sums[:, :LANES] = columns([norm, scaled])
    sums[:, LANES:] = block_sums(vec, wfloat[:, own], onehot[...])


def tangents(pieces, examples, x, tang):
    def step(i, _):
        rows = chunk(i, 256)
        total = None
        for s, piece in enumerate(pieces):
            cols = chunk((x - s + NX) % NX, OWN)
            term = lax.dot_general(
                piece[...], examples[rows, cols], NT, preferred_element_type=F32
            )
            total = term if total is None else total + term
        tang[:, rows] = total
        return 0

    lax.fori_loop(0, N // 256, step, 0)


def halves(tang, scalars, blocks, core, keep, send):
    for out, which in ((keep, core), (send, 1 - core)):
        out[:, :HALF] = tang[:, chunk(which, HALF)]
        out[:, HALF : HALF + LANES] = scalars
        out[:, HALF + LANES :] = blocks[:, chunk(which, LANES)]


def first_tangents(low0, low1, low2, low3, examples, sums, place, keep, send, tang, blocks):
    tangents([low0, low1, low2, low3], examples, place[3], tang)
    blocks[...] = sums[:, LANES:]
    halves(tang, sums[:, :LANES], blocks, place[2], keep, send)


def to_wire(keep, arrived, wire):
    total = keep[...] + arrived[...]
    wire[:, :HALF] = total[:, :HALF].astype(BF16)
    scalars = total[:, HALF : HALF + LANES]
    wire[:, HALF : HALF + LANES] = packed([column(scalars, i) for i in range(3)]).astype(BF16)
    high, rest = terms(total[:, HALF + LANES :], 2)
    wire[:, HALF + LANES : HALF + 2 * LANES] = high.astype(BF16)
    wire[:, HALF + 2 * LANES :] = rest.astype(BF16)


def along_y(wire0, wire1, wire2, wire3, place, out):
    total = wire0[...].astype(F32)
    for wire in (wire1, wire2, wire3):
        total = total + wire[...].astype(F32)
    tang = total[:, :HALF].astype(BF16)
    scalars = total[:, HALF : HALF + LANES]
    tile = packed([unpacked(scalars, i) for i in range(3)])
    blocks = total[:, HALF + LANES : HALF + 2 * LANES] + total[:, HALF + 2 * LANES :]
    lanes = lane_ids()
    at64 = pltpu.roll(blocks, (64 - 32 * place[0] + LANES) % LANES, 1)
    at96 = pltpu.roll(blocks, (96 - 32 * place[0] + LANES) % LANES, 1)
    tile = jnp.where((lanes >= 64) & (lanes < 96), terms(at64, 1)[0], tile)
    tile = jnp.where(lanes >= 96, terms(at96, 2)[1], tile)
    tile = tile.astype(BF16)
    for i in range(NZ):
        out[i, :, :HALF] = tang
        out[i, :, HALF:] = tile


def along_z(arrived):
    tang = arrived[0, :, :HALF].astype(F32)
    tile = arrived[0, :, HALF:].astype(F32)
    for i in range(1, NZ):
        tang = tang + arrived[i, :, :HALF].astype(F32)
        tile = tile + arrived[i, :, HALF:].astype(F32)
    scalars = [unpacked(tile, i) for i in range(3)]
    blocks = pltpu.roll(tile, 64, 1) + pltpu.roll(tile, 32, 1)
    return tang, scalars, jnp.where(lane_ids() < 32, blocks, 0.0)


def weigh(arrived, curvew, place, tang_out, weighted, kept):
    tang, (norm, scaled, _), blocks = along_z(arrived)
    tang_out[...] = tang
    half = curvew[:, chunk(place[2], HALF)]
    product = half * tang
    curv = jnp.sum(product * tang, axis=1, keepdims=True)
    weighted[:, :HALF] = product.astype(BF16)
    weighted[:, HALF:] = packed([curv]).astype(BF16)
    kept[:, :LANES] = columns([norm, scaled, curv])
    kept[:, LANES:] = blocks


def products(weighted, other, kept, examples, place, part):
    core = place[2]

    def step(i, _):
        cols = chunk(i, 256)
        mine = jnp.dot(
            weighted[:, :HALF], examples[chunk(core, HALF), cols], preferred_element_type=F32
        )
        rest = jnp.dot(
            other[:, :HALF], examples[chunk(1 - core, HALF), cols], preferred_element_type=F32
        )
        part[:, cols] = (mine + rest).astype(BF16)
        return 0

    lax.fori_loop(0, W // 256, step, 0)
    tile = kept[:, :LANES]
    curv = column(tile, 2) + unpacked(other[:, HALF:].astype(F32), 0)
    part[:, W:] = packed([column(tile, 0), column(tile, 1), curv]).astype(BF16)


def second_tangents(
    part0, part1, part2, part3, rhs, low1, low2, low3, examples, lamf, wfloat, onehot, place,
    resid, keep, send, kept, tang, blocks, pieces,
):
    x = place[3]
    parts = (part0, part1, part2, part3)
    tile = sum(p[:, W:].astype(F32) for p in parts)
    norm, scaled, curv = (unpacked(tile, i) for i in range(3))
    alpha = norm / (curv / F32(TOTAL) + scaled)
    kept[...] = columns([alpha, norm, scaled, curv])
    for s, vec in enumerate((rhs, low1, low2, low3)):
        cols = chunk((x - s + NX) % NX, OWN)
        total = sum(p[:, cols].astype(F32) for p in parts)
        direc = vec[...].astype(F32)
        lam = lamf[:, cols]
        left = direc - alpha * (total / F32(TOTAL) + lam * direc)
        pieces[s] = left.astype(BF16)
        if s == 0:
            resid[...] = left
            scalars = columns(
                [
                    jnp.sum(left * left, axis=1, keepdims=True),
                    jnp.sum(lam * left * left, axis=1, keepdims=True),
                    jnp.sum(lam * left * direc, axis=1, keepdims=True),
                ]
            )
            blocks[...] = block_sums(left, wfloat[:, cols], onehot[...])
    tangents([pieces.at[s] for s in range(NX)], examples, x, tang)
    halves(tang, scalars, blocks, place[2], keep, send)


def curvature(arrived, curvew, tang_first, kept, place, out):
    tang, (norm, scaled, mixed), blocks = along_z(arrived)
    half = curvew[:, chunk(place[2], HALF)]
    product = half * tang
    both = jnp.sum(product * tang, axis=1, keepdims=True)
    cross = jnp.sum(product * tang_first[...], axis=1, keepdims=True)
    tile = columns([both, cross, norm, scaled, mixed])
    lanes = lane_ids()
    shift = 4 * place[1]
    now = pltpu.roll(blocks, (32 - shift + LANES) % LANES, 1)
    before = pltpu.roll(kept[:, LANES:], (36 - shift + LANES) % LANES, 1)
    tile = jnp.where((lanes >= 32) & (lanes < 36), now, tile)
    tile = jnp.where((lanes >= 36) & (lanes < 40), before, tile)
    for i in range(NC * NX):
        out[i] = tile


def finish(arrived, kept, rhs, resid, strengths, place, solve, hyper):
    core, x = place[2], place[3]
    mine = sum(arrived[core * NX + i] for i in range(NX))
    rest = sum(arrived[(1 - core) * NX + i] for i in range(NX))
    every = mine + rest
    tile = kept[...]
    alpha, norm, scaled_first, curv_first = (column(tile, i) for i in range(4))
    both, cross = column(every, 0), column(every, 1)
    norm_next, scaled, mixed = (column(mine, i) for i in range(2, 5))
    beta = norm_next / norm
    curv = (both + 2.0 * beta * cross + beta * beta * curv_first) / F32(TOTAL)
    curv = curv + (scaled + 2.0 * beta * mixed + beta * beta * scaled_first)
    alpha_next = norm_next / curv
    first = rhs[...]
    solve[...] = alpha * first + alpha_next * (resid[...] + beta * first)
    now, before = column(mine, 32 + x), column(mine, 36 + x)
    block = ((place[0] * NZ + place[1]) * NC + core) * NX + x
    kinds = lax.broadcasted_iota(jnp.int32, (1, NB), 1)
    strength = jnp.sum(jnp.where(kinds == block, strengths[...], 0.0), axis=1, keepdims=True)
    hyper[...] = -strength * (alpha * before + alpha_next * (now + beta * before))


def shifted(array, axis, length):
    return [
        lax.ppermute(array, axis, [(i, (i + s) % length) for i in range(length)])
        for s in range(1, length)
    ]


def swapped(array):
    return lax.ppermute(array, "c", [(0, 1), (1, 0)])


def summed(keep, send, place):
    wire = call(to_wire, shape(R, HALF + 3 * LANES, dtype=BF16), keep, swapped(send))
    arrived = shifted(wire, "y", NY)
    out = call(
        along_y, shape(NZ, R, HALF + LANES, dtype=BF16), wire, *arrived, place, smem=(4,)
    )
    return lax.all_to_all(out, "z", 0, 0, tiled=True)


def shards(examples, weights, labels, split, val_weight, strengths, block_ids):
    place = jnp.stack([lax.axis_index(axis) for axis in ("y", "z", "c", "x")]).astype(jnp.int32)
    ids = block_ids.reshape(1, W)
    strengths = strengths.reshape(1, NB)
    wrows = jnp.broadcast_to(weights[None, :], (16, W))
    wfloat = weights.astype(F32).reshape(1, W)
    lamf, onehot = call(
        prepare, [shape(1, W), shape(NB, OWN, dtype=BF16)], ids, strengths, place, smem=(2,)
    )
    margin = call(margins, shape(8, 128), examples, wrows)
    margin = margin + swapped(margin)
    margin_parts = lax.all_to_all(
        jnp.broadcast_to(margin[None], (NY * NZ, 8, 128)), ("y", "z"), 0, 0, tiled=True
    )
    part, curvew = call(
        gradients,
        [shape(NX, R, OWN), shape(1, N)],
        margin_parts,
        labels.reshape(1, N),
        split.reshape(1, N),
        val_weight,
        examples,
    )
    arrived = lax.all_to_all(part, "x", 0, 0, tiled=True)
    rhs, low = call(start_rhs, [shape(R, OWN), shape(R, OWN, dtype=BF16)], arrived)
    lows = shifted(low, "x", NX)
    sums = call(rhs_sums, shape(R, LANES + NB), rhs, lamf, wfloat, onehot, place, smem=(4,))
    pair = [shape(R, HALF + 2 * LANES)] * 2
    keep, send = call(
        first_tangents,
        pair,
        low,
        *lows,
        examples,
        sums,
        place,
        scratch=[pltpu.VMEM((R, N), F32), pltpu.VMEM((R, NB), F32)],
        smem=(6,),
    )
    arrived = summed(keep, send, place)
    tang_first, weighted, kept_first = call(
        weigh,
        [shape(R, HALF), shape(R, HALF + LANES, dtype=BF16), shape(R, 2 * LANES)],
        arrived,
        curvew,
        place,
        smem=(2,),
    )
    part = call(
        products,
        shape(R, W + LANES, dtype=BF16),
        weighted,
        swapped(weighted),
        kept_first,
        examples,
        place,
        smem=(4,),
    )
    resid, keep, send, kept = call(
        second_tangents,
        [shape(R, OWN), *pair, shape(R, LANES)],
        part,
        *shifted(part, "x", NX),
        rhs,
        *lows,
        examples,
        lamf,
        wfloat,
        onehot,
        place,
        scratch=[
            pltpu.VMEM((R, N), F32),
            pltpu.VMEM((R, NB), F32),
            pltpu.VMEM((NX, R, OWN), BF16),
        ],
        smem=(12,),
    )
    arrived = summed(keep, send, place)
    out = call(
        curvature,
        shape(NC * NX, R, LANES),
        arrived,
        curvew,
        tang_first,
        kept_first,
        place,
        smem=(4,),
    )
    arrived = lax.all_to_all(out, ("c", "x"), 0, 0, tiled=True)
    return tuple(
        call(
            finish,
            [shape(R, OWN), shape(R, 1)],
            arrived,
            kept,
            rhs,
            resid,
            strengths,
            place,
            smem=(5,),
        )
    )


def solution(mesh):
    fine = Mesh(mesh.devices.reshape(NY, NZ, NC, NX), ("y", "z", "c", "x"))
    feat = ("y", "z", "c")
    placed = (P("x", feat), P(feat), P("x"), P("x"), P(None, "x"), P(), P(feat))
    return jax.shard_map(
        shards,
        mesh=fine,
        in_specs=placed,
        out_specs=(P(None, (*feat, "x")), P(None, (*feat, "x"))),
        check_vma=False,
    )
```

time: 295 us -> 155 us (0.53)
  blocking collectives: 173 us -> 56.1 us
  matrix products: 38.4 us -> 0 us
  Pallas kernels: 0 us -> 24 us
  waiting for transfers between devices: 49.8 us -> 37.5 us
  other arithmetic: 6.07 us -> 0.08 us
  starting transfers between devices: 18.6 us -> 24.5 us
  local copies, waits for them, and re-layouts: 7.42 us -> 11.5 us
    all_to_all x9 -> x4, blocking collectives: 173 us -> 56.1 us  [the longest x2 27.7 us: summed(): return lax.all_to_all(out, 'z', 0, 0, tiled=True)]
    all_to_all x4 -> x1, waiting for transfers between devices: 49.8 us -> 6.94 us  [shards(): arrived = lax.all_to_all(part, 'x', 0, 0, tiled=True)]
    dot_general x8 -> x0, matrix products: 38.4 us -> none  [the longest x2 11.9 us: shards(): lax.dot_general(direc.astype(jnp.bfloat16), examples, (((1,), (1,)), ((),...]
    ppermute x0 -> x16, waiting for transfers between devices: none -> 30.6 us  [the longest x12 27 us: shifted(): lax.ppermute(array, axis, [(i, (i + s) % length) for i in range(length)])]
    pallas_call x0 -> x15, Pallas kernels: none -> 24 us  [call(): pl.pallas_call(body, out_shape=outs, in_specs=[SMEM if i in smem else VME...]
    ppermute x0 -> x16, starting transfers between devices: none -> 20.5 us  [the longest x4 12.9 us: swapped(): return lax.ppermute(array, 'c', [(0, 1), (1, 0)])]
    all_to_all x4 -> x1, starting transfers between devices: 18.6 us -> 4.02 us  [shards(): arrived = lax.all_to_all(part, 'x', 0, 0, tiled=True)]
    unnamed x15 -> x18, local copies, waits for them, and re-layouts: 1.63 us -> 10.2 us
  transfers between devices with their start and end apart: 4 -> 17, of which waited for: 4 -> 16; matrix products, arithmetic and copies ran while one was open for 1% -> 0% of each run, Pallas kernels for 0% -> 1%
where the time goes in v1:
time: 155 us; the launch traced here: 154 us
  blocking collectives  56.1 us (36%)
  waiting for transfers between devices  37.5 us (24%)
  starting transfers between devices  24.5 us (16%)
  Pallas kernels  24 us (15%)
  local copies, waits for them, and re-layouts  11.5 us (7%)
    all_to_all x2, blocking collectives, summed(): return lax.all_to_all(out, 'z', 0, 0, tiled=True)  27.7 us
    ppermute x12, waiting for transfers between devices, shifted(): lax.ppermute(array, axis, [(i, (i + s) % length) for i in range(length)])  27 us
    pallas_call x15, Pallas kernels, call(): pl.pallas_call(body, out_shape=outs, in_specs=[SMEM if i in smem else VME...  24 us
    all_to_all x1, blocking collectives, shards(): lax.all_to_all(jnp.broadcast_to(margin[None], (NY * NZ, 8, 128)), ('y', '...  18.4 us
    ppermute x4, starting transfers between devices, swapped(): return lax.ppermute(array, 'c', [(0, 1), (1, 0)])  12.9 us
    unnamed x18, local copies, waits for them, and re-layouts  10.2 us
    all_to_all x1, blocking collectives, shards(): arrived = lax.all_to_all(out, ('c', 'x'), 0, 0, tiled=True)  10 us
    ppermute x12, starting transfers between devices, shifted(): lax.ppermute(array, axis, [(i, (i + s) % length) for i in range(length)])  7.61 us
  transfers between devices with their start and end apart: 17, of which 16 were waited for; matrix products, arithmetic and copies ran while one was open for 0% of the time, Pallas kernels for 1%

profile of v1, /device:TPU:1, one launch (start us, length us, event | category | flops | bytes accessed | tf_op | source)
XLA Modules:
  0.0 154.5 jit_solution(397812312819360209)
XLA Ops:
  0.7 0.8 broadcast_in_dim.4.weights
  1.4 3.4 %copy-done = bf16[1024,4096]{1,0:T(8,128)(2,1)S(1)} copy-done((bf16[1024,4096]{1,0:T(8,128)(2,1)S(1)}, bf16[1024,4096]{1,0:T(8,128)(2,1)}, u32[]{:S(2)}) %copy-start) | copy-done | bytes 8388632
  4.8 2.3 %shard_map.86 = f32[8,128]{1,0:T(8,128)S(1)} custom-call(bf16[1024,4096]{1,0:T(8,128)(2,1)S(1)} %copy-done, bf16[16,4096]{1,0:T(8,128)(2,1)S(1)} %broadcast_in_dim.4.weights), custom_call_target="tpu_custom_call" | custom-call | tf_op jit(solution)/shard_map/pallas_call | solution.py:28
  7.1 3.3 %collective-permute-start = (f32[8,128]{1,0:T(8,128)S(1)}, f32[8,128]{1,0:T(8,128)S(1)}, u32[]{:S(2)}, u32[]{:S(2)}) collective-permute-start(f32[8,128]{1,0:T(8,128)S(1)} %shard_map.86), channel_id=1, source_target_pairs={{0,4},{4,0},{1,5},{5,1},{2,6},{6,2},{3,7},{7,3},{8,12},{12,8},{9,1... | collective-permute-start | bytes 12296 | tf_op jit(solution)/shard_map/ppermute | solution.py:326
  10.3 0.8 collective-permute-done
  11.2 18.4 %all_to_all.25.margin_parts = f32[32,8,128]{2,1,0:T(8,128)S(1)} all-to-all(f32[32,8,128]{2,1,0:T(8,128)S(1)} %broadcast_in_dim.5), channel_id=1, replica_groups=mesh['y'=4,'z'=8,'c'=2,'x'=4] {'y','z'}, dimensions={0} | all-to-all | bytes 262144 | tf_op jit(solution)/shard_map/all_to_all | solution.py:349
  29.6 4.1 %shard_map.87 = (f32[4,32,1024]{2,1,0:T(8,128)}, f32[1,1024]{1,0:T(1,128)S(1)}) custom-call(f32[32,8,128]{2,1,0:T(8,128)S(1)} %all_to_all.25.margin_parts, s32[1,1024]{1,0:T(1,128)S(1)} %bitcast.12, s32[1,1024]{1,0:T(1,128)S(1)} %bitcast.13, f32[32,1024]{1,0:T(8,128)S(1)} %copy-done.3, bf16[1024,4096]{1,0:T(8,128)(2,1)S(1)} %copy-done), custom_call_target="tpu_custom_call" | custom-call | tf_op jit(solution)/shard_map/pallas_call | solution.py:28
  33.7 4.0 %all-to-all-start.1 = ((f32[4,32,1024]{2,1,0:T(8,128)}), f32[4,32,1024]{2,1,0:T(8,128)S(1)}, u32[]{:S(2)}, u32[]{:S(2)}) async-start(f32[4,32,1024]{2,1,0:T(8,128)} %get-tuple-element.17), calls=%async_computation.1 | async-start | bytes 1048576 | tf_op jit(solution)/shard_map/all_to_all | solution.py:361
  37.8 6.9 %all-to-all-done.1.arrived = f32[4,32,1024]{2,1,0:T(8,128)S(1)} async-done(((f32[4,32,1024]{2,1,0:T(8,128)}), f32[4,32,1024]{2,1,0:T(8,128)S(1)}, u32[]{:S(2)}, u32[]{:S(2)}) %all-to-all-start.1) | async-done | bytes 524320 | tf_op jit(solution)/shard_map/all_to_all | solution.py:361
  44.7 1.0 collective-permute-start.3
  45.8 1.1 collective-permute-start.2
  47.0 1.2 shard_map.89
  48.2 0.8 shard_map.90.sums
  49.1 1.3 collective-permute-done.2.low2
  50.4 0.8 collective-permute-done.1.low1
  51.2 3.4 %copy-done.1 = bf16[1024,4096]{1,0:T(8,128)(2,1)S(1)} copy-done((bf16[1024,4096]{1,0:T(8,128)(2,1)S(1)}, bf16[1024,4096]{1,0:T(8,128)(2,1)}, u32[]{:S(2)}) %copy-start.1) | copy-done | bytes 8388632
  54.6 3.4 %shard_map.91 = (f32[32,768]{1,0:T(8,128)S(1)}, f32[32,768]{1,0:T(8,128)S(1)}) custom-call(bf16[32,1024]{1,0:T(8,128)(2,1)S(1)} %get-tuple-element.18.low0, bf16[32,1024]{1,0:T(8,128)(2,1)S(1)} %collective-permute-done.1.low1, bf16[32,1024]{1,0:T(8,128)(2,1)S(1)} %collective-permute-done.2.low2, bf16[32,1024]{1,0:T(8,128)(2,1)S(1)} %collective-permute-done.3.low3, ...), custom_call_target="tpu_custom_call" | custom-call | tf_op jit(solution)/shard_map/pallas_call | solution.py:28
  58.1 5.7 %collective-permute-start.4 = (f32[32,768]{1,0:T(8,128)S(1)}, f32[32,768]{1,0:T(8,128)S(1)}, u32[]{:S(2)}, u32[]{:S(2)}) collective-permute-start(f32[32,768]{1,0:T(8,128)S(1)} %get-tuple-element.23), channel_id=1, source_target_pairs={{0,4},{4,0},{1,5},{5,1},{2,6},{6,2},{3,7},{7,3},{8,12},{12,8},{9,1... | collective-permute-start | bytes 294920 | tf_op jit(solution)/shard_map/ppermute | solution.py:326
  63.8 0.9 collective-permute-done.4.arrived
  64.8 1.0 collective-permute-start.7
  65.8 1.3 collective-permute-start.6
  67.0 0.9 collective-permute-done.7.wire3
  67.9 2.4 %collective-permute-done.6.wire2 = bf16[32,896]{1,0:T(8,128)(2,1)S(1)} collective-permute-done((bf16[32,896]{1,0:T(8,128)(2,1)S(1)}, bf16[32,896]{1,0:T(8,128)(2,1)S(1)}, u32[]{:S(2)}, u32[]{:S(2)}) %collective-permute-start.6) | collective-permute-done | bytes 57376 | tf_op jit(solution)/shard_map/ppermute | solution.py:320
  70.3 1.8 %collective-permute-done.5.wire1 = bf16[32,896]{1,0:T(8,128)(2,1)S(1)} collective-permute-done((bf16[32,896]{1,0:T(8,128)(2,1)S(1)}, bf16[32,896]{1,0:T(8,128)(2,1)S(1)}, u32[]{:S(2)}, u32[]{:S(2)}) %collective-permute-start.5) | collective-permute-done | bytes 57376 | tf_op jit(solution)/shard_map/ppermute | solution.py:320
  72.1 0.6 shard_map.93
  72.8 13.5 %all_to_all.26.arrived = bf16[8,32,640]{2,1,0:T(8,128)(2,1)S(1)} all-to-all(bf16[8,32,640]{2,1,0:T(8,128)(2,1)S(1)} %shard_map.93), channel_id=1, replica_groups=mesh['y'=4,'z'=8,'c'=2,'x'=4] {'z'}, dimensions={0} | all-to-all | bytes 655360 | tf_op jit(solution)/shard_map/all_to_all | solution.py:335
  86.3 0.7 shard_map.94
  87.0 3.4 %collective-permute-start.8 = (bf16[32,640]{1,0:T(8,128)(2,1)S(1)}, bf16[32,640]{1,0:T(8,128)(2,1)S(1)}, u32[]{:S(2)}, u32[]{:S(2)}) collective-permute-start(bf16[32,640]{1,0:T(8,128)(2,1)S(1)} %get-tuple-element.25.weighted), channel_id=1, source_target_pairs={{0,4},{4,0},{1,5},{5,1},{2,6},{6,2},{3,7},{7,3},{8,12},{12,8},{9,1... | collective-permute-start | bytes 122888 | tf_op jit(solution)/shard_map/ppermute | solution.py:326
  90.3 0.9 collective-permute-done.8.other
  91.2 3.4 %copy-done.2 = bf16[1024,4096]{1,0:T(8,128)(2,1)S(1)} copy-done((bf16[1024,4096]{1,0:T(8,128)(2,1)S(1)}, bf16[1024,4096]{1,0:T(8,128)(2,1)}, u32[]{:S(2)}) %copy-start.2) | copy-done | bytes 8388632
  94.6 3.9 %shard_map.95.part0 = bf16[32,4224]{1,0:T(8,128)(2,1)S(1)} custom-call(bf16[32,640]{1,0:T(8,128)(2,1)S(1)} %get-tuple-element.25.weighted, bf16[32,640]{1,0:T(8,128)(2,1)S(1)} %collective-permute-done.8.other, f32[32,256]{1,0:T(8,128)S(1)} %get-tuple-element.26.kept, bf16[1024,4096]{1,0:T(8,128)(2,1)S(1)} %copy-done.2, s32[4]{0:T(128)S(1)} %pad_add_fusion.place), custom_call_target="tpu_custom_call" | custom-call | tf_op jit(solution)/shard_map/pallas_call | solution.py:28
  98.5 0.7 collective-permute-start.11
  99.1 0.6 collective-permute-start.10
  100.1 6.1 %collective-permute-done.11.part3 = bf16[32,4224]{1,0:T(8,128)(2,1)S(1)} collective-permute-done((bf16[32,4224]{1,0:T(8,128)(2,1)S(1)}, bf16[32,4224]{1,0:T(8,128)(2,1)S(1)}, u32[]{:S(2)}, u32[]{:S(2)}) %collective-permute-start.11) | collective-permute-done | bytes 270368 | tf_op jit(solution)/shard_map/ppermute | solution.py:320
  106.3 1.8 %collective-permute-done.10.part2 = bf16[32,4224]{1,0:T(8,128)(2,1)S(1)} collective-permute-done((bf16[32,4224]{1,0:T(8,128)(2,1)S(1)}, bf16[32,4224]{1,0:T(8,128)(2,1)S(1)}, u32[]{:S(2)}, u32[]{:S(2)}) %collective-permute-start.10) | collective-permute-done | bytes 270368 | tf_op jit(solution)/shard_map/ppermute | solution.py:320
  108.1 6.8 %collective-permute-done.9.part1 = bf16[32,4224]{1,0:T(8,128)(2,1)S(1)} collective-permute-done((bf16[32,4224]{1,0:T(8,128)(2,1)S(1)}, bf16[32,4224]{1,0:T(8,128)(2,1)S(1)}, u32[]{:S(2)}, u32[]{:S(2)}) %collective-permute-start.9) | collective-permute-done | bytes 270368 | tf_op jit(solution)/shard_map/ppermute | solution.py:320
  114.8 4.0 %shard_map.96 = (f32[32,1024]{1,0:T(8,128)S(1)}, f32[32,768]{1,0:T(8,128)S(1)}, f32[32,768]{1,0:T(8,128)S(1)}, f32[32,128]{1,0:T(8,128)S(1)}) custom-call(bf16[32,4224]{1,0:T(8,128)(2,1)S(1)} %shard_map.95.part0, bf16[32,4224]{1,0:T(8,128)(2,1)S(1)} %collective-permute-done.9.part1, bf16[32,4224]{1,0:T(8,128)(2,1)S(1)} %collective-permute-done.10.part2, ...), custom_call_target="tpu_custom_call" | custom-call | tf_op jit(solution)/shard_map/pallas_call | solution.py:28
  118.8 0.6 collective-permute-start.12
  119.4 0.9 collective-permute-done.12.arrived
  121.1 0.9 collective-permute-start.13
  122.0 1.6 %collective-permute-done.15.wire3 = bf16[32,896]{1,0:T(8,128)(2,1)S(1)} collective-permute-done((bf16[32,896]{1,0:T(8,128)(2,1)S(1)}, bf16[32,896]{1,0:T(8,128)(2,1)S(1)}, u32[]{:S(2)}, u32[]{:S(2)}) %collective-permute-start.15) | collective-permute-done | bytes 57376 | tf_op jit(solution)/shard_map/ppermute | solution.py:320
  123.6 1.9 %collective-permute-done.14.wire2 = bf16[32,896]{1,0:T(8,128)(2,1)S(1)} collective-permute-done((bf16[32,896]{1,0:T(8,128)(2,1)S(1)}, bf16[32,896]{1,0:T(8,128)(2,1)S(1)}, u32[]{:S(2)}, u32[]{:S(2)}) %collective-permute-start.14) | collective-permute-done | bytes 57376 | tf_op jit(solution)/shard_map/ppermute | solution.py:320
  125.5 1.6 %collective-permute-done.13.wire1 = bf16[32,896]{1,0:T(8,128)(2,1)S(1)} collective-permute-done((bf16[32,896]{1,0:T(8,128)(2,1)S(1)}, bf16[32,896]{1,0:T(8,128)(2,1)S(1)}, u32[]{:S(2)}, u32[]{:S(2)}) %collective-permute-start.13) | collective-permute-done | bytes 57376 | tf_op jit(solution)/shard_map/ppermute | solution.py:320
  127.0 0.6 shard_map.98
  127.7 14.1 %all_to_all.27.arrived = bf16[8,32,640]{2,1,0:T(8,128)(2,1)S(1)} all-to-all(bf16[8,32,640]{2,1,0:T(8,128)(2,1)S(1)} %shard_map.98), channel_id=1, replica_groups=mesh['y'=4,'z'=8,'c'=2,'x'=4] {'z'}, dimensions={0} | all-to-all | bytes 655360 | tf_op jit(solution)/shard_map/all_to_all | solution.py:335
  141.8 0.7 shard_map.99
  142.5 10.0 %all_to_all.28.arrived = f32[8,32,128]{2,1,0:T(8,128)S(1)} all-to-all(f32[8,32,128]{2,1,0:T(8,128)S(1)} %shard_map.99), channel_id=1, replica_groups=mesh['y'=4,'z'=8,'c'=2,'x'=4] {'c','x'}, dimensions={0} | all-to-all | bytes 262144 | tf_op jit(solution)/shard_map/all_to_all | solution.py:426
  152.5 1.3 shard_map.100
  (29 shorter events, 2.0 us)
Async XLA Ops:
  0.6 29.0 %copy-start.3 = (f32[32,1024]{1,0:T(8,128)S(1)}, f32[32,1024]{1,0:T(8,128)}, u32[]{:S(2)}) copy-start(f32[32,1024]{1,0:T(8,128)} %val_weight.1) | copy-start | bytes 393220
  0.6 29.0 %copy-start.6 = (s32[1024]{0:T(1024)S(1)}, s32[1024]{0:T(1024)}, u32[]{:S(2)}) copy-start(s32[1024]{0:T(1024)} %param.10) | copy-start | bytes 12292
  0.7 29.0 %copy-start.5 = (s32[1024]{0:T(1024)S(1)}, s32[1024]{0:T(1024)}, u32[]{:S(2)}) copy-start(s32[1024]{0:T(1024)} %param.9) | copy-start | bytes 12292
  1.4 3.4 %copy-start = (bf16[1024,4096]{1,0:T(8,128)(2,1)S(1)}, bf16[1024,4096]{1,0:T(8,128)(2,1)}, u32[]{:S(2)}) copy-start(bf16[1024,4096]{1,0:T(8,128)(2,1)} %examples.9) | copy-start | bytes 25165828
  4.8 32.9 %copy-start.8 = (bf16[4096]{0:T(1024)(128)(2,1)S(1)}, bf16[4096]{0:T(1024)(128)(2,1)}, u32[]{:S(2)}) copy-start(bf16[4096]{0:T(1024)(128)(2,1)} %param.8) | copy-start | bytes 24580
  4.8 42.2 %copy-start.4 = (s32[4096]{0:T(1024)S(1)}, s32[4096]{0:T(1024)}, u32[]{:S(2)}) copy-start(s32[4096]{0:T(1024)} %param.13) | copy-start | bytes 49156
  4.8 42.2 %copy-start.7 = (f32[256]{0:T(256)S(1)}, f32[256]{0:T(256)}, u32[]{:S(2)}) copy-start(f32[256]{0:T(256)} %param.12) | copy-start | bytes 3076
  7.1 4.1 %collective-permute-start = (f32[8,128]{1,0:T(8,128)S(1)}, f32[8,128]{1,0:T(8,128)S(1)}, u32[]{:S(2)}, u32[]{:S(2)}) collective-permute-start(f32[8,128]{1,0:T(8,128)S(1)} %shard_map.86), channel_id=1, source_target_pairs={{0,4},{4,0},{1,5},{5,1},{2,6},{6,2},{3,7},{7,3},{8,12},{12,8},{9,1... | collective-permute-start | bytes 12296 | tf_op jit(solution)/shard_map/ppermute | solution.py:326
  33.7 11.0 %all-to-all-start.1 = ((f32[4,32,1024]{2,1,0:T(8,128)}), f32[4,32,1024]{2,1,0:T(8,128)S(1)}, u32[]{:S(2)}, u32[]{:S(2)}) async-start(f32[4,32,1024]{2,1,0:T(8,128)} %get-tuple-element.17), calls=%async_computation.1 | async-start | bytes 1048576 | tf_op jit(solution)/shard_map/all_to_all | solution.py:361
  44.7 4.4 %collective-permute-start.3 = (bf16[32,1024]{1,0:T(8,128)(2,1)S(1)}, bf16[32,1024]{1,0:T(8,128)(2,1)S(1)}, u32[]{:S(2)}, u32[]{:S(2)}) collective-permute-start(bf16[32,1024]{1,0:T(8,128)(2,1)S(1)} %get-tuple-element.18.low0), channel_id=1, source_target_pairs={{0,3},{1,0},{2,1},{3,2},{4,7},{5,4},{6,5},{7,6},{8,11},{9,8},{10,9... | collective-permute-start | bytes 196616 | tf_op jit(solution)/shard_map/ppermute | solution.py:320
  45.8 4.6 %collective-permute-start.2 = (bf16[32,1024]{1,0:T(8,128)(2,1)S(1)}, bf16[32,1024]{1,0:T(8,128)(2,1)S(1)}, u32[]{:S(2)}, u32[]{:S(2)}) collective-permute-start(bf16[32,1024]{1,0:T(8,128)(2,1)S(1)} %get-tuple-element.18.low0), channel_id=1, source_target_pairs={{0,2},{1,3},{2,0},{3,1},{4,6},{5,7},{6,4},{7,5},{8,10},{9,11},{10,... | collective-permute-start | bytes 196616 | tf_op jit(solution)/shard_map/ppermute | solution.py:320
  46.9 4.3 %collective-permute-start.1 = (bf16[32,1024]{1,0:T(8,128)(2,1)S(1)}, bf16[32,1024]{1,0:T(8,128)(2,1)S(1)}, u32[]{:S(2)}, u32[]{:S(2)}) collective-permute-start(bf16[32,1024]{1,0:T(8,128)(2,1)S(1)} %get-tuple-element.18.low0), channel_id=1, source_target_pairs={{0,1},{1,2},{2,3},{3,0},{4,5},{5,6},{6,7},{7,4},{8,9},{9,10},{10,1... | collective-permute-start | bytes 196616 | tf_op jit(solution)/shard_map/ppermute | solution.py:320
  51.2 3.4 %copy-start.1 = (bf16[1024,4096]{1,0:T(8,128)(2,1)S(1)}, bf16[1024,4096]{1,0:T(8,128)(2,1)}, u32[]{:S(2)}) copy-start(bf16[1024,4096]{1,0:T(8,128)(2,1)} %examples.9) | copy-start | bytes 25165828
  58.1 6.6 %collective-permute-start.4 = (f32[32,768]{1,0:T(8,128)S(1)}, f32[32,768]{1,0:T(8,128)S(1)}, u32[]{:S(2)}, u32[]{:S(2)}) collective-permute-start(f32[32,768]{1,0:T(8,128)S(1)} %get-tuple-element.23), channel_id=1, source_target_pairs={{0,4},{4,0},{1,5},{5,1},{2,6},{6,2},{3,7},{7,3},{8,12},{12,8},{9,1... | collective-permute-start | bytes 294920 | tf_op jit(solution)/shard_map/ppermute | solution.py:326
  64.8 3.1 %collective-permute-start.7 = (bf16[32,896]{1,0:T(8,128)(2,1)S(1)}, bf16[32,896]{1,0:T(8,128)(2,1)S(1)}, u32[]{:S(2)}, u32[]{:S(2)}) collective-permute-start(bf16[32,896]{1,0:T(8,128)(2,1)S(1)} %shard_map.92.wire0), channel_id=1, source_target_pairs={{0,192},{64,0},{128,64},{192,128},{1,193},{65,1},{129,65},{193,129... | collective-permute-start | bytes 172040 | tf_op jit(solution)/shard_map/ppermute | solution.py:320
  65.8 4.5 %collective-permute-start.6 = (bf16[32,896]{1,0:T(8,128)(2,1)S(1)}, bf16[32,896]{1,0:T(8,128)(2,1)S(1)}, u32[]{:S(2)}, u32[]{:S(2)}) collective-permute-start(bf16[32,896]{1,0:T(8,128)(2,1)S(1)} %shard_map.92.wire0), channel_id=1, source_target_pairs={{0,128},{64,192},{128,0},{192,64},{1,129},{65,193},{129,1},{193,65... | collective-permute-start | bytes 172040 | tf_op jit(solution)/shard_map/ppermute | solution.py:320
  67.0 5.1 %collective-permute-start.5 = (bf16[32,896]{1,0:T(8,128)(2,1)S(1)}, bf16[32,896]{1,0:T(8,128)(2,1)S(1)}, u32[]{:S(2)}, u32[]{:S(2)}) collective-permute-start(bf16[32,896]{1,0:T(8,128)(2,1)S(1)} %shard_map.92.wire0), channel_id=1, source_target_pairs={{0,64},{64,128},{128,192},{192,0},{1,65},{65,129},{129,193},{193,1... | collective-permute-start | bytes 172040 | tf_op jit(solution)/shard_map/ppermute | solution.py:320
  87.0 4.2 %collective-permute-start.8 = (bf16[32,640]{1,0:T(8,128)(2,1)S(1)}, bf16[32,640]{1,0:T(8,128)(2,1)S(1)}, u32[]{:S(2)}, u32[]{:S(2)}) collective-permute-start(bf16[32,640]{1,0:T(8,128)(2,1)S(1)} %get-tuple-element.25.weighted), channel_id=1, source_target_pairs={{0,4},{4,0},{1,5},{5,1},{2,6},{6,2},{3,7},{7,3},{8,12},{12,8},{9,1... | collective-permute-start | bytes 122888 | tf_op jit(solution)/shard_map/ppermute | solution.py:326
  91.2 3.4 %copy-start.2 = (bf16[1024,4096]{1,0:T(8,128)(2,1)S(1)}, bf16[1024,4096]{1,0:T(8,128)(2,1)}, u32[]{:S(2)}) copy-start(bf16[1024,4096]{1,0:T(8,128)(2,1)} %examples.9) | copy-start | bytes 25165828
  98.5 7.8 %collective-permute-start.11 = (bf16[32,4224]{1,0:T(8,128)(2,1)S(1)}, bf16[32,4224]{1,0:T(8,128)(2,1)S(1)}, u32[]{:S(2)}, u32[]{:S(2)}) collective-permute-start(bf16[32,4224]{1,0:T(8,128)(2,1)S(1)} %shard_map.95.part0), channel_id=1, source_target_pairs={{0,3},{1,0},{2,1},{3,2},{4,7},{5,4},{6,5},{7,6},{8,11},{9,8},{10,9... | collective-permute-start | bytes 811016 | tf_op jit(solution)/shard_map/ppermute | solution.py:320
  99.1 8.9 %collective-permute-start.10 = (bf16[32,4224]{1,0:T(8,128)(2,1)S(1)}, bf16[32,4224]{1,0:T(8,128)(2,1)S(1)}, u32[]{:S(2)}, u32[]{:S(2)}) collective-permute-start(bf16[32,4224]{1,0:T(8,128)(2,1)S(1)} %shard_map.95.part0), channel_id=1, source_target_pairs={{0,2},{1,3},{2,0},{3,1},{4,6},{5,7},{6,4},{7,5},{8,10},{9,11},{10,... | collective-permute-start | bytes 811016 | tf_op jit(solution)/shard_map/ppermute | solution.py:320
  99.7 15.1 %collective-permute-start.9 = (bf16[32,4224]{1,0:T(8,128)(2,1)S(1)}, bf16[32,4224]{1,0:T(8,128)(2,1)S(1)}, u32[]{:S(2)}, u32[]{:S(2)}) collective-permute-start(bf16[32,4224]{1,0:T(8,128)(2,1)S(1)} %shard_map.95.part0), channel_id=1, source_target_pairs={{0,1},{1,2},{2,3},{3,0},{4,5},{5,6},{6,7},{7,4},{8,9},{9,10},{10,1... | collective-permute-start | bytes 811016 | tf_op jit(solution)/shard_map/ppermute | solution.py:320
  118.8 1.5 collective-permute-start.12
  120.5 3.1 %collective-permute-start.15 = (bf16[32,896]{1,0:T(8,128)(2,1)S(1)}, bf16[32,896]{1,0:T(8,128)(2,1)S(1)}, u32[]{:S(2)}, u32[]{:S(2)}) collective-permute-start(bf16[32,896]{1,0:T(8,128)(2,1)S(1)} %shard_map.97.wire0), channel_id=1, source_target_pairs={{0,192},{64,0},{128,64},{192,128},{1,193},{65,1},{129,65},{193,129... | collective-permute-start | bytes 172040 | tf_op jit(solution)/shard_map/ppermute | solution.py:320
  120.9 4.5 %collective-permute-start.14 = (bf16[32,896]{1,0:T(8,128)(2,1)S(1)}, bf16[32,896]{1,0:T(8,128)(2,1)S(1)}, u32[]{:S(2)}, u32[]{:S(2)}) collective-permute-start(bf16[32,896]{1,0:T(8,128)(2,1)S(1)} %shard_map.97.wire0), channel_id=1, source_target_pairs={{0,128},{64,192},{128,0},{192,64},{1,129},{65,193},{129,1},{193,65... | collective-permute-start | bytes 172040 | tf_op jit(solution)/shard_map/ppermute | solution.py:320
  121.1 5.9 %collective-permute-start.13 = (bf16[32,896]{1,0:T(8,128)(2,1)S(1)}, bf16[32,896]{1,0:T(8,128)(2,1)S(1)}, u32[]{:S(2)}, u32[]{:S(2)}) collective-permute-start(bf16[32,896]{1,0:T(8,128)(2,1)S(1)} %shard_map.97.wire0), channel_id=1, source_target_pairs={{0,64},{64,128},{128,192},{192,0},{1,65},{65,129},{129,193},{193,1... | collective-permute-start | bytes 172040 | tf_op jit(solution)/shard_map/ppermute | solution.py:320

commit v2 on v1

--- a/solution.py
+++ b/solution.py
@@ -1,5 +1,3 @@
-import functools
-
 import jax
 import jax.numpy as jnp
 from jax import lax
@@ -87,9 +85,8 @@
 def prepare(ids, strengths, place, lamf, onehot):
     kinds = lax.broadcasted_iota(jnp.int32, (NB, OWN), 0)
     rows = lax.broadcasted_iota(jnp.int32, (16, NB), 0)
-    value = strengths[...]
     split3 = jnp.zeros((16, NB), F32)
-    for i, term in enumerate(terms(value, 3)):
+    for i, term in enumerate(terms(strengths[...], 3)):
         split3 = jnp.where(rows == i, term, split3)
     split3 = split3.astype(BF16)
     for j in range(NX):
@@ -102,15 +99,28 @@
     onehot[...] = (kinds == moved).astype(F32).astype(BF16)
 
 
-def margins(examples, weights, margin):
+def margins(
+    source, wfloat, ids, strengths, place, margin, examples, lamf, onehot, arrival
+):
+    def fetch(i):
+        rows = pl.ds(i * 128, 128)
+        return pltpu.make_async_copy(source.at[rows], examples.at[rows], arrival.at[i])
+
     for i in range(8):
+        fetch(i).start()
+    prepare(ids, strengths, place, lamf, onehot)
+    weights = jnp.broadcast_to(wfloat[...], (16, W)).astype(BF16)
+    for i in range(8):
+        fetch(i).wait()
         rows = lax.dot_general(
-            weights[...], examples[i * 128 : (i + 1) * 128, :], NT, preferred_element_type=F32
+            weights, examples[i * 128 : (i + 1) * 128, :], NT, preferred_element_type=F32
         )
         margin[i : i + 1, :] = rows[0:1]
 
 
-def gradients(margin_parts, labels, split, val_weight, examples, part, curvew):
+def gradients(
+    margin_parts, labels, split, val_weight, examples, place, part, send1, send2, send3, curvew
+):
     whole = jnp.sum(margin_parts[...], axis=0)
     margin = jnp.concatenate([whole[i : i + 1] for i in range(8)], axis=1)
     prob = 1.0 / (1.0 + jnp.exp(-margin))
@@ -118,35 +128,22 @@
     curvew[...] = train * prob * (1.0 - prob)
     err = (1.0 - train) * (prob - labels[...].astype(F32))
     gradw = (val_weight[...] * err / jnp.sqrt(F32(TOTAL))).astype(BF16)
-    for j in range(NX):
-
-        def step(i, _, j=j):
-            at = chunk(i, 256)
-            cols = pl.ds(pl.multiple_of(j * OWN + i * 256, 256), 256)
-            part[j, :, at] = jnp.dot(gradw, examples[:, cols], preferred_element_type=F32)
-            return 0
-
-        lax.fori_loop(0, OWN // 256, step, 0)
-
-
-def start_rhs(arrived, rhs, low):
-    total = jnp.sum(arrived[...], axis=0)
-    rhs[...] = total
-    low[...] = total.astype(BF16)
-
-
-def rhs_sums(rhs, lamf, wfloat, onehot, place, sums):
-    own = chunk(place[3], OWN)
-    vec = rhs[...]
-    norm = jnp.sum(vec * vec, axis=1, keepdims=True)
-    scaled = jnp.sum(lamf[:, own] * vec * vec, axis=1, keepdims=True)
-    sums[:, :LANES] = columns([norm, scaled])
-    sums[:, LANES:] = block_sums(vec, wfloat[:, own], onehot[...])
+    sends = (send1, send2, send3)
+    for j in range(W // 512):
+        cols = slice(j * 512, (j + 1) * 512)
+        found = jnp.dot(gradw, examples[:, cols], preferred_element_type=F32)
+        part[:, cols] = found
+        high = found.astype(BF16)
+        for send in sends:
+            send[:, cols] = high
+    for s, send in enumerate(sends):
+        found = part[:, chunk((place[3] + s + 1) % NX, OWN)]
+        send[:, W:] = (found - found.astype(BF16).astype(F32)).astype(BF16)
 
 
 def tangents(pieces, examples, x, tang):
-    def step(i, _):
-        rows = chunk(i, 256)
+    for i in range(N // 256):
+        rows = slice(i * 256, (i + 1) * 256)
         total = None
         for s, piece in enumerate(pieces):
             cols = chunk((x - s + NX) % NX, OWN)
@@ -155,9 +152,6 @@
             )
             total = term if total is None else total + term
         tang[:, rows] = total
-        return 0
-
-    lax.fori_loop(0, N // 256, step, 0)
 
 
 def halves(tang, scalars, blocks, core, keep, send):
@@ -167,10 +161,25 @@
         out[:, HALF + LANES :] = blocks[:, chunk(which, LANES)]
 
 
-def first_tangents(low0, low1, low2, low3, examples, sums, place, keep, send, tang, blocks):
-    tangents([low0, low1, low2, low3], examples, place[3], tang)
-    blocks[...] = sums[:, LANES:]
-    halves(tang, sums[:, :LANES], blocks, place[2], keep, send)
+def first_tangents(
+    part, wire1, wire2, wire3, examples, lamf, wfloat, onehot, place,
+    rhs, lows, keep, send, tang, blocks,
+):
+    x = place[3]
+    wires = (wire1, wire2, wire3)
+    for s in range(NX):
+        cols = chunk((x - s + NX) % NX, OWN)
+        vec = part[:, cols] + sum(w[:, cols].astype(F32) for w in wires)
+        if s == 0:
+            vec = vec + sum(w[:, W:].astype(F32) for w in wires)
+            rhs[...] = vec
+            square = vec * vec
+            norm = jnp.sum(square, axis=1, keepdims=True)
+            scaled = jnp.sum(lamf[:, cols] * square, axis=1, keepdims=True)
+            blocks[...] = block_sums(vec, wfloat[:, cols], onehot[...])
+        lows[s] = vec.astype(BF16)
+    tangents([lows.at[s] for s in range(NX)], examples, x, tang)
+    halves(tang, columns([norm, scaled]), blocks, place[2], keep, send)
 
 
 def to_wire(keep, arrived, wire):
@@ -227,9 +236,8 @@
 
 def products(weighted, other, kept, examples, place, part):
     core = place[2]
-
-    def step(i, _):
-        cols = chunk(i, 256)
+    for j in range(W // 512):
+        cols = slice(j * 512, (j + 1) * 512)
         mine = jnp.dot(
             weighted[:, :HALF], examples[chunk(core, HALF), cols], preferred_element_type=F32
         )
@@ -237,16 +245,13 @@
             other[:, :HALF], examples[chunk(1 - core, HALF), cols], preferred_element_type=F32
         )
         part[:, cols] = (mine + rest).astype(BF16)
-        return 0
-
-    lax.fori_loop(0, W // 256, step, 0)
     tile = kept[:, :LANES]
     curv = column(tile, 2) + unpacked(other[:, HALF:].astype(F32), 0)
     part[:, W:] = packed([column(tile, 0), column(tile, 1), curv]).astype(BF16)
 
 
 def second_tangents(
-    part0, part1, part2, part3, rhs, low1, low2, low3, examples, lamf, wfloat, onehot, place,
+    part0, part1, part2, part3, rhs, lows, examples, lamf, wfloat, onehot, place,
     resid, keep, send, kept, tang, blocks, pieces,
 ):
     x = place[3]
@@ -255,10 +260,10 @@
     norm, scaled, curv = (unpacked(tile, i) for i in range(3))
     alpha = norm / (curv / F32(TOTAL) + scaled)
     kept[...] = columns([alpha, norm, scaled, curv])
-    for s, vec in enumerate((rhs, low1, low2, low3)):
+    for s in range(NX):
         cols = chunk((x - s + NX) % NX, OWN)
         total = sum(p[:, cols].astype(F32) for p in parts)
-        direc = vec[...].astype(F32)
+        direc = rhs[...] if s == 0 else lows[s].astype(F32)
         lam = lamf[:, cols]
         left = direc - alpha * (total / F32(TOTAL) + lam * direc)
         pieces[s] = left.astype(BF16)
@@ -312,14 +317,16 @@
     block = ((place[0] * NZ + place[1]) * NC + core) * NX + x
     kinds = lax.broadcasted_iota(jnp.int32, (1, NB), 1)
     strength = jnp.sum(jnp.where(kinds == block, strengths[...], 0.0), axis=1, keepdims=True)
-    hyper[...] = -strength * (alpha * before + alpha_next * (now + beta * before))
+    found = -strength * (alpha * before + alpha_next * (now + beta * before))
+    hyper[...] = jnp.transpose(jnp.broadcast_to(found, (R, LANES)))[0:1]
+
+
+def shift(array, axis, length, by):
+    return lax.ppermute(array, axis, [(i, (i + by) % length) for i in range(length)])
 
 
 def shifted(array, axis, length):
-    return [
-        lax.ppermute(array, axis, [(i, (i + s) % length) for i in range(length)])
-        for s in range(1, length)
-    ]
+    return [shift(array, axis, length, s) for s in range(1, length)]
 
 
 def swapped(array):
@@ -337,42 +344,56 @@
 
 def shards(examples, weights, labels, split, val_weight, strengths, block_ids):
     place = jnp.stack([lax.axis_index(axis) for axis in ("y", "z", "c", "x")]).astype(jnp.int32)
-    ids = block_ids.reshape(1, W)
     strengths = strengths.reshape(1, NB)
-    wrows = jnp.broadcast_to(weights[None, :], (16, W))
     wfloat = weights.astype(F32).reshape(1, W)
-    lamf, onehot = call(
-        prepare, [shape(1, W), shape(NB, OWN, dtype=BF16)], ids, strengths, place, smem=(2,)
-    )
-    margin = call(margins, shape(8, 128), examples, wrows)
+    margin, examples, lamf, onehot = pl.pallas_call(
+        margins,
+        out_shape=[
+            shape(8, 128),
+            pltpu.VMEM((N, W), BF16),
+            shape(1, W),
+            shape(NB, OWN, dtype=BF16),
+        ],
+        in_specs=[pl.BlockSpec(memory_space=pltpu.HBM), VMEM, VMEM, VMEM, SMEM],
+        out_specs=[VMEM] * 4,
+        scratch_shapes=[pltpu.SemaphoreType.DMA((8,))],
+        compiler_params=pltpu.CompilerParams(vmem_limit_bytes=16 << 20),
+    )(
+        pltpu.with_memory_space_constraint(examples, pltpu.HBM),
+        wfloat,
+        block_ids.reshape(1, W),
+        strengths,
+        place,
+    )
     margin = margin + swapped(margin)
     margin_parts = lax.all_to_all(
         jnp.broadcast_to(margin[None], (NY * NZ, 8, 128)), ("y", "z"), 0, 0, tiled=True
     )
-    part, curvew = call(
+    part, *sends, curvew = call(
         gradients,
-        [shape(NX, R, OWN), shape(1, N)],
+        [shape(R, W), *[shape(R, W + OWN, dtype=BF16)] * (NX - 1), shape(1, N)],
         margin_parts,
         labels.reshape(1, N),
         split.reshape(1, N),
         val_weight,
         examples,
-    )
-    arrived = lax.all_to_all(part, "x", 0, 0, tiled=True)
-    rhs, low = call(start_rhs, [shape(R, OWN), shape(R, OWN, dtype=BF16)], arrived)
-    lows = shifted(low, "x", NX)
-    sums = call(rhs_sums, shape(R, LANES + NB), rhs, lamf, wfloat, onehot, place, smem=(4,))
+        place,
+        smem=(5,),
+    )
+    wires = [shift(send, "x", NX, s + 1) for s, send in enumerate(sends)]
     pair = [shape(R, HALF + 2 * LANES)] * 2
-    keep, send = call(
+    rhs, lows, keep, send = call(
         first_tangents,
-        pair,
-        low,
-        *lows,
+        [shape(R, OWN), shape(NX, R, OWN, dtype=BF16), *pair],
+        part,
+        *wires,
         examples,
-        sums,
+        lamf,
+        wfloat,
+        onehot,
         place,
         scratch=[pltpu.VMEM((R, N), F32), pltpu.VMEM((R, NB), F32)],
-        smem=(6,),
+        smem=(8,),
     )
     arrived = summed(keep, send, place)
     tang_first, weighted, kept_first = call(
@@ -399,7 +420,7 @@
         part,
         *shifted(part, "x", NX),
         rhs,
-        *lows,
+        lows,
         examples,
         lamf,
         wfloat,
@@ -410,7 +431,7 @@
             pltpu.VMEM((R, NB), F32),
             pltpu.VMEM((NX, R, OWN), BF16),
         ],
-        smem=(12,),
+        smem=(10,),
     )
     arrived = summed(keep, send, place)
     out = call(
@@ -424,19 +445,18 @@
         smem=(4,),
     )
     arrived = lax.all_to_all(out, ("c", "x"), 0, 0, tiled=True)
-    return tuple(
-        call(
-            finish,
-            [shape(R, OWN), shape(R, 1)],
-            arrived,
-            kept,
-            rhs,
-            resid,
-            strengths,
-            place,
-            smem=(5,),
-        )
-    )
+    solve, hyper = call(
+        finish,
+        [shape(R, OWN), shape(1, R)],
+        arrived,
+        kept,
+        rhs,
+        resid,
+        strengths,
+        place,
+        smem=(5,),
+    )
+    return solve, hyper.reshape(R, 1)
 
 
 def solution(mesh):

time: 155 us -> 144 us (0.929)
  local copies, waits for them, and re-layouts: 11.5 us -> 1.43 us
  waiting for transfers between devices: 37.5 us -> 40.3 us
  starting transfers between devices: 24.5 us -> 21.8 us
  Pallas kernels: 24 us -> 22.2 us
    ppermute x12, waiting for transfers between devices: 27 us -> 36.7 us  [shift(): lax.ppermute(array, axis, [(i, (i + by) % length) for i in range(length)])]
    pallas_call x15 -> x11, Pallas kernels: 24 us -> 15.1 us  [call(): pl.pallas_call(body, out_shape=outs, in_specs=[SMEM if i in smem else VME...]
    unnamed x18 -> x12, local copies, waits for them, and re-layouts: 10.2 us -> 1.41 us
    pallas_call x0 -> x1, Pallas kernels: none -> 7.09 us  [shards(): pl.pallas_call(margins, out_shape=[shape(8, 128), pltpu.VMEM((N, W), BF16...]
    all_to_all x1 -> x0, waiting for transfers between devices: 6.94 us -> none  [shards(): arrived = lax.all_to_all(part, 'x', 0, 0, tiled=True)]
    ppermute x12, starting transfers between devices: 7.61 us -> 11.9 us  [shift(): lax.ppermute(array, axis, [(i, (i + by) % length) for i in range(length)])]
    all_to_all x1 -> x0, starting transfers between devices: 4.02 us -> none  [shards(): arrived = lax.all_to_all(part, 'x', 0, 0, tiled=True)]
    ppermute x4, starting transfers between devices: 12.9 us -> 9.85 us  [swapped(): return lax.ppermute(array, 'c', [(0, 1), (1, 0)])]
  transfers between devices with their start and end apart: 17 -> 16, of which waited for: 16 -> 16; matrix products, arithmetic and copies ran while one was open for 0% -> 0% of each run, Pallas kernels for 1% -> 0%
where the time goes in v2:
time: 144 us
  blocking collectives  56.6 us (39%)
  waiting for transfers between devices  40.3 us (28%)
  Pallas kernels  22.2 us (15%)
  starting transfers between devices  21.8 us (15%)
    ppermute x12, waiting for transfers between devices, shift(): lax.ppermute(array, axis, [(i, (i + by) % length) for i in range(length)])  36.7 us
    all_to_all x2, blocking collectives, summed(): return lax.all_to_all(out, 'z', 0, 0, tiled=True)  28.1 us
    all_to_all x1, blocking collectives, shards(): lax.all_to_all(jnp.broadcast_to(margin[None], (NY * NZ, 8, 128)), ('y', '...  18.4 us
    pallas_call x11, Pallas kernels, call(): pl.pallas_call(body, out_shape=outs, in_specs=[SMEM if i in smem else VME...  15.1 us
    ppermute x12, starting transfers between devices, shift(): lax.ppermute(array, axis, [(i, (i + by) % length) for i in range(length)])  11.9 us
    all_to_all x1, blocking collectives, shards(): arrived = lax.all_to_all(out, ('c', 'x'), 0, 0, tiled=True)  10 us
    ppermute x4, starting transfers between devices, swapped(): return lax.ppermute(array, 'c', [(0, 1), (1, 0)])  9.85 us
    pallas_call x1, Pallas kernels, shards(): pl.pallas_call(margins, out_shape=[shape(8, 128), pltpu.VMEM((N, W), BF16...  7.09 us
  transfers between devices with their start and end apart: 16, of which 16 were waited for; matrix products, arithmetic and copies ran while one was open for 0% of the time, Pallas kernels for 0%

profile of v2, /device:TPU:1, one launch (start us, length us, event | category | flops | bytes accessed | tf_op | source)
XLA Modules:
  0.0 143.9 jit_solution(11621908267627105049)
XLA Ops:
  0.6 0.7 reshape.32
  1.5 0.7 copy-done.1
  2.2 0.7 copy-done.4
  2.9 7.1 %shard_map.86 = (f32[8,128]{1,0:T(8,128)S(1)}, bf16[1024,4096]{1,0:T(8,128)(2,1)S(1)}, f32[1,4096]{1,0:T(1,128)S(1)}, bf16[256,1024]{1,0:T(8,128)(2,1)S(1)}) custom-call(bf16[1024,4096]{1,0:T(8,128)(2,1)} %source.1, f32[1,4096]{1,0:T(1,128)S(1)} %bitcast.10, s32[1,4096]{1,0:T(1,128)S(1)} %bitcast.13, f32[1,256]{1,0:T(1,128)S(1)} %bitcast.16, ...), custom_call_target="tpu_custom_call" | custom-call | tf_op jit(solution)/shard_map/pallas_call | solution.py:349
  10.0 3.3 %collective-permute-start = (f32[8,128]{1,0:T(8,128)S(1)}, f32[8,128]{1,0:T(8,128)S(1)}, u32[]{:S(2)}, u32[]{:S(2)}) collective-permute-start(f32[8,128]{1,0:T(8,128)S(1)} %get-tuple-element.24), channel_id=1, source_target_pairs={{0,4},{4,0},{1,5},{5,1},{2,6},{6,2},{3,7},{7,3},{8,12},{12,8},{9,1... | collective-permute-start | bytes 12296 | tf_op jit(solution)/shard_map/ppermute | solution.py:333
  13.3 0.8 collective-permute-done
  14.1 18.4 %all_to_all.20.margin_parts = f32[32,8,128]{2,1,0:T(8,128)S(1)} all-to-all(f32[32,8,128]{2,1,0:T(8,128)S(1)} %broadcast_in_dim.2), channel_id=1, replica_groups=mesh['y'=4,'z'=8,'c'=2,'x'=4] {'y','z'}, dimensions={0} | all-to-all | bytes 262144 | tf_op jit(solution)/shard_map/all_to_all | solution.py:369
  32.6 2.2 %shard_map.87 = (f32[32,4096]{1,0:T(8,128)S(1)}, bf16[32,5120]{1,0:T(8,128)(2,1)S(1)}, bf16[32,5120]{1,0:T(8,128)(2,1)S(1)}, bf16[32,5120]{1,0:T(8,128)(2,1)S(1)}, f32[1,1024]{1,0:T(1,128)S(1)}) custom-call(f32[32,8,128]{2,1,0:T(8,128)S(1)} %all_to_all.20.margin_parts, s32[1,1024]{1,0:T(1,128)S(1)} %bitcast.14, s32[1,1024]{1,0:T(1,128)S(1)} %bitcast.15, ...), custom_call_target="tpu_custom_call" | custom-call | tf_op jit(solution)/shard_map/pallas_call | solution.py:26
  34.8 1.3 collective-permute-start.1
  36.0 2.5 %collective-permute-start.2 = (bf16[32,5120]{1,0:T(8,128)(2,1)S(1)}, bf16[32,5120]{1,0:T(8,128)(2,1)S(1)}, u32[]{:S(2)}, u32[]{:S(2)}) collective-permute-start(bf16[32,5120]{1,0:T(8,128)(2,1)S(1)} %get-tuple-element.28), channel_id=1, source_target_pairs={{0,2},{1,3},{2,0},{3,1},{4,6},{5,7},{6,4},{7,5},{8,10},{9,11},{10,... | collective-permute-start | bytes 983048 | tf_op jit(solution)/shard_map/ppermute | solution.py:325
  38.5 1.2 collective-permute-start.3
  39.6 3.5 %collective-permute-done.1.wire1 = bf16[32,5120]{1,0:T(8,128)(2,1)S(1)} collective-permute-done((bf16[32,5120]{1,0:T(8,128)(2,1)S(1)}, bf16[32,5120]{1,0:T(8,128)(2,1)S(1)}, u32[]{:S(2)}, u32[]{:S(2)}) %collective-permute-start.1) | collective-permute-done | bytes 327712 | tf_op jit(solution)/shard_map/ppermute | solution.py:325
  43.1 8.0 %collective-permute-done.2.wire2 = bf16[32,5120]{1,0:T(8,128)(2,1)S(1)} collective-permute-done((bf16[32,5120]{1,0:T(8,128)(2,1)S(1)}, bf16[32,5120]{1,0:T(8,128)(2,1)S(1)}, u32[]{:S(2)}, u32[]{:S(2)}) %collective-permute-start.2) | collective-permute-done | bytes 327712 | tf_op jit(solution)/shard_map/ppermute | solution.py:325
  51.2 0.7 collective-permute-done.3.wire3
  51.8 3.3 %shard_map.88 = (f32[32,1024]{1,0:T(8,128)S(1)}, bf16[4,32,1024]{2,1,0:T(8,128)(2,1)S(1)}, f32[32,768]{1,0:T(8,128)S(1)}, f32[32,768]{1,0:T(8,128)S(1)}) custom-call(f32[32,4096]{1,0:T(8,128)S(1)} %get-tuple-element.26.part, bf16[32,5120]{1,0:T(8,128)(2,1)S(1)} %collective-permute-done.1.wire1, bf16[32,5120]{1,0:T(8,128)(2,1)S(1)} %collective-permute-done.2.wire2, ...), custom_call_target="tpu_custom_call" | custom-call | tf_op jit(solution)/shard_map/pallas_call | solution.py:26
  55.2 2.4 %collective-permute-start.4 = (f32[32,768]{1,0:T(8,128)S(1)}, f32[32,768]{1,0:T(8,128)S(1)}, u32[]{:S(2)}, u32[]{:S(2)}) collective-permute-start(f32[32,768]{1,0:T(8,128)S(1)} %get-tuple-element.33), channel_id=1, source_target_pairs={{0,4},{4,0},{1,5},{5,1},{2,6},{6,2},{3,7},{7,3},{8,12},{12,8},{9,1... | collective-permute-start | bytes 294920 | tf_op jit(solution)/shard_map/ppermute | solution.py:333
  57.6 0.9 collective-permute-done.4.arrived
  58.6 1.0 collective-permute-start.7
  59.6 1.2 collective-permute-start.6
  60.8 0.9 collective-permute-done.7.wire3
  61.7 2.4 %collective-permute-done.6.wire2 = bf16[32,896]{1,0:T(8,128)(2,1)S(1)} collective-permute-done((bf16[32,896]{1,0:T(8,128)(2,1)S(1)}, bf16[32,896]{1,0:T(8,128)(2,1)S(1)}, u32[]{:S(2)}, u32[]{:S(2)}) %collective-permute-start.6) | collective-permute-done | bytes 57376 | tf_op jit(solution)/shard_map/ppermute | solution.py:325
  64.1 1.8 %collective-permute-done.5.wire1 = bf16[32,896]{1,0:T(8,128)(2,1)S(1)} collective-permute-done((bf16[32,896]{1,0:T(8,128)(2,1)S(1)}, bf16[32,896]{1,0:T(8,128)(2,1)S(1)}, u32[]{:S(2)}, u32[]{:S(2)}) %collective-permute-start.5) | collective-permute-done | bytes 57376 | tf_op jit(solution)/shard_map/ppermute | solution.py:325
  65.9 0.6 shard_map.90
  66.6 14.0 %all_to_all.21.arrived = bf16[8,32,640]{2,1,0:T(8,128)(2,1)S(1)} all-to-all(bf16[8,32,640]{2,1,0:T(8,128)(2,1)S(1)} %shard_map.90), channel_id=1, replica_groups=mesh['y'=4,'z'=8,'c'=2,'x'=4] {'z'}, dimensions={0} | all-to-all | bytes 655360 | tf_op jit(solution)/shard_map/all_to_all | solution.py:342
  80.6 0.7 shard_map.91
  81.3 3.5 %collective-permute-start.8 = (bf16[32,640]{1,0:T(8,128)(2,1)S(1)}, bf16[32,640]{1,0:T(8,128)(2,1)S(1)}, u32[]{:S(2)}, u32[]{:S(2)}) collective-permute-start(bf16[32,640]{1,0:T(8,128)(2,1)S(1)} %get-tuple-element.35.weighted), channel_id=1, source_target_pairs={{0,4},{4,0},{1,5},{5,1},{2,6},{6,2},{3,7},{7,3},{8,12},{12,8},{9,1... | collective-permute-start | bytes 122888 | tf_op jit(solution)/shard_map/ppermute | solution.py:333
  84.8 0.9 collective-permute-done.8.other
  85.7 2.1 %shard_map.92.part0 = bf16[32,4224]{1,0:T(8,128)(2,1)S(1)} custom-call(bf16[32,640]{1,0:T(8,128)(2,1)S(1)} %get-tuple-element.35.weighted, bf16[32,640]{1,0:T(8,128)(2,1)S(1)} %collective-permute-done.8.other, f32[32,256]{1,0:T(8,128)S(1)} %get-tuple-element.36.kept, bf16[1024,4096]{1,0:T(8,128)(2,1)S(1)} %get-tuple-element.25.examples, s32[4]{0:T(128)S(1)} %pad_add_fusion.place), custom_call_target="tpu_custom_call" | custom-call | tf_op jit(solution)/shard_map/pallas_call | solution.py:26
  87.8 2.0 %collective-permute-start.11 = (bf16[32,4224]{1,0:T(8,128)(2,1)S(1)}, bf16[32,4224]{1,0:T(8,128)(2,1)S(1)}, u32[]{:S(2)}, u32[]{:S(2)}) collective-permute-start(bf16[32,4224]{1,0:T(8,128)(2,1)S(1)} %shard_map.92.part0), channel_id=1, source_target_pairs={{0,3},{1,0},{2,1},{3,2},{4,7},{5,4},{6,5},{7,6},{8,11},{9,8},{10,9... | collective-permute-start | bytes 811016 | tf_op jit(solution)/shard_map/ppermute | solution.py:325
  89.8 0.9 collective-permute-start.10
  90.7 0.4 collective-permute-start.9
  91.1 4.5 %collective-permute-done.11.part3 = bf16[32,4224]{1,0:T(8,128)(2,1)S(1)} collective-permute-done((bf16[32,4224]{1,0:T(8,128)(2,1)S(1)}, bf16[32,4224]{1,0:T(8,128)(2,1)S(1)}, u32[]{:S(2)}, u32[]{:S(2)}) %collective-permute-start.11) | collective-permute-done | bytes 270368 | tf_op jit(solution)/shard_map/ppermute | solution.py:325
  95.6 3.1 %collective-permute-done.10.part2 = bf16[32,4224]{1,0:T(8,128)(2,1)S(1)} collective-permute-done((bf16[32,4224]{1,0:T(8,128)(2,1)S(1)}, bf16[32,4224]{1,0:T(8,128)(2,1)S(1)}, u32[]{:S(2)}, u32[]{:S(2)}) %collective-permute-start.10) | collective-permute-done | bytes 270368 | tf_op jit(solution)/shard_map/ppermute | solution.py:325
  98.8 6.8 %collective-permute-done.9.part1 = bf16[32,4224]{1,0:T(8,128)(2,1)S(1)} collective-permute-done((bf16[32,4224]{1,0:T(8,128)(2,1)S(1)}, bf16[32,4224]{1,0:T(8,128)(2,1)S(1)}, u32[]{:S(2)}, u32[]{:S(2)}) %collective-permute-start.9) | collective-permute-done | bytes 270368 | tf_op jit(solution)/shard_map/ppermute | solution.py:325
  105.5 3.3 %shard_map.93 = (f32[32,1024]{1,0:T(8,128)S(1)}, f32[32,768]{1,0:T(8,128)S(1)}, f32[32,768]{1,0:T(8,128)S(1)}, f32[32,128]{1,0:T(8,128)S(1)}) custom-call(bf16[32,4224]{1,0:T(8,128)(2,1)S(1)} %shard_map.92.part0, bf16[32,4224]{1,0:T(8,128)(2,1)S(1)} %collective-permute-done.9.part1, bf16[32,4224]{1,0:T(8,128)(2,1)S(1)} %collective-permute-done.10.part2, ...), custom_call_target="tpu_custom_call" | custom-call | tf_op jit(solution)/shard_map/pallas_call | solution.py:26
  108.9 0.6 collective-permute-start.12
  109.4 0.9 collective-permute-done.12.arrived
  110.5 0.5 collective-permute-start.15
  110.9 0.2 collective-permute-start.14
  111.2 0.9 collective-permute-start.13
  112.0 1.6 %collective-permute-done.15.wire3 = bf16[32,896]{1,0:T(8,128)(2,1)S(1)} collective-permute-done((bf16[32,896]{1,0:T(8,128)(2,1)S(1)}, bf16[32,896]{1,0:T(8,128)(2,1)S(1)}, u32[]{:S(2)}, u32[]{:S(2)}) %collective-permute-start.15) | collective-permute-done | bytes 57376 | tf_op jit(solution)/shard_map/ppermute | solution.py:325
  113.6 1.9 %collective-permute-done.14.wire2 = bf16[32,896]{1,0:T(8,128)(2,1)S(1)} collective-permute-done((bf16[32,896]{1,0:T(8,128)(2,1)S(1)}, bf16[32,896]{1,0:T(8,128)(2,1)S(1)}, u32[]{:S(2)}, u32[]{:S(2)}) %collective-permute-start.14) | collective-permute-done | bytes 57376 | tf_op jit(solution)/shard_map/ppermute | solution.py:325
  115.5 1.6 %collective-permute-done.13.wire1 = bf16[32,896]{1,0:T(8,128)(2,1)S(1)} collective-permute-done((bf16[32,896]{1,0:T(8,128)(2,1)S(1)}, bf16[32,896]{1,0:T(8,128)(2,1)S(1)}, u32[]{:S(2)}, u32[]{:S(2)}) %collective-permute-start.13) | collective-permute-done | bytes 57376 | tf_op jit(solution)/shard_map/ppermute | solution.py:325
  117.1 0.6 shard_map.95
  117.7 14.1 %all_to_all.22.arrived = bf16[8,32,640]{2,1,0:T(8,128)(2,1)S(1)} all-to-all(bf16[8,32,640]{2,1,0:T(8,128)(2,1)S(1)} %shard_map.95), channel_id=1, replica_groups=mesh['y'=4,'z'=8,'c'=2,'x'=4] {'z'}, dimensions={0} | all-to-all | bytes 655360 | tf_op jit(solution)/shard_map/all_to_all | solution.py:342
  131.9 0.7 shard_map.96
  132.6 10.0 %all_to_all.23.arrived = f32[8,32,128]{2,1,0:T(8,128)S(1)} all-to-all(f32[8,32,128]{2,1,0:T(8,128)S(1)} %shard_map.96), channel_id=1, replica_groups=mesh['y'=4,'z'=8,'c'=2,'x'=4] {'c','x'}, dimensions={0} | all-to-all | bytes 262144 | tf_op jit(solution)/shard_map/all_to_all | solution.py:447
  142.6 1.3 shard_map.97
  (16 shorter events, 0.3 us)
Async XLA Ops:
  0.6 31.9 %copy-start = (f32[32,1024]{1,0:T(8,128)S(1)}, f32[32,1024]{1,0:T(8,128)}, u32[]{:S(2)}) copy-start(f32[32,1024]{1,0:T(8,128)} %val_weight.1) | copy-start | bytes 393220
  1.5 0.7 copy-start.1
  2.2 0.7 copy-start.4
  2.9 29.7 %copy-start.2 = (s32[1024]{0:T(1024)S(1)}, s32[1024]{0:T(1024)}, u32[]{:S(2)}) copy-start(s32[1024]{0:T(1024)} %param.9) | copy-start | bytes 12292
  2.9 29.7 %copy-start.3 = (s32[1024]{0:T(1024)S(1)}, s32[1024]{0:T(1024)}, u32[]{:S(2)}) copy-start(s32[1024]{0:T(1024)} %param.10) | copy-start | bytes 12292
  10.0 4.2 %collective-permute-start = (f32[8,128]{1,0:T(8,128)S(1)}, f32[8,128]{1,0:T(8,128)S(1)}, u32[]{:S(2)}, u32[]{:S(2)}) collective-permute-start(f32[8,128]{1,0:T(8,128)S(1)} %get-tuple-element.24), channel_id=1, source_target_pairs={{0,4},{4,0},{1,5},{5,1},{2,6},{6,2},{3,7},{7,3},{8,12},{12,8},{9,1... | collective-permute-start | bytes 12296 | tf_op jit(solution)/shard_map/ppermute | solution.py:333
  34.8 8.4 %collective-permute-start.1 = (bf16[32,5120]{1,0:T(8,128)(2,1)S(1)}, bf16[32,5120]{1,0:T(8,128)(2,1)S(1)}, u32[]{:S(2)}, u32[]{:S(2)}) collective-permute-start(bf16[32,5120]{1,0:T(8,128)(2,1)S(1)} %get-tuple-element.27), channel_id=1, source_target_pairs={{0,1},{1,2},{2,3},{3,0},{4,5},{5,6},{6,7},{7,4},{8,9},{9,10},{10,1... | collective-permute-start | bytes 983048 | tf_op jit(solution)/shard_map/ppermute | solution.py:325
  36.0 15.1 %collective-permute-start.2 = (bf16[32,5120]{1,0:T(8,128)(2,1)S(1)}, bf16[32,5120]{1,0:T(8,128)(2,1)S(1)}, u32[]{:S(2)}, u32[]{:S(2)}) collective-permute-start(bf16[32,5120]{1,0:T(8,128)(2,1)S(1)} %get-tuple-element.28), channel_id=1, source_target_pairs={{0,2},{1,3},{2,0},{3,1},{4,6},{5,7},{6,4},{7,5},{8,10},{9,11},{10,... | collective-permute-start | bytes 983048 | tf_op jit(solution)/shard_map/ppermute | solution.py:325
  38.5 13.3 %collective-permute-start.3 = (bf16[32,5120]{1,0:T(8,128)(2,1)S(1)}, bf16[32,5120]{1,0:T(8,128)(2,1)S(1)}, u32[]{:S(2)}, u32[]{:S(2)}) collective-permute-start(bf16[32,5120]{1,0:T(8,128)(2,1)S(1)} %get-tuple-element.29), channel_id=1, source_target_pairs={{0,3},{1,0},{2,1},{3,2},{4,7},{5,4},{6,5},{7,6},{8,11},{9,8},{10,9... | collective-permute-start | bytes 983048 | tf_op jit(solution)/shard_map/ppermute | solution.py:325
  55.2 3.4 %collective-permute-start.4 = (f32[32,768]{1,0:T(8,128)S(1)}, f32[32,768]{1,0:T(8,128)S(1)}, u32[]{:S(2)}, u32[]{:S(2)}) collective-permute-start(f32[32,768]{1,0:T(8,128)S(1)} %get-tuple-element.33), channel_id=1, source_target_pairs={{0,4},{4,0},{1,5},{5,1},{2,6},{6,2},{3,7},{7,3},{8,12},{12,8},{9,1... | collective-permute-start | bytes 294920 | tf_op jit(solution)/shard_map/ppermute | solution.py:333
  58.6 3.1 %collective-permute-start.7 = (bf16[32,896]{1,0:T(8,128)(2,1)S(1)}, bf16[32,896]{1,0:T(8,128)(2,1)S(1)}, u32[]{:S(2)}, u32[]{:S(2)}) collective-permute-start(bf16[32,896]{1,0:T(8,128)(2,1)S(1)} %shard_map.89.wire0), channel_id=1, source_target_pairs={{0,192},{64,0},{128,64},{192,128},{1,193},{65,1},{129,65},{193,129... | collective-permute-start | bytes 172040 | tf_op jit(solution)/shard_map/ppermute | solution.py:325
  59.6 4.5 %collective-permute-start.6 = (bf16[32,896]{1,0:T(8,128)(2,1)S(1)}, bf16[32,896]{1,0:T(8,128)(2,1)S(1)}, u32[]{:S(2)}, u32[]{:S(2)}) collective-permute-start(bf16[32,896]{1,0:T(8,128)(2,1)S(1)} %shard_map.89.wire0), channel_id=1, source_target_pairs={{0,128},{64,192},{128,0},{192,64},{1,129},{65,193},{129,1},{193,65... | collective-permute-start | bytes 172040 | tf_op jit(solution)/shard_map/ppermute | solution.py:325
  60.8 5.1 %collective-permute-start.5 = (bf16[32,896]{1,0:T(8,128)(2,1)S(1)}, bf16[32,896]{1,0:T(8,128)(2,1)S(1)}, u32[]{:S(2)}, u32[]{:S(2)}) collective-permute-start(bf16[32,896]{1,0:T(8,128)(2,1)S(1)} %shard_map.89.wire0), channel_id=1, source_target_pairs={{0,64},{64,128},{128,192},{192,0},{1,65},{65,129},{129,193},{193,1... | collective-permute-start | bytes 172040 | tf_op jit(solution)/shard_map/ppermute | solution.py:325
  81.3 4.4 %collective-permute-start.8 = (bf16[32,640]{1,0:T(8,128)(2,1)S(1)}, bf16[32,640]{1,0:T(8,128)(2,1)S(1)}, u32[]{:S(2)}, u32[]{:S(2)}) collective-permute-start(bf16[32,640]{1,0:T(8,128)(2,1)S(1)} %get-tuple-element.35.weighted), channel_id=1, source_target_pairs={{0,4},{4,0},{1,5},{5,1},{2,6},{6,2},{3,7},{7,3},{8,12},{12,8},{9,1... | collective-permute-start | bytes 122888 | tf_op jit(solution)/shard_map/ppermute | solution.py:333
  87.8 54.8 %copy-start.5 = (f32[256]{0:T(256)S(1)}, f32[256]{0:T(256)}, u32[]{:S(2)}) copy-start(f32[256]{0:T(256)} %param.12) | copy-start | bytes 3076
  87.8 7.9 %collective-permute-start.11 = (bf16[32,4224]{1,0:T(8,128)(2,1)S(1)}, bf16[32,4224]{1,0:T(8,128)(2,1)S(1)}, u32[]{:S(2)}, u32[]{:S(2)}) collective-permute-start(bf16[32,4224]{1,0:T(8,128)(2,1)S(1)} %shard_map.92.part0), channel_id=1, source_target_pairs={{0,3},{1,0},{2,1},{3,2},{4,7},{5,4},{6,5},{7,6},{8,11},{9,8},{10,9... | collective-permute-start | bytes 811016 | tf_op jit(solution)/shard_map/ppermute | solution.py:325
  89.8 8.9 %collective-permute-start.10 = (bf16[32,4224]{1,0:T(8,128)(2,1)S(1)}, bf16[32,4224]{1,0:T(8,128)(2,1)S(1)}, u32[]{:S(2)}, u32[]{:S(2)}) collective-permute-start(bf16[32,4224]{1,0:T(8,128)(2,1)S(1)} %shard_map.92.part0), channel_id=1, source_target_pairs={{0,2},{1,3},{2,0},{3,1},{4,6},{5,7},{6,4},{7,5},{8,10},{9,11},{10,... | collective-permute-start | bytes 811016 | tf_op jit(solution)/shard_map/ppermute | solution.py:325
  90.7 14.8 %collective-permute-start.9 = (bf16[32,4224]{1,0:T(8,128)(2,1)S(1)}, bf16[32,4224]{1,0:T(8,128)(2,1)S(1)}, u32[]{:S(2)}, u32[]{:S(2)}) collective-permute-start(bf16[32,4224]{1,0:T(8,128)(2,1)S(1)} %shard_map.92.part0), channel_id=1, source_target_pairs={{0,1},{1,2},{2,3},{3,0},{4,5},{5,6},{6,7},{7,4},{8,9},{9,10},{10,1... | collective-permute-start | bytes 811016 | tf_op jit(solution)/shard_map/ppermute | solution.py:325
  108.9 1.5 %collective-permute-start.12 = (f32[32,768]{1,0:T(8,128)S(1)}, f32[32,768]{1,0:T(8,128)S(1)}, u32[]{:S(2)}, u32[]{:S(2)}) collective-permute-start(f32[32,768]{1,0:T(8,128)S(1)} %get-tuple-element.40), channel_id=1, source_target_pairs={{0,4},{4,0},{1,5},{5,1},{2,6},{6,2},{3,7},{7,3},{8,12},{12,8},{9,1... | collective-permute-start | bytes 294920 | tf_op jit(solution)/shard_map/ppermute | solution.py:333
  110.5 3.1 %collective-permute-start.15 = (bf16[32,896]{1,0:T(8,128)(2,1)S(1)}, bf16[32,896]{1,0:T(8,128)(2,1)S(1)}, u32[]{:S(2)}, u32[]{:S(2)}) collective-permute-start(bf16[32,896]{1,0:T(8,128)(2,1)S(1)} %shard_map.94.wire0), channel_id=1, source_target_pairs={{0,192},{64,0},{128,64},{192,128},{1,193},{65,1},{129,65},{193,129... | collective-permute-start | bytes 172040 | tf_op jit(solution)/shard_map/ppermute | solution.py:325
  110.9 4.5 %collective-permute-start.14 = (bf16[32,896]{1,0:T(8,128)(2,1)S(1)}, bf16[32,896]{1,0:T(8,128)(2,1)S(1)}, u32[]{:S(2)}, u32[]{:S(2)}) collective-permute-start(bf16[32,896]{1,0:T(8,128)(2,1)S(1)} %shard_map.94.wire0), channel_id=1, source_target_pairs={{0,128},{64,192},{128,0},{192,64},{1,129},{65,193},{129,1},{193,65... | collective-permute-start | bytes 172040 | tf_op jit(solution)/shard_map/ppermute | solution.py:325
  111.2 5.9 %collective-permute-start.13 = (bf16[32,896]{1,0:T(8,128)(2,1)S(1)}, bf16[32,896]{1,0:T(8,128)(2,1)S(1)}, u32[]{:S(2)}, u32[]{:S(2)}) collective-permute-start(bf16[32,896]{1,0:T(8,128)(2,1)S(1)} %shard_map.94.wire0), channel_id=1, source_target_pairs={{0,64},{64,128},{128,192},{192,0},{1,65},{65,129},{129,193},{193,1... | collective-permute-start | bytes 172040 | tf_op jit(solution)/shard_map/ppermute | solution.py:325

commit v3 on v2

v3 whole, which is shorter than its diff:
```python
import jax
import jax.numpy as jnp
from jax import lax
from jax.experimental import pallas as pl
from jax.experimental.pallas import tpu as pltpu
from jax.sharding import Mesh
from jax.sharding import PartitionSpec as P

F32 = jnp.float32
BF16 = jnp.bfloat16
NT = (((1,), (1,)), ((), ()))
NY, NZ, NC, NX = 4, 8, 2, 4
R = 32
N = 1024
HALF = N // NC
W = 4096
OWN = W // NX
NB = 256
TOTAL = float(N * NX)
LANES = 128
PART = OWN // 2
VMEM = pl.BlockSpec(memory_space=pltpu.VMEM)
SMEM = pl.BlockSpec(memory_space=pltpu.SMEM)
HBM = pl.BlockSpec(memory_space=pltpu.HBM)


def call(body, outs, *arrays, scratch=(), limit=16, smem=(), hbm=(), flops=0):
    specs = [SMEM if i in smem else HBM if i in hbm else VMEM for i in range(len(arrays))]
    arrays = [
        pltpu.with_memory_space_constraint(a, pltpu.HBM) if i in hbm else a
        for i, a in enumerate(arrays)
    ]
    return pl.pallas_call(
        body,
        out_shape=outs,
        in_specs=specs,
        out_specs=jax.tree.map(lambda _: VMEM, outs),
        scratch_shapes=scratch,
        compiler_params=pltpu.CompilerParams(vmem_limit_bytes=limit << 20),
        cost_estimate=pl.CostEstimate(flops=flops, bytes_accessed=4 << 20, transcendentals=0),
    )(*arrays)


def shape(*dims, dtype=F32):
    return jax.ShapeDtypeStruct(dims, dtype)


def lane_ids(lanes=LANES):
    return lax.broadcasted_iota(jnp.int32, (R, lanes), 1)


def column(tile, lane):
    return jnp.sum(jnp.where(lane_ids(tile.shape[1]) == lane, tile, 0.0), axis=1, keepdims=True)


def columns(values, first=0):
    lanes = lane_ids()
    tile = jnp.zeros((R, LANES), F32)
    for i, value in enumerate(values):
        tile = jnp.where(lanes == first + i, value, tile)
    return tile


def terms(value, count):
    found = []
    for _ in range(count):
        term = value.astype(BF16).astype(F32)
        found.append(term)
        value = value - term
    return found


def to_terms(tile):
    first, second, third = terms(tile, 3)
    return first + pltpu.roll(second, 8, 1) + pltpu.roll(third, 16, 1)


def from_terms(tile):
    total = tile + pltpu.roll(tile, LANES - 8, 1) + pltpu.roll(tile, LANES - 16, 1)
    return jnp.where(lane_ids() < 8, total, 0.0)


def chunk(index, size):
    return pl.ds(pl.multiple_of(index * size, size), size)


def block_sums(vec, weight, onehot):
    parts = jnp.concatenate(terms(vec * weight, 3), axis=0).astype(BF16)
    sums = lax.dot_general(parts, onehot, NT, preferred_element_type=F32)
    return sums[:R] + sums[R : 2 * R] + sums[2 * R :]


def prepare(ids, strengths, place, gradw, lamf, onehot):
    kinds = lax.broadcasted_iota(jnp.int32, (NB, OWN), 0)
    rows = lax.broadcasted_iota(jnp.int32, (16, NB), 0)
    split3 = jnp.zeros((16, NB), F32)
    for i, term in enumerate(terms(strengths[...], 3)):
        split3 = jnp.where(rows == i, term, split3)
    split3 = split3.astype(BF16)
    for j in range(NX):
        hot = (kinds == ids[:, j * OWN : (j + 1) * OWN]).astype(F32).astype(BF16)
        found = jnp.dot(split3, hot, preferred_element_type=F32)
        lamf[:, j * OWN : (j + 1) * OWN] = found[0:1] + found[1:2] + found[2:3]
    own = ids[:, chunk(place[3], OWN)]
    core = lax.shift_right_logical(own, 2) & 1
    moved = core * 128 + lax.shift_right_logical(own, 3) * 4 + (own & 3)
    onehot[...] = (kinds == moved).astype(F32).astype(BF16)


def margins(source, given, place, margin, examples, wfloat, weights, arrival):
    def fetch(i):
        rows = pl.ds(i * 128, 128)
        return pltpu.make_async_copy(source.at[rows], examples.at[rows], arrival.at[i])

    small = pltpu.make_async_copy(given, weights, arrival.at[8])
    small.start()
    for i in range(3):
        fetch(i).start()
    small.wait()
    lines = weights[...].astype(F32)
    line = jnp.concatenate([lines[i : i + 1] for i in range(W // LANES)], axis=1)
    wfloat[...] = line
    rhs = jnp.broadcast_to(line, (16, W)).astype(BF16)
    for i in range(8):
        fetch(i).wait()
        if i + 3 < 8:
            fetch(i + 3).start()
        rows = lax.dot_general(
            rhs, examples[i * 128 : (i + 1) * 128, :], NT, preferred_element_type=F32
        )
        margin[i : i + 1, :] = rows[0:1]


def part_of(owner, which):
    return pl.ds(pl.multiple_of(owner * OWN + which * PART, PART), PART)


def rhs_parts(which, gradw, examples, place, part, sends):
    for k in range(NX):
        found = jnp.dot(
            gradw, examples[:, part_of(k, which)], preferred_element_type=F32
        )
        cols = slice(k * PART, (k + 1) * PART)
        part[:, cols] = found
        high = found.astype(BF16)
        for send in sends:
            send[:, cols] = high
    for s, send in enumerate(sends):
        found = part[:, chunk((place[3] + s + 1) % NX, PART)]
        send[:, NX * PART :] = (found - found.astype(BF16).astype(F32)).astype(BF16)


def gradients(
    margin_parts, labels, split, val_weight, examples, place,
    part, send1, send2, send3, curvew, gradw,
):
    whole = jnp.sum(margin_parts[...], axis=0)
    margin = jnp.concatenate([whole[i : i + 1] for i in range(8)], axis=1)
    prob = 1.0 / (1.0 + jnp.exp(-margin))
    train = split[...].astype(F32)
    curvew[...] = train * prob * (1.0 - prob)
    err = (1.0 - train) * (prob - labels[...].astype(F32))
    found = (val_weight[...] * err / jnp.sqrt(F32(TOTAL))).astype(BF16)
    gradw[...] = found
    rhs_parts(0, found, examples, place, part, (send1, send2, send3))


def gradients_rest(gradw, examples, place, part, send1, send2, send3):
    rhs_parts(1, gradw[...], examples, place, part, (send1, send2, send3))


def tangents(pieces, which, examples, x, before, tang):
    for i in range(N // 256):
        rows = slice(i * 256, (i + 1) * 256)
        total = None if before is None else before[:, rows]
        for s, piece in enumerate(pieces):
            cols = part_of((x - s + NX) % NX, which)
            term = lax.dot_general(
                piece[...], examples[rows, cols], NT, preferred_element_type=F32
            )
            total = term if total is None else total + term
        tang[:, rows] = total


def halves(tang, scalars, blocks, core, keep, send):
    for out, which in ((keep, core), (send, 1 - core)):
        out[:, :HALF] = tang[:, chunk(which, HALF)]
        out[:, HALF : HALF + LANES] = scalars
        out[:, HALF + LANES :] = blocks[:, chunk(which, LANES)]


def first_part(
    which, part, wires, examples, lamf, wfloat, onehot, place, rhs, lows, before, tang
):
    x = place[3]
    for s in range(NX):
        cols = chunk((x - s + NX) % NX, PART)
        vec = part[:, cols] + sum(w[:, cols].astype(F32) for w in wires)
        if s == 0:
            vec = vec + sum(w[:, NX * PART :].astype(F32) for w in wires)
            rhs[...] = vec
            own = part_of(x, which)
            square = vec * vec
            norm = jnp.sum(square, axis=1, keepdims=True)
            scaled = jnp.sum(lamf[:, own] * square, axis=1, keepdims=True)
            hot = onehot[:, which * PART : (which + 1) * PART]
            blocks = block_sums(vec, wfloat[:, own], hot)
        lows[s] = vec.astype(BF16)
    tangents([lows.at[s] for s in range(NX)], which, examples, x, before, tang)
    return columns([norm, scaled]), blocks


def first_tangents(
    part, wire1, wire2, wire3, examples, lamf, wfloat, onehot, place,
    rhs, lows, tang, sums,
):
    scalars, blocks = first_part(
        0, part, (wire1, wire2, wire3), examples, lamf, wfloat, onehot, place,
        rhs, lows, None, tang,
    )
    sums[:, :LANES] = scalars
    sums[:, LANES:] = blocks


def first_tangents_rest(
    part, wire1, wire2, wire3, examples, lamf, wfloat, onehot, before, sums, place,
    rhs, lows, keep, send, tang, total,
):
    scalars, blocks = first_part(
        1, part, (wire1, wire2, wire3), examples, lamf, wfloat, onehot, place,
        rhs, lows, before, tang,
    )
    total[...] = sums[:, LANES:] + blocks
    halves(tang, sums[:, :LANES] + scalars, total, place[2], keep, send)


def to_wire(keep, arrived, wire):
    total = keep[...] + arrived[...]
    wire[:, :HALF] = total[:, :HALF].astype(BF16)
    wire[:, HALF : HALF + LANES] = to_terms(total[:, HALF : HALF + LANES]).astype(BF16)
    high, rest = terms(total[:, HALF + LANES :], 2)
    wire[:, HALF + LANES : HALF + 2 * LANES] = high.astype(BF16)
    wire[:, HALF + 2 * LANES :] = rest.astype(BF16)


def along_y(wire0, wire1, wire2, wire3, place, out):
    total = wire0[...].astype(F32)
    for wire in (wire1, wire2, wire3):
        total = total + wire[...].astype(F32)
    tang = total[:, :HALF].astype(BF16)
    tile = to_terms(from_terms(total[:, HALF : HALF + LANES]))
    blocks = total[:, HALF + LANES : HALF + 2 * LANES] + total[:, HALF + 2 * LANES :]
    high, rest = terms(blocks, 2)
    lanes = lane_ids()
    at64 = pltpu.roll(high, (64 - 32 * place[0] + LANES) % LANES, 1)
    at96 = pltpu.roll(rest, (96 - 32 * place[0] + LANES) % LANES, 1)
    tile = jnp.where(lanes >= 96, at96, jnp.where(lanes >= 64, at64, tile)).astype(BF16)
    for i in range(NZ):
        out[i, :, :HALF] = tang
        out[i, :, HALF:] = tile


def along_z(arrived):
    tang = arrived[0, :, :HALF].astype(F32)
    tile = arrived[0, :, HALF:].astype(F32)
    for i in range(1, NZ):
        tang = tang + arrived[i, :, :HALF].astype(F32)
        tile = tile + arrived[i, :, HALF:].astype(F32)
    blocks = pltpu.roll(tile, 64, 1) + pltpu.roll(tile, 32, 1)
    return tang, from_terms(tile), jnp.where(lane_ids() < 32, blocks, 0.0)


def weigh(arrived, curvew, place, tang_out, weighted, kept):
    tang, scalars, blocks = along_z(arrived)
    tang_out[...] = tang
    half = curvew[:, chunk(place[2], HALF)]
    product = half * tang
    weighted[:, :HALF] = product.astype(BF16)
    curv = columns([jnp.sum(product * tang, axis=1, keepdims=True)], 2)
    weighted[:, HALF:] = to_terms(curv).astype(BF16)
    kept[:, :LANES] = scalars + curv
    kept[:, LANES:] = blocks


def product_parts(which, weighted, other, examples, place, part):
    core = place[2]
    for k in range(NX):
        cols = part_of(k, which)
        mine = jnp.dot(
            weighted[:, :HALF], examples[chunk(core, HALF), cols], preferred_element_type=F32
        )
        rest = jnp.dot(
            other[:, :HALF], examples[chunk(1 - core, HALF), cols], preferred_element_type=F32
        )
        part[:, k * PART : (k + 1) * PART] = (mine + rest).astype(BF16)


def products(weighted, other, kept, examples, place, part):
    scalars = kept[:, :LANES] + from_terms(other[:, HALF:].astype(F32))
    part[:, NX * PART :] = to_terms(scalars).astype(BF16)
    product_parts(0, weighted, other, examples, place, part)


def products_rest(weighted, other, examples, place, part):
    product_parts(1, weighted, other, examples, place, part)


def second_part(
    which, alpha, parts, rhs, lows, examples, lamf, wfloat, onehot, place,
    resid, pieces, before, tang,
):
    x = place[3]
    for s in range(NX):
        owner = (x - s + NX) % NX
        total = sum(p[:, chunk(owner, PART)].astype(F32) for p in parts)
        direc = rhs[...] if s == 0 else lows[s].astype(F32)
        cols = part_of(owner, which)
        lam = lamf[:, cols]
        left = direc - alpha * (total / F32(TOTAL) + lam * direc)
        pieces[s] = left.astype(BF16)
        if s == 0:
            resid[...] = left
            scalars = columns(
                [
                    jnp.sum(left * left, axis=1, keepdims=True),
                    jnp.sum(lam * left * left, axis=1, keepdims=True),
                    jnp.sum(lam * left * direc, axis=1, keepdims=True),
                ]
            )
            hot = onehot[:, which * PART : (which + 1) * PART]
            blocks = block_sums(left, wfloat[:, cols], hot)
    tangents([pieces.at[s] for s in range(NX)], which, examples, x, before, tang)
    return scalars, blocks


def second_tangents(
    part0, part1, part2, part3, rhs, lows, examples, lamf, wfloat, onehot, place,
    resid, tang, sums, kept, pieces,
):
    parts = (part0, part1, part2, part3)
    tile = from_terms(sum(p[:, NX * PART :].astype(F32) for p in parts))
    norm, scaled, curv = (column(tile, i) for i in range(3))
    alpha = norm / (curv / F32(TOTAL) + scaled)
    kept[...] = jnp.where(lane_ids() == 3, alpha, tile)
    scalars, blocks = second_part(
        0, alpha, parts, rhs, lows, examples, lamf, wfloat, onehot, place,
        resid, pieces, None, tang,
    )
    sums[:, :LANES] = scalars
    sums[:, LANES:] = blocks


def second_tangents_rest(
    part0, part1, part2, part3, rhs, lows, examples, lamf, wfloat, onehot, before, sums, kept,
    place, resid, keep, send, tang, total, pieces,
):
    scalars, blocks = second_part(
        1, column(kept[...], 3), (part0, part1, part2, part3), rhs, lows, examples, lamf,
        wfloat, onehot, place, resid, pieces, before, tang,
    )
    total[...] = sums[:, LANES:] + blocks
    halves(tang, sums[:, :LANES] + scalars, total, place[2], keep, send)


def curvature(arrived, curvew, tang_first, kept, place, out):
    tang, scalars, blocks = along_z(arrived)
    half = curvew[:, chunk(place[2], HALF)]
    product = half * tang
    both = jnp.sum(product * tang, axis=1, keepdims=True)
    cross = jnp.sum(product * tang_first[...], axis=1, keepdims=True)
    tile = jnp.where(lane_ids() < 3, scalars, columns([both, cross], 3))
    lanes = lane_ids()
    shift = 4 * place[1]
    now = pltpu.roll(blocks, (32 - shift + LANES) % LANES, 1)
    before = pltpu.roll(kept[:, LANES:], (36 - shift + LANES) % LANES, 1)
    tile = jnp.where((lanes >= 32) & (lanes < 36), now, tile)
    tile = jnp.where((lanes >= 36) & (lanes < 40), before, tile)
    for i in range(NC * NX):
        out[i] = tile


def finish(
    arrived, kept, rhs_a, rhs_b, resid_a, resid_b, strengths, place, solve, hyper
):
    core, x = place[2], place[3]
    mine = sum(arrived[core * NX + i] for i in range(NX))
    rest = sum(arrived[(1 - core) * NX + i] for i in range(NX))
    every = mine + rest
    tile = kept[...]
    norm, scaled_first, curv_first, alpha = (column(tile, i) for i in range(4))
    norm_next, scaled, mixed = (column(mine, i) for i in range(3))
    both, cross = column(every, 3), column(every, 4)
    beta = norm_next / norm
    curv = (both + 2.0 * beta * cross + beta * beta * curv_first) / F32(TOTAL)
    curv = curv + (scaled + 2.0 * beta * mixed + beta * beta * scaled_first)
    alpha_next = norm_next / curv
    for i, (rhs, resid) in enumerate(((rhs_a, resid_a), (rhs_b, resid_b))):
        first = rhs[...]
        solve[:, i * PART : (i + 1) * PART] = alpha * first + alpha_next * (
            resid[...] + beta * first
        )
    now, before = column(mine, 32 + x), column(mine, 36 + x)
    block = ((place[0] * NZ + place[1]) * NC + core) * NX + x
    kinds = lax.broadcasted_iota(jnp.int32, (1, NB), 1)
    strength = jnp.sum(jnp.where(kinds == block, strengths[...], 0.0), axis=1, keepdims=True)
    found = -strength * (alpha * before + alpha_next * (now + beta * before))
    hyper[...] = jnp.transpose(jnp.broadcast_to(found, (R, LANES)))[0:1]


def shift(array, axis, length, by):
    return lax.ppermute(array, axis, [(i, (i + by) % length) for i in range(length)])


def shifted(array, axis, length):
    return [shift(array, axis, length, s) for s in range(1, length)]


def swapped(array):
    return lax.ppermute(array, "c", [(0, 1), (1, 0)])


def summed(keep, send, place):
    wire = call(to_wire, shape(R, HALF + 3 * LANES, dtype=BF16), keep, swapped(send))
    arrived = shifted(wire, "y", NY)
    out = call(
        along_y, shape(NZ, R, HALF + LANES, dtype=BF16), wire, *arrived, place, smem=(4,)
    )
    return lax.all_to_all(out, "z", 0, 0, tiled=True)


def shards(examples, weights, labels, split, val_weight, strengths, block_ids):
    place = jnp.stack([lax.axis_index(axis) for axis in ("y", "z", "c", "x")]).astype(jnp.int32)
    strengths = strengths.reshape(1, NB)
    margin, examples, wfloat = call(
        margins,
        [shape(8, 128), pltpu.VMEM((N, W), BF16), shape(1, W)],
        examples,
        weights.reshape(W // LANES, LANES),
        place,
        scratch=[pltpu.VMEM((W // LANES, LANES), BF16), pltpu.SemaphoreType.DMA((9,))],
        hbm=(0, 1),
        smem=(2,),
    )
    margin = margin + swapped(margin)
    margin_parts = lax.all_to_all(
        jnp.broadcast_to(margin[None], (NY * NZ, 8, 128)), ("y", "z"), 0, 0, tiled=True
    )
    work = 2 * R * N * W // 2
    sends = [shape(R, (NX + 1) * PART, dtype=BF16)] * (NX - 1)
    part_a, *sends_a, curvew, gradw = call(
        gradients,
        [shape(R, NX * PART), *sends, shape(1, N), shape(R, N, dtype=BF16)],
        margin_parts,
        labels.reshape(1, N),
        split.reshape(1, N),
        val_weight,
        examples,
        place,
        smem=(5,),
        flops=work,
    )
    wires_a = [shift(send, "x", NX, s + 1) for s, send in enumerate(sends_a)]
    part_b, *sends_b = call(
        gradients_rest,
        [shape(R, NX * PART), *sends],
        gradw,
        examples,
        place,
        smem=(2,),
        flops=work,
    )
    lamf, onehot = call(
        prepare,
        [shape(1, W), shape(NB, OWN, dtype=BF16)],
        block_ids.reshape(1, W),
        strengths,
        place,
        gradw,
        smem=(2,),
    )
    wires_b = [shift(send, "x", NX, s + 1) for s, send in enumerate(sends_b)]
    pair = [shape(R, HALF + 2 * LANES)] * 2
    low = shape(NX, R, PART, dtype=BF16)
    rhs_a, lows_a, tang, sums = call(
        first_tangents,
        [shape(R, PART), low, shape(R, N), shape(R, LANES + NB)],
        part_a,
        *wires_a,
        examples,
        lamf,
        wfloat,
        onehot,
        place,
        smem=(8,),
        flops=work,
    )
    rhs_b, lows_b, keep, send = call(
        first_tangents_rest,
        [shape(R, PART), low, *pair],
        part_b,
        *wires_b,
        examples,
        lamf,
        wfloat,
        onehot,
        tang,
        sums,
        place,
        scratch=[pltpu.VMEM((R, N), F32), pltpu.VMEM((R, NB), F32)],
        smem=(10,),
        flops=work,
    )
    arrived = summed(keep, send, place)
    tang_first, weighted, kept_first = call(
        weigh,
        [shape(R, HALF), shape(R, HALF + LANES, dtype=BF16), shape(R, 2 * LANES)],
        arrived,
        curvew,
        place,
        smem=(2,),
    )
    other = swapped(weighted)
    part_a = call(
        products,
        shape(R, NX * PART + LANES, dtype=BF16),
        weighted,
        other,
        kept_first,
        examples,
        place,
        smem=(4,),
        flops=work,
    )
    wires_a = shifted(part_a, "x", NX)
    part_b = call(
        products_rest,
        shape(R, NX * PART, dtype=BF16),
        weighted,
        other,
        examples,
        place,
        smem=(3,),
        flops=work,
    )
    wires_b = shifted(part_b, "x", NX)
    resid_a, tang, sums, kept = call(
        second_tangents,
        [shape(R, PART), shape(R, N), shape(R, LANES + NB), shape(R, LANES)],
        part_a,
        *wires_a,
        rhs_a,
        lows_a,
        examples,
        lamf,
        wfloat,
        onehot,
        place,
        scratch=[pltpu.VMEM((NX, R, PART), BF16)],
        smem=(10,),
        flops=work,
    )
    resid_b, keep, send = call(
        second_tangents_rest,
        [shape(R, PART), *pair],
        part_b,
        *wires_b,
        rhs_b,
        lows_b,
        examples,
        lamf,
        wfloat,
        onehot,
        tang,
        sums,
        kept,
        place,
        scratch=[
            pltpu.VMEM((R, N), F32),
            pltpu.VMEM((R, NB), F32),
            pltpu.VMEM((NX, R, PART), BF16),
        ],
        smem=(13,),
        flops=work,
    )
    arrived = summed(keep, send, place)
    out = call(
        curvature,
        shape(NC * NX, R, LANES),
        arrived,
        curvew,
        tang_first,
        kept_first,
        place,
        smem=(4,),
    )
    arrived = lax.all_to_all(out, ("c", "x"), 0, 0, tiled=True)
    solve, hyper = call(
        finish,
        [shape(R, OWN), shape(1, R)],
        arrived,
        kept,
        rhs_a,
        rhs_b,
        resid_a,
        resid_b,
        strengths,
        place,
        smem=(7,),
    )
    return solve, hyper.reshape(R, 1)


def solution(mesh):
    fine = Mesh(mesh.devices.reshape(NY, NZ, NC, NX), ("y", "z", "c", "x"))
    feat = ("y", "z", "c")
    placed = (P("x", feat), P(feat), P("x"), P("x"), P(None, "x"), P(), P(feat))
    return jax.shard_map(
        shards,
        mesh=fine,
        in_specs=placed,
        out_specs=(P(None, (*feat, "x")), P(None, (*feat, "x"))),
        check_vma=False,
    )
```

time: 144 us -> 137 us (0.951)
  waiting for transfers between devices: 40.3 us -> 19.1 us
  starting transfers between devices: 21.8 us -> 33.3 us
  Pallas kernels: 22.2 us -> 26.3 us
    ppermute x12 -> x18, waiting for transfers between devices: 36.7 us -> 15.5 us  [shift(): lax.ppermute(array, axis, [(i, (i + by) % length) for i in range(length)])]
    ppermute x12 -> x18, starting transfers between devices: 11.9 us -> 21.2 us  [shift(): lax.ppermute(array, axis, [(i, (i + by) % length) for i in range(length)])]
    pallas_call x12 -> x17, Pallas kernels: 22.2 us -> 26.3 us  [call(): pl.pallas_call(body, out_shape=outs, in_specs=specs, out_specs=jax.tree.m...]
    ppermute x4, starting transfers between devices: 9.85 us -> 12.1 us  [swapped(): return lax.ppermute(array, 'c', [(0, 1), (1, 0)])]
    all_to_all x1, blocking collectives: 10 us -> 12.1 us  [shards(): arrived = lax.all_to_all(out, ('c', 'x'), 0, 0, tiled=True)]
    all_to_all x2, blocking collectives: 28.1 us -> 26.2 us  [summed(): return lax.all_to_all(out, 'z', 0, 0, tiled=True)]
  transfers between devices with their start and end apart: 16 -> 22, of which waited for: 16 -> 16; matrix products, arithmetic and copies ran while one was open for 0% -> 0% of each run, Pallas kernels for 0% -> 6%
where the time goes in v3:
time: 137 us; the launch traced here: 136 us
  blocking collectives  56.8 us (41%)
  starting transfers between devices  33.3 us (24%)
  Pallas kernels  26.3 us (19%)
  waiting for transfers between devices  19.1 us (14%)
    pallas_call x17, Pallas kernels, call(): pl.pallas_call(body, out_shape=outs, in_specs=specs, out_specs=jax.tree.m...  26.3 us
    all_to_all x2, blocking collectives, summed(): return lax.all_to_all(out, 'z', 0, 0, tiled=True)  26.2 us
    ppermute x18, starting transfers between devices, shift(): lax.ppermute(array, axis, [(i, (i + by) % length) for i in range(length)])  21.2 us
    all_to_all x1, blocking collectives, shards(): lax.all_to_all(jnp.broadcast_to(margin[None], (NY * NZ, 8, 128)), ('y', '...  18.4 us
    ppermute x18, waiting for transfers between devices, shift(): lax.ppermute(array, axis, [(i, (i + by) % length) for i in range(length)])  15.5 us
    all_to_all x1, blocking collectives, shards(): arrived = lax.all_to_all(out, ('c', 'x'), 0, 0, tiled=True)  12.1 us
    ppermute x4, starting transfers between devices, swapped(): return lax.ppermute(array, 'c', [(0, 1), (1, 0)])  12.1 us
    ppermute x4, waiting for transfers between devices, swapped(): return lax.ppermute(array, 'c', [(0, 1), (1, 0)])  3.58 us
  transfers between devices with their start and end apart: 22, of which 16 were waited for; matrix products, arithmetic and copies ran while one was open for 0% of the time, Pallas kernels for 6%

profile of v3, /device:TPU:1, one launch (start us, length us, event | category | flops | bytes accessed | tf_op | source)
XLA Modules:
  0.0 136.4 jit_solution(1574946290530109943)
XLA Ops:
  0.7 7.1 %shard_map.86 = (f32[8,128]{1,0:T(8,128)S(1)}, bf16[1024,4096]{1,0:T(8,128)(2,1)S(1)}, f32[1,4096]{1,0:T(1,128)S(1)}) custom-call(bf16[1024,4096]{1,0:T(8,128)(2,1)} %source.1, bf16[32,128]{1,0:T(8,128)(2,1)} %bitcast.15, s32[4]{0:T(128)S(1)} %pad_add_fusion.place), custom_call_target="tpu_custom_call" | custom-call | bytes 4194304 | tf_op jit(solution)/shard_map/pallas_call | solution.py:33
  7.9 3.3 %collective-permute-start = (f32[8,128]{1,0:T(8,128)S(1)}, f32[8,128]{1,0:T(8,128)S(1)}, u32[]{:S(2)}, u32[]{:S(2)}) collective-permute-start(f32[8,128]{1,0:T(8,128)S(1)} %get-tuple-element.37), channel_id=1, source_target_pairs={{0,4},{4,0},{1,5},{5,1},{2,6},{6,2},{3,7},{7,3},{8,12},{12,8},{9,1... | collective-permute-start | bytes 12296 | tf_op jit(solution)/shard_map/ppermute | solution.py:419
  11.2 0.8 collective-permute-done
  12.0 18.4 %all_to_all.20.margin_parts = f32[32,8,128]{2,1,0:T(8,128)S(1)} all-to-all(f32[32,8,128]{2,1,0:T(8,128)S(1)} %broadcast_in_dim.2), channel_id=1, replica_groups=mesh['y'=4,'z'=8,'c'=2,'x'=4] {'y','z'}, dimensions={0} | all-to-all | bytes 262144 | tf_op jit(solution)/shard_map/all_to_all | solution.py:445
  30.5 1.4 %shard_map.87 = (f32[32,2048]{1,0:T(8,128)S(1)}, bf16[32,2560]{1,0:T(8,128)(2,1)S(1)}, bf16[32,2560]{1,0:T(8,128)(2,1)S(1)}, bf16[32,2560]{1,0:T(8,128)(2,1)S(1)...) custom-call(f32[32,8,128]{2,1,0:T(8,128)S(1)} %all_to_all.20.margin_parts, s32[1,1024]{1,0:T(1,128)S(1)} %bitcast.11, ...), custom_call_target="tpu_custom_call" | custom-call | flops 134217728 | bytes 4194304 | tf_op jit(solution)/shard_map/pallas_call | solution.py:33
  32.0 1.3 collective-permute-start.4
  33.2 2.5 %collective-permute-start.5 = (bf16[32,2560]{1,0:T(8,128)(2,1)S(1)}, bf16[32,2560]{1,0:T(8,128)(2,1)S(1)}, u32[]{:S(2)}, u32[]{:S(2)}) collective-permute-start(bf16[32,2560]{1,0:T(8,128)(2,1)S(1)} %get-tuple-element.49), channel_id=1, source_target_pairs={{0,2},{1,3},{2,0},{3,1},{4,6},{5,7},{6,4},{7,5},{8,10},{9,11},{10,... | collective-permute-start | bytes 491528 | tf_op jit(solution)/shard_map/ppermute | solution.py:411
  35.7 1.2 collective-permute-start.6
  36.8 1.4 %shard_map.88 = (f32[32,2048]{1,0:T(8,128)S(1)}, bf16[32,2560]{1,0:T(8,128)(2,1)S(1)}, bf16[32,2560]{1,0:T(8,128)(2,1)S(1)}, bf16[32,2560]{1,0:T(8,128)(2,1)S(1)}) custom-call(bf16[32,1024]{1,0:T(8,128)(2,1)S(1)} %get-tuple-element.39.gradw, bf16[1024,4096]{1,0:T(8,128)(2,1)S(1)} %get-tuple-element.38.examples, s32[4]{0:T(128)S(1)} %pad_add_fusion.place), custom_call_target="tpu_custom_call" | custom-call | flops 134217728 | bytes 4194304 | tf_op jit(solution)/shard_map/pallas_call | solution.py:33
  38.6 0.9 collective-permute-start.2
  39.5 1.6 %collective-permute-start.3 = (bf16[32,2560]{1,0:T(8,128)(2,1)S(1)}, bf16[32,2560]{1,0:T(8,128)(2,1)S(1)}, u32[]{:S(2)}, u32[]{:S(2)}) collective-permute-start(bf16[32,2560]{1,0:T(8,128)(2,1)S(1)} %get-tuple-element.43), channel_id=1, source_target_pairs={{0,3},{1,0},{2,1},{3,2},{4,7},{5,4},{6,5},{7,6},{8,11},{9,8},{10,9... | collective-permute-start | bytes 491528 | tf_op jit(solution)/shard_map/ppermute | solution.py:411
  41.1 1.2 shard_map.89
  42.4 1.9 %shard_map.90 = (f32[32,512]{1,0:T(8,128)S(1)}, bf16[4,32,512]{2,1,0:T(8,128)(2,1)S(1)}, f32[32,1024]{1,0:T(8,128)S(1)}, f32[32,384]{1,0:T(8,128)S(1)}) custom-call(f32[32,2048]{1,0:T(8,128)S(1)} %get-tuple-element.47.part, bf16[32,2560]{1,0:T(8,128)(2,1)S(1)} %collective-permute-done.4.wire1, bf16[32,2560]{1,0:T(8,128)(2,1)S(1)} %collective-permute-done.5.wire2, ...), custom_call_target="tpu_custom_call" | custom-call | flops 134217728 | bytes 4194304 | tf_op jit(solution)/shard_map/pallas_call | solution.py:33
  44.9 3.2 %collective-permute-done.2.wire2 = bf16[32,2560]{1,0:T(8,128)(2,1)S(1)} collective-permute-done((bf16[32,2560]{1,0:T(8,128)(2,1)S(1)}, bf16[32,2560]{1,0:T(8,128)(2,1)S(1)}, u32[]{:S(2)}, u32[]{:S(2)}) %collective-permute-start.2) | collective-permute-done | bytes 163872 | tf_op jit(solution)/shard_map/ppermute | solution.py:411
  48.5 2.0 %shard_map.91 = (f32[32,512]{1,0:T(8,128)S(1)}, bf16[4,32,512]{2,1,0:T(8,128)(2,1)S(1)}, f32[32,768]{1,0:T(8,128)S(1)}, f32[32,768]{1,0:T(8,128)S(1)}) custom-call(f32[32,2048]{1,0:T(8,128)S(1)} %get-tuple-element.40.part, bf16[32,2560]{1,0:T(8,128)(2,1)S(1)} %collective-permute-done.1.wire1, bf16[32,2560]{1,0:T(8,128)(2,1)S(1)} %collective-permute-done.2.wire2, ...), custom_call_target="tpu_custom_call" | custom-call | flops 134217728 | bytes 4194304 | tf_op jit(solution)/shard_map/pallas_call | solution.py:33
  50.5 3.0 %collective-permute-start.7 = (f32[32,768]{1,0:T(8,128)S(1)}, f32[32,768]{1,0:T(8,128)S(1)}, u32[]{:S(2)}, u32[]{:S(2)}) collective-permute-start(f32[32,768]{1,0:T(8,128)S(1)} %get-tuple-element.54), channel_id=1, source_target_pairs={{0,4},{4,0},{1,5},{5,1},{2,6},{6,2},{3,7},{7,3},{8,12},{12,8},{9,1... | collective-permute-start | bytes 294920 | tf_op jit(solution)/shard_map/ppermute | solution.py:419
  53.5 0.9 collective-permute-done.7.arrived
  54.5 0.9 collective-permute-start.10
  56.0 1.1 collective-permute-start.9
  57.6 2.1 %collective-permute-done.8.wire1 = bf16[32,896]{1,0:T(8,128)(2,1)S(1)} collective-permute-done((bf16[32,896]{1,0:T(8,128)(2,1)S(1)}, bf16[32,896]{1,0:T(8,128)(2,1)S(1)}, u32[]{:S(2)}, u32[]{:S(2)}) %collective-permute-start.8) | collective-permute-done | bytes 57376 | tf_op jit(solution)/shard_map/ppermute | solution.py:411
  59.7 0.9 collective-permute-done.9.wire2
  60.6 0.7 shard_map.93
  61.3 12.9 %all_to_all.21.arrived = bf16[8,32,640]{2,1,0:T(8,128)(2,1)S(1)} all-to-all(bf16[8,32,640]{2,1,0:T(8,128)(2,1)S(1)} %shard_map.93), channel_id=1, replica_groups=mesh['y'=4,'z'=8,'c'=2,'x'=4] {'z'}, dimensions={0} | all-to-all | bytes 655360 | tf_op jit(solution)/shard_map/all_to_all | solution.py:428
  74.2 0.7 shard_map.94
  74.9 4.5 %collective-permute-start.11 = (bf16[32,640]{1,0:T(8,128)(2,1)S(1)}, bf16[32,640]{1,0:T(8,128)(2,1)S(1)}, u32[]{:S(2)}, u32[]{:S(2)}) collective-permute-start(bf16[32,640]{1,0:T(8,128)(2,1)S(1)} %get-tuple-element.56.weighted), channel_id=1, source_target_pairs={{0,4},{4,0},{1,5},{5,1},{2,6},{6,2},{3,7},{7,3},{8,12},{12,8},{9,1... | collective-permute-start | bytes 122888 | tf_op jit(solution)/shard_map/ppermute | solution.py:419
  79.4 0.9 collective-permute-done.11.other
  80.2 1.4 %shard_map.96.part0 = bf16[32,2176]{1,0:T(8,128)(2,1)S(1)} custom-call(bf16[32,640]{1,0:T(8,128)(2,1)S(1)} %get-tuple-element.56.weighted, bf16[32,640]{1,0:T(8,128)(2,1)S(1)} %collective-permute-done.11.other, f32[32,256]{1,0:T(8,128)S(1)} %get-tuple-element.59.kept, bf16[1024,4096]{1,0:T(8,128)(2,1)S(1)} %get-tuple-element.38.examples, s32[4]{0:T(128)S(1)} %pad_add_fusion.place), custom_call_target="tpu_custom_call" | custom-call | flops 134217728 | bytes 4194304 | tf_op jit(solution)/shard_map/pallas_call | solution.py:33
  81.6 1.1 collective-permute-start.15
  82.7 2.2 %collective-permute-start.16 = (bf16[32,2176]{1,0:T(8,128)(2,1)S(1)}, bf16[32,2176]{1,0:T(8,128)(2,1)S(1)}, u32[]{:S(2)}, u32[]{:S(2)}) collective-permute-start(bf16[32,2176]{1,0:T(8,128)(2,1)S(1)} %shard_map.96.part0), channel_id=1, source_target_pairs={{0,2},{1,3},{2,0},{3,1},{4,6},{5,7},{6,4},{7,5},{8,10},{9,11},{10,... | collective-permute-start | bytes 417800 | tf_op jit(solution)/shard_map/ppermute | solution.py:411
  84.9 1.2 collective-permute-start.17
  86.1 1.4 %shard_map.95.part0 = bf16[32,2048]{1,0:T(8,128)(2,1)S(1)} custom-call(bf16[32,640]{1,0:T(8,128)(2,1)S(1)} %get-tuple-element.56.weighted, bf16[32,640]{1,0:T(8,128)(2,1)S(1)} %collective-permute-done.11.other, bf16[1024,4096]{1,0:T(8,128)(2,1)S(1)} %get-tuple-element.38.examples, s32[4]{0:T(128)S(1)} %pad_add_fusion.place), custom_call_target="tpu_custom_call" | custom-call | flops 134217728 | bytes 4194304 | tf_op jit(solution)/shard_map/pallas_call | solution.py:33
  87.7 0.9 collective-permute-start.13
  88.6 1.6 %collective-permute-start.14 = (bf16[32,2048]{1,0:T(8,128)(2,1)S(1)}, bf16[32,2048]{1,0:T(8,128)(2,1)S(1)}, u32[]{:S(2)}, u32[]{:S(2)}) collective-permute-start(bf16[32,2048]{1,0:T(8,128)(2,1)S(1)} %shard_map.95.part0), channel_id=1, source_target_pairs={{0,3},{1,0},{2,1},{3,2},{4,7},{5,4},{6,5},{7,6},{8,11},{9,8},{10,9... | collective-permute-start | bytes 393224 | tf_op jit(solution)/shard_map/ppermute | solution.py:411
  90.2 1.1 collective-permute-done.16.part2
  91.3 2.1 %shard_map.97 = (f32[32,512]{1,0:T(8,128)S(1)}, f32[32,1024]{1,0:T(8,128)S(1)}, f32[32,384]{1,0:T(8,128)S(1)}, f32[32,128]{1,0:T(8,128)S(1)}) custom-call(bf16[32,2176]{1,0:T(8,128)(2,1)S(1)} %shard_map.96.part0, bf16[32,2176]{1,0:T(8,128)(2,1)S(1)} %collective-permute-done.15.part1, bf16[32,2176]{1,0:T(8,128)(2,1)S(1)} %collective-permute-done.16.part2, ...), custom_call_target="tpu_custom_call" | custom-call | flops 134217728 | bytes 4194304 | tf_op jit(solution)/shard_map/pallas_call | solution.py:33
  94.0 3.0 %collective-permute-done.13.part2 = bf16[32,2048]{1,0:T(8,128)(2,1)S(1)} collective-permute-done((bf16[32,2048]{1,0:T(8,128)(2,1)S(1)}, bf16[32,2048]{1,0:T(8,128)(2,1)S(1)}, u32[]{:S(2)}, u32[]{:S(2)}) %collective-permute-start.13) | collective-permute-done | bytes 131104 | tf_op jit(solution)/shard_map/ppermute | solution.py:411
  96.9 2.0 %shard_map.98 = (f32[32,512]{1,0:T(8,128)S(1)}, f32[32,768]{1,0:T(8,128)S(1)}, f32[32,768]{1,0:T(8,128)S(1)}) custom-call(bf16[32,2048]{1,0:T(8,128)(2,1)S(1)} %shard_map.95.part0, bf16[32,2048]{1,0:T(8,128)(2,1)S(1)} %collective-permute-done.12.part1, bf16[32,2048]{1,0:T(8,128)(2,1)S(1)} %collective-permute-done.13.part2, ...), custom_call_target="tpu_custom_call" | custom-call | flops 134217728 | bytes 4194304 | tf_op jit(solution)/shard_map/pallas_call | solution.py:33
  98.9 1.3 collective-permute-start.18
  100.3 0.9 collective-permute-done.18.arrived
  101.6 3.0 %collective-permute-start.20 = (bf16[32,896]{1,0:T(8,128)(2,1)S(1)}, bf16[32,896]{1,0:T(8,128)(2,1)S(1)}, u32[]{:S(2)}, u32[]{:S(2)}) collective-permute-start(bf16[32,896]{1,0:T(8,128)(2,1)S(1)} %shard_map.99.wire0), channel_id=1, source_target_pairs={{0,128},{64,192},{128,0},{192,64},{1,129},{65,193},{129,1},{193,65... | collective-permute-start | bytes 172040 | tf_op jit(solution)/shard_map/ppermute | solution.py:411
  104.9 0.7 collective-permute-done.19.wire1
  105.5 1.6 %collective-permute-done.20.wire2 = bf16[32,896]{1,0:T(8,128)(2,1)S(1)} collective-permute-done((bf16[32,896]{1,0:T(8,128)(2,1)S(1)}, bf16[32,896]{1,0:T(8,128)(2,1)S(1)}, u32[]{:S(2)}, u32[]{:S(2)}) %collective-permute-start.20) | collective-permute-done | bytes 57376 | tf_op jit(solution)/shard_map/ppermute | solution.py:411
  107.2 1.0 collective-permute-done.21.wire3
  108.1 0.7 shard_map.100
  108.8 13.4 %all_to_all.22.arrived = bf16[8,32,640]{2,1,0:T(8,128)(2,1)S(1)} all-to-all(bf16[8,32,640]{2,1,0:T(8,128)(2,1)S(1)} %shard_map.100), channel_id=1, replica_groups=mesh['y'=4,'z'=8,'c'=2,'x'=4] {'z'}, dimensions={0} | all-to-all | bytes 655360 | tf_op jit(solution)/shard_map/all_to_all | solution.py:428
  122.2 0.7 shard_map.101
  122.9 12.1 %all_to_all.23.arrived = f32[8,32,128]{2,1,0:T(8,128)S(1)} all-to-all(f32[8,32,128]{2,1,0:T(8,128)S(1)} %shard_map.101), channel_id=1, replica_groups=mesh['y'=4,'z'=8,'c'=2,'x'=4] {'c','x'}, dimensions={0} | all-to-all | bytes 262144 | tf_op jit(solution)/shard_map/all_to_all | solution.py:596
  135.0 1.3 shard_map.102
  (30 shorter events, 4.2 us)
Async XLA Ops:
  0.6 29.8 %copy-start.2 = (s32[1024]{0:T(1024)S(1)}, s32[1024]{0:T(1024)}, u32[]{:S(2)}) copy-start(s32[1024]{0:T(1024)} %param.9) | copy-start | bytes 12292
  0.6 29.8 %copy-start.3 = (s32[1024]{0:T(1024)S(1)}, s32[1024]{0:T(1024)}, u32[]{:S(2)}) copy-start(s32[1024]{0:T(1024)} %param.10) | copy-start | bytes 12292
  0.7 29.8 %copy-start = (f32[32,1024]{1,0:T(8,128)S(1)}, f32[32,1024]{1,0:T(8,128)}, u32[]{:S(2)}) copy-start(f32[32,1024]{1,0:T(8,128)} %val_weight.1) | copy-start | bytes 393220
  7.9 4.2 %collective-permute-start = (f32[8,128]{1,0:T(8,128)S(1)}, f32[8,128]{1,0:T(8,128)S(1)}, u32[]{:S(2)}, u32[]{:S(2)}) collective-permute-start(f32[8,128]{1,0:T(8,128)S(1)} %get-tuple-element.37), channel_id=1, source_target_pairs={{0,4},{4,0},{1,5},{5,1},{2,6},{6,2},{3,7},{7,3},{8,12},{12,8},{9,1... | collective-permute-start | bytes 12296 | tf_op jit(solution)/shard_map/ppermute | solution.py:419
  30.5 10.7 %copy-start.1 = (s32[4096]{0:T(1024)S(1)}, s32[4096]{0:T(1024)}, u32[]{:S(2)}) copy-start(s32[4096]{0:T(1024)} %param.13) | copy-start | bytes 49156
  30.5 10.7 %copy-start.4 = (f32[256]{0:T(256)S(1)}, f32[256]{0:T(256)}, u32[]{:S(2)}) copy-start(f32[256]{0:T(256)} %param.12) | copy-start | bytes 3076
  32.0 7.6 %collective-permute-start.4 = (bf16[32,2560]{1,0:T(8,128)(2,1)S(1)}, bf16[32,2560]{1,0:T(8,128)(2,1)S(1)}, u32[]{:S(2)}, u32[]{:S(2)}) collective-permute-start(bf16[32,2560]{1,0:T(8,128)(2,1)S(1)} %get-tuple-element.48), channel_id=1, source_target_pairs={{0,1},{1,2},{2,3},{3,0},{4,5},{5,6},{6,7},{7,4},{8,9},{9,10},{10,1... | collective-permute-start | bytes 491528 | tf_op jit(solution)/shard_map/ppermute | solution.py:411
  33.2 9.1 %collective-permute-start.5 = (bf16[32,2560]{1,0:T(8,128)(2,1)S(1)}, bf16[32,2560]{1,0:T(8,128)(2,1)S(1)}, u32[]{:S(2)}, u32[]{:S(2)}) collective-permute-start(bf16[32,2560]{1,0:T(8,128)(2,1)S(1)} %get-tuple-element.49), channel_id=1, source_target_pairs={{0,2},{1,3},{2,0},{3,1},{4,6},{5,7},{6,4},{7,5},{8,10},{9,11},{10,... | collective-permute-start | bytes 491528 | tf_op jit(solution)/shard_map/ppermute | solution.py:411
  35.7 6.7 %collective-permute-start.6 = (bf16[32,2560]{1,0:T(8,128)(2,1)S(1)}, bf16[32,2560]{1,0:T(8,128)(2,1)S(1)}, u32[]{:S(2)}, u32[]{:S(2)}) collective-permute-start(bf16[32,2560]{1,0:T(8,128)(2,1)S(1)} %get-tuple-element.50), channel_id=1, source_target_pairs={{0,3},{1,0},{2,1},{3,2},{4,7},{5,4},{6,5},{7,6},{8,11},{9,8},{10,9... | collective-permute-start | bytes 491528 | tf_op jit(solution)/shard_map/ppermute | solution.py:411
  38.2 6.6 %collective-permute-start.1 = (bf16[32,2560]{1,0:T(8,128)(2,1)S(1)}, bf16[32,2560]{1,0:T(8,128)(2,1)S(1)}, u32[]{:S(2)}, u32[]{:S(2)}) collective-permute-start(bf16[32,2560]{1,0:T(8,128)(2,1)S(1)} %get-tuple-element.41), channel_id=1, source_target_pairs={{0,1},{1,2},{2,3},{3,0},{4,5},{5,6},{6,7},{7,4},{8,9},{9,10},{10,1... | collective-permute-start | bytes 491528 | tf_op jit(solution)/shard_map/ppermute | solution.py:411
  38.6 9.4 %collective-permute-start.2 = (bf16[32,2560]{1,0:T(8,128)(2,1)S(1)}, bf16[32,2560]{1,0:T(8,128)(2,1)S(1)}, u32[]{:S(2)}, u32[]{:S(2)}) collective-permute-start(bf16[32,2560]{1,0:T(8,128)(2,1)S(1)} %get-tuple-element.42), channel_id=1, source_target_pairs={{0,2},{1,3},{2,0},{3,1},{4,6},{5,7},{6,4},{7,5},{8,10},{9,11},{10,... | collective-permute-start | bytes 491528 | tf_op jit(solution)/shard_map/ppermute | solution.py:411
  39.5 9.0 %collective-permute-start.3 = (bf16[32,2560]{1,0:T(8,128)(2,1)S(1)}, bf16[32,2560]{1,0:T(8,128)(2,1)S(1)}, u32[]{:S(2)}, u32[]{:S(2)}) collective-permute-start(bf16[32,2560]{1,0:T(8,128)(2,1)S(1)} %get-tuple-element.43), channel_id=1, source_target_pairs={{0,3},{1,0},{2,1},{3,2},{4,7},{5,4},{6,5},{7,6},{8,11},{9,8},{10,9... | collective-permute-start | bytes 491528 | tf_op jit(solution)/shard_map/ppermute | solution.py:411
  50.5 3.9 %collective-permute-start.7 = (f32[32,768]{1,0:T(8,128)S(1)}, f32[32,768]{1,0:T(8,128)S(1)}, u32[]{:S(2)}, u32[]{:S(2)}) collective-permute-start(f32[32,768]{1,0:T(8,128)S(1)} %get-tuple-element.54), channel_id=1, source_target_pairs={{0,4},{4,0},{1,5},{5,1},{2,6},{6,2},{3,7},{7,3},{8,12},{12,8},{9,1... | collective-permute-start | bytes 294920 | tf_op jit(solution)/shard_map/ppermute | solution.py:419
  54.5 3.0 %collective-permute-start.10 = (bf16[32,896]{1,0:T(8,128)(2,1)S(1)}, bf16[32,896]{1,0:T(8,128)(2,1)S(1)}, u32[]{:S(2)}, u32[]{:S(2)}) collective-permute-start(bf16[32,896]{1,0:T(8,128)(2,1)S(1)} %shard_map.92.wire0), channel_id=1, source_target_pairs={{0,192},{64,0},{128,64},{192,128},{1,193},{65,1},{129,65},{193,129... | collective-permute-start | bytes 172040 | tf_op jit(solution)/shard_map/ppermute | solution.py:411
  55.4 4.2 %collective-permute-start.8 = (bf16[32,896]{1,0:T(8,128)(2,1)S(1)}, bf16[32,896]{1,0:T(8,128)(2,1)S(1)}, u32[]{:S(2)}, u32[]{:S(2)}) collective-permute-start(bf16[32,896]{1,0:T(8,128)(2,1)S(1)} %shard_map.92.wire0), channel_id=1, source_target_pairs={{0,64},{64,128},{128,192},{192,0},{1,65},{65,129},{129,193},{193,1... | collective-permute-start | bytes 172040 | tf_op jit(solution)/shard_map/ppermute | solution.py:411
  56.0 4.6 %collective-permute-start.9 = (bf16[32,896]{1,0:T(8,128)(2,1)S(1)}, bf16[32,896]{1,0:T(8,128)(2,1)S(1)}, u32[]{:S(2)}, u32[]{:S(2)}) collective-permute-start(bf16[32,896]{1,0:T(8,128)(2,1)S(1)} %shard_map.92.wire0), channel_id=1, source_target_pairs={{0,128},{64,192},{128,0},{192,64},{1,129},{65,193},{129,1},{193,65... | collective-permute-start | bytes 172040 | tf_op jit(solution)/shard_map/ppermute | solution.py:411
  74.9 5.3 %collective-permute-start.11 = (bf16[32,640]{1,0:T(8,128)(2,1)S(1)}, bf16[32,640]{1,0:T(8,128)(2,1)S(1)}, u32[]{:S(2)}, u32[]{:S(2)}) collective-permute-start(bf16[32,640]{1,0:T(8,128)(2,1)S(1)} %get-tuple-element.56.weighted), channel_id=1, source_target_pairs={{0,4},{4,0},{1,5},{5,1},{2,6},{6,2},{3,7},{7,3},{8,12},{12,8},{9,1... | collective-permute-start | bytes 122888 | tf_op jit(solution)/shard_map/ppermute | solution.py:419
  81.6 7.0 %collective-permute-start.15 = (bf16[32,2176]{1,0:T(8,128)(2,1)S(1)}, bf16[32,2176]{1,0:T(8,128)(2,1)S(1)}, u32[]{:S(2)}, u32[]{:S(2)}) collective-permute-start(bf16[32,2176]{1,0:T(8,128)(2,1)S(1)} %shard_map.96.part0), channel_id=1, source_target_pairs={{0,1},{1,2},{2,3},{3,0},{4,5},{5,6},{6,7},{7,4},{8,9},{9,10},{10,1... | collective-permute-start | bytes 417800 | tf_op jit(solution)/shard_map/ppermute | solution.py:411
  82.7 8.6 %collective-permute-start.16 = (bf16[32,2176]{1,0:T(8,128)(2,1)S(1)}, bf16[32,2176]{1,0:T(8,128)(2,1)S(1)}, u32[]{:S(2)}, u32[]{:S(2)}) collective-permute-start(bf16[32,2176]{1,0:T(8,128)(2,1)S(1)} %shard_map.96.part0), channel_id=1, source_target_pairs={{0,2},{1,3},{2,0},{3,1},{4,6},{5,7},{6,4},{7,5},{8,10},{9,11},{10,... | collective-permute-start | bytes 417800 | tf_op jit(solution)/shard_map/ppermute | solution.py:411
  84.9 6.4 %collective-permute-start.17 = (bf16[32,2176]{1,0:T(8,128)(2,1)S(1)}, bf16[32,2176]{1,0:T(8,128)(2,1)S(1)}, u32[]{:S(2)}, u32[]{:S(2)}) collective-permute-start(bf16[32,2176]{1,0:T(8,128)(2,1)S(1)} %shard_map.96.part0), channel_id=1, source_target_pairs={{0,3},{1,0},{2,1},{3,2},{4,7},{5,4},{6,5},{7,6},{8,11},{9,8},{10,9... | collective-permute-start | bytes 417800 | tf_op jit(solution)/shard_map/ppermute | solution.py:411
  87.4 6.5 %collective-permute-start.12 = (bf16[32,2048]{1,0:T(8,128)(2,1)S(1)}, bf16[32,2048]{1,0:T(8,128)(2,1)S(1)}, u32[]{:S(2)}, u32[]{:S(2)}) collective-permute-start(bf16[32,2048]{1,0:T(8,128)(2,1)S(1)} %shard_map.95.part0), channel_id=1, source_target_pairs={{0,1},{1,2},{2,3},{3,0},{4,5},{5,6},{6,7},{7,4},{8,9},{9,10},{10,1... | collective-permute-start | bytes 393224 | tf_op jit(solution)/shard_map/ppermute | solution.py:411
  87.7 9.2 %collective-permute-start.13 = (bf16[32,2048]{1,0:T(8,128)(2,1)S(1)}, bf16[32,2048]{1,0:T(8,128)(2,1)S(1)}, u32[]{:S(2)}, u32[]{:S(2)}) collective-permute-start(bf16[32,2048]{1,0:T(8,128)(2,1)S(1)} %shard_map.95.part0), channel_id=1, source_target_pairs={{0,2},{1,3},{2,0},{3,1},{4,6},{5,7},{6,4},{7,5},{8,10},{9,11},{10,... | collective-permute-start | bytes 393224 | tf_op jit(solution)/shard_map/ppermute | solution.py:411
  88.6 8.3 %collective-permute-start.14 = (bf16[32,2048]{1,0:T(8,128)(2,1)S(1)}, bf16[32,2048]{1,0:T(8,128)(2,1)S(1)}, u32[]{:S(2)}, u32[]{:S(2)}) collective-permute-start(bf16[32,2048]{1,0:T(8,128)(2,1)S(1)} %shard_map.95.part0), channel_id=1, source_target_pairs={{0,3},{1,0},{2,1},{3,2},{4,7},{5,4},{6,5},{7,6},{8,11},{9,8},{10,9... | collective-permute-start | bytes 393224 | tf_op jit(solution)/shard_map/ppermute | solution.py:411
  98.9 2.3 %collective-permute-start.18 = (f32[32,768]{1,0:T(8,128)S(1)}, f32[32,768]{1,0:T(8,128)S(1)}, u32[]{:S(2)}, u32[]{:S(2)}) collective-permute-start(f32[32,768]{1,0:T(8,128)S(1)} %get-tuple-element.66), channel_id=1, source_target_pairs={{0,4},{4,0},{1,5},{5,1},{2,6},{6,2},{3,7},{7,3},{8,12},{12,8},{9,1... | collective-permute-start | bytes 294920 | tf_op jit(solution)/shard_map/ppermute | solution.py:419
  101.3 4.3 %collective-permute-start.19 = (bf16[32,896]{1,0:T(8,128)(2,1)S(1)}, bf16[32,896]{1,0:T(8,128)(2,1)S(1)}, u32[]{:S(2)}, u32[]{:S(2)}) collective-permute-start(bf16[32,896]{1,0:T(8,128)(2,1)S(1)} %shard_map.99.wire0), channel_id=1, source_target_pairs={{0,64},{64,128},{128,192},{192,0},{1,65},{65,129},{129,193},{193,1... | collective-permute-start | bytes 172040 | tf_op jit(solution)/shard_map/ppermute | solution.py:411
  101.6 5.6 %collective-permute-start.20 = (bf16[32,896]{1,0:T(8,128)(2,1)S(1)}, bf16[32,896]{1,0:T(8,128)(2,1)S(1)}, u32[]{:S(2)}, u32[]{:S(2)}) collective-permute-start(bf16[32,896]{1,0:T(8,128)(2,1)S(1)} %shard_map.99.wire0), channel_id=1, source_target_pairs={{0,128},{64,192},{128,0},{192,64},{1,129},{65,193},{129,1},{193,65... | collective-permute-start | bytes 172040 | tf_op jit(solution)/shard_map/ppermute | solution.py:411
  104.5 3.6 %collective-permute-start.21 = (bf16[32,896]{1,0:T(8,128)(2,1)S(1)}, bf16[32,896]{1,0:T(8,128)(2,1)S(1)}, u32[]{:S(2)}, u32[]{:S(2)}) collective-permute-start(bf16[32,896]{1,0:T(8,128)(2,1)S(1)} %shard_map.99.wire0), channel_id=1, source_target_pairs={{0,192},{64,0},{128,64},{192,128},{1,193},{65,1},{129,65},{193,129... | collective-permute-start | bytes 172040 | tf_op jit(solution)/shard_map/ppermute | solution.py:411

commit v4 on v3

v4 whole, which is shorter than its diff:
```python
import functools

import jax
import jax.numpy as jnp
from jax import lax
from jax.experimental import pallas as pl
from jax.experimental.pallas import tpu as pltpu
from jax.sharding import Mesh
from jax.sharding import PartitionSpec as P

F32 = jnp.float32
BF16 = jnp.bfloat16
NT = (((1,), (1,)), ((), ()))
NY, NZ, NC, NX = 4, 8, 2, 4
R = 32
N = 1024
HALF = N // NC
W = 4096
OWN = W // NX
NB = 256
TOTAL = float(N * NX)
LANES = 128
PART = OWN // 2
VMEM = pl.BlockSpec(memory_space=pltpu.VMEM)
HBM = pl.BlockSpec(memory_space=pltpu.HBM)


def call(body, outs, *arrays, scratch=(), limit=16, hbm=(), flops=0):
    specs = [HBM if i in hbm else VMEM for i in range(len(arrays))]
    arrays = [
        pltpu.with_memory_space_constraint(a, pltpu.HBM) if i in hbm else a
        for i, a in enumerate(arrays)
    ]
    return pl.pallas_call(
        body,
        out_shape=outs,
        in_specs=specs,
        out_specs=jax.tree.map(lambda _: VMEM, outs),
        scratch_shapes=scratch,
        compiler_params=pltpu.CompilerParams(vmem_limit_bytes=limit << 20),
        cost_estimate=pl.CostEstimate(flops=flops, bytes_accessed=4 << 20, transcendentals=0),
    )(*arrays)


def shape(*dims, dtype=F32):
    return jax.ShapeDtypeStruct(dims, dtype)


def lane_ids(lanes=LANES):
    return lax.broadcasted_iota(jnp.int32, (R, lanes), 1)


def column(tile, lane):
    return jnp.sum(jnp.where(lane_ids(tile.shape[1]) == lane, tile, 0.0), axis=1, keepdims=True)


def columns(values, first=0):
    lanes = lane_ids()
    tile = jnp.zeros((R, LANES), F32)
    for i, value in enumerate(values):
        tile = jnp.where(lanes == first + i, value, tile)
    return tile


def terms(value, count):
    found = []
    for _ in range(count):
        term = value.astype(BF16).astype(F32)
        found.append(term)
        value = value - term
    return found


def to_terms(tile):
    first, second, third = terms(tile, 3)
    return first + pltpu.roll(second, 8, 1) + pltpu.roll(third, 16, 1)


def from_terms(tile):
    total = tile + pltpu.roll(tile, LANES - 8, 1) + pltpu.roll(tile, LANES - 16, 1)
    return jnp.where(lane_ids() < 8, total, 0.0)


def chunk(index, size):
    return pl.ds(pl.multiple_of(index * size, size), size)


def block_sums(vec, weight, onehot):
    parts = jnp.concatenate(terms(vec * weight, 3), axis=0).astype(BF16)
    sums = lax.dot_general(parts, onehot, NT, preferred_element_type=F32)
    return sums[:R] + sums[R : 2 * R] + sums[2 * R :]


def prepare(ids, strengths, place, gradw, lamf, onehot):
    kinds = lax.broadcasted_iota(jnp.int32, (NB, OWN), 0)
    rows = lax.broadcasted_iota(jnp.int32, (16, NB), 0)
    split3 = jnp.zeros((16, NB), F32)
    for i, term in enumerate(terms(strengths[...], 3)):
        split3 = jnp.where(rows == i, term, split3)
    split3 = split3.astype(BF16)
    for j in range(NX):
        hot = (kinds == ids[:, j * OWN : (j + 1) * OWN]).astype(F32).astype(BF16)
        found = jnp.dot(split3, hot, preferred_element_type=F32)
        lamf[:, j * OWN : (j + 1) * OWN] = found[0:1] + found[1:2] + found[2:3]
    own = ids[:, chunk(place[0, 3], OWN)]
    core = lax.shift_right_logical(own, 2) & 1
    moved = core * 128 + lax.shift_right_logical(own, 3) * 4 + (own & 3)
    onehot[...] = (kinds == moved).astype(F32).astype(BF16)


def margins(source, given, place, margin, examples, wfloat, weights, arrival):
    width = W // 8

    def fetch(i):
        at = (slice(None), pl.ds(i * width, width))
        return pltpu.make_async_copy(source.at[at], examples.at[at], arrival.at[i])

    small = pltpu.make_async_copy(given, weights, arrival.at[8])
    small.start()
    for i in range(8):
        fetch(i).start()
    small.wait()
    lines = weights[...].astype(F32)
    line = jnp.concatenate([lines[i : i + 1] for i in range(W // LANES)], axis=1)
    wfloat[...] = line
    rhs = jnp.broadcast_to(line, (16, W)).astype(BF16)
    total = None
    for i in range(8):
        fetch(i).wait()
        cols = slice(i * width, (i + 1) * width)
        term = lax.dot_general(
            rhs[:, cols], examples[:, cols], NT, preferred_element_type=F32
        )
        total = term if total is None else total + term
    for i in range(8):
        margin[i : i + 1, :] = total[0:1, i * LANES : (i + 1) * LANES]


def partner(x, which, stage):
    return x ^ (1 if which == stage else 3)


def part_of(owner, which):
    return pl.ds(pl.multiple_of(owner * OWN + which * PART, PART), PART)


def rhs_parts(which, gradw, examples, place, part, wire):
    x = place[0, 3]
    for k in range(NX):
        found = jnp.dot(
            gradw, examples[:, part_of(k, which)], preferred_element_type=F32
        )
        cols = slice(k * PART, (k + 1) * PART)
        part[:, cols] = found
        wire[:, cols] = found.astype(BF16)
    for i, owner in enumerate((partner(x, which, 0), x ^ 2)):
        found = part[:, chunk(owner, PART)]
        rest = found - found.astype(BF16).astype(F32)
        wire[:, (NX + i) * PART : (NX + i + 1) * PART] = rest.astype(BF16)


def gradients(
    margin_parts, labels, split, val_weight, examples, place, part, wire, curvew, gradw
):
    whole = jnp.sum(margin_parts[...], axis=0)
    margin = jnp.concatenate([whole[i : i + 1] for i in range(8)], axis=1)
    prob = 1.0 / (1.0 + jnp.exp(-margin))
    train = split[...].astype(F32)
    curvew[...] = train * prob * (1.0 - prob)
    err = (1.0 - train) * (prob - labels[...].astype(F32))
    found = (val_weight[...] * err / jnp.sqrt(F32(TOTAL))).astype(BF16)
    gradw[...] = found
    rhs_parts(0, found, examples, place, part, wire)


def gradients_rest(gradw, examples, place, part, wire):
    rhs_parts(1, gradw[...], examples, place, part, wire)


def rhs_pairs(which, part, arrived, place, both, wire):
    x = place[0, 3]
    other = partner(x, which, 1)
    both[...] = part[...] + arrived[:, : NX * PART].astype(F32)
    for i, owner in enumerate((x, other)):
        rest = arrived[:, (NX + i) * PART : (NX + i + 1) * PART].astype(F32)
        both[:, chunk(owner, PART)] += rest
    wire[:, : NX * PART] = both[...].astype(BF16)
    found = both[:, chunk(other, PART)]
    wire[:, NX * PART :] = (found - found.astype(BF16).astype(F32)).astype(BF16)


def tangents(pieces, which, examples, before, tang):
    for i in range(N // 256):
        rows = slice(i * 256, (i + 1) * 256)
        total = None if before is None else before[:, rows]
        for k in range(NX):
            term = lax.dot_general(
                pieces[:, k * PART : (k + 1) * PART],
                examples[rows, part_of(k, which)],
                NT,
                preferred_element_type=F32,
            )
            total = term if total is None else total + term
        tang[:, rows] = total


def halves(tang, scalars, blocks, core, keep, send):
    for out, which in ((keep, core), (send, 1 - core)):
        out[:, :HALF] = tang[:, chunk(which, HALF)]
        out[:, HALF : HALF + LANES] = scalars
        out[:, HALF + LANES :] = blocks[:, chunk(which, LANES)]


def first_part(
    which, part, wire, examples, lamf, wfloat, onehot, place, rhs, lows, before, tang
):
    x = place[0, 3]
    lows[...] = (part[...] + wire[:, : NX * PART].astype(F32)).astype(BF16)
    cols = chunk(x, PART)
    vec = part[:, cols] + wire[:, cols].astype(F32) + wire[:, NX * PART :].astype(F32)
    rhs[...] = vec
    lows[:, cols] = vec.astype(BF16)
    own = part_of(x, which)
    square = vec * vec
    norm = jnp.sum(square, axis=1, keepdims=True)
    scaled = jnp.sum(lamf[:, own] * square, axis=1, keepdims=True)
    hot = onehot[:, which * PART : (which + 1) * PART]
    blocks = block_sums(vec, wfloat[:, own], hot)
    tangents(lows, which, examples, before, tang)
    return columns([norm, scaled]), blocks


def first_tangents(
    part, wire, examples, lamf, wfloat, onehot, place, rhs, lows, tang, sums
):
    scalars, blocks = first_part(
        0, part, wire, examples, lamf, wfloat, onehot, place, rhs, lows, None, tang
    )
    sums[:, :LANES] = scalars
    sums[:, LANES:] = blocks


def first_tangents_rest(
    part, wire, examples, lamf, wfloat, onehot, before, sums, place,
    rhs, lows, keep, send, tang, total,
):
    scalars, blocks = first_part(
        1, part, wire, examples, lamf, wfloat, onehot, place, rhs, lows, before, tang
    )
    total[...] = sums[:, LANES:] + blocks
    halves(tang, sums[:, :LANES] + scalars, total, place[0, 2], keep, send)


def to_wire(keep, arrived, wire):
    total = keep[...] + arrived[...]
    wire[:, :HALF] = total[:, :HALF].astype(BF16)
    wire[:, HALF : HALF + LANES] = to_terms(total[:, HALF : HALF + LANES]).astype(BF16)
    high, rest = terms(total[:, HALF + LANES :], 2)
    wire[:, HALF + LANES : HALF + 2 * LANES] = high.astype(BF16)
    wire[:, HALF + 2 * LANES :] = rest.astype(BF16)


def along_y(wire0, wire1, wire2, wire3, place, out):
    total = wire0[...].astype(F32)
    for wire in (wire1, wire2, wire3):
        total = total + wire[...].astype(F32)
    tang = total[:, :HALF].astype(BF16)
    tile = to_terms(from_terms(total[:, HALF : HALF + LANES]))
    blocks = total[:, HALF + LANES : HALF + 2 * LANES] + total[:, HALF + 2 * LANES :]
    high, rest = terms(blocks, 2)
    lanes = lane_ids()
    at64 = pltpu.roll(high, (64 - 32 * place[0, 0] + LANES) % LANES, 1)
    at96 = pltpu.roll(rest, (96 - 32 * place[0, 0] + LANES) % LANES, 1)
    tile = jnp.where(lanes >= 96, at96, jnp.where(lanes >= 64, at64, tile)).astype(BF16)
    for i in range(NZ):
        out[i, :, :HALF] = tang
        out[i, :, HALF:] = tile


def along_z(arrived):
    tang = arrived[0, :, :HALF].astype(F32)
    tile = arrived[0, :, HALF:].astype(F32)
    for i in range(1, NZ):
        tang = tang + arrived[i, :, :HALF].astype(F32)
        tile = tile + arrived[i, :, HALF:].astype(F32)
    blocks = pltpu.roll(tile, 64, 1) + pltpu.roll(tile, 32, 1)
    return tang, from_terms(tile), jnp.where(lane_ids() < 32, blocks, 0.0)


def weigh(arrived, curvew, place, tang_out, weighted, kept):
    tang, scalars, blocks = along_z(arrived)
    tang_out[...] = tang
    half = curvew[:, chunk(place[0, 2], HALF)]
    product = half * tang
    weighted[:, :HALF] = product.astype(BF16)
    curv = columns([jnp.sum(product * tang, axis=1, keepdims=True)], 2)
    weighted[:, HALF:] = to_terms(curv).astype(BF16)
    kept[:, :LANES] = scalars + curv
    kept[:, LANES:] = blocks


def product_parts(which, weighted, other, examples, place, part):
    core = place[0, 2]
    for k in range(NX):
        cols = part_of(k, which)
        mine = jnp.dot(
            weighted[:, :HALF], examples[chunk(core, HALF), cols], preferred_element_type=F32
        )
        rest = jnp.dot(
            other[:, :HALF], examples[chunk(1 - core, HALF), cols], preferred_element_type=F32
        )
        part[:, k * PART : (k + 1) * PART] = (mine + rest).astype(BF16)


def products(weighted, other, kept, examples, place, part):
    scalars = kept[:, :LANES] + from_terms(other[:, HALF:].astype(F32))
    part[:, NX * PART :] = to_terms(scalars).astype(BF16)
    product_parts(0, weighted, other, examples, place, part)


def products_rest(weighted, other, examples, place, part):
    product_parts(1, weighted, other, examples, place, part)


def product_pairs(mine, other, wire):
    both = mine[...].astype(F32) + other[...].astype(F32)
    wire[:, : NX * PART] = both[:, : NX * PART].astype(BF16)
    if mine.shape[1] > NX * PART:
        wire[:, NX * PART :] = to_terms(from_terms(both[:, NX * PART :])).astype(BF16)


def second_part(
    which, alpha, mine, other, rhs, lows, examples, lamf, wfloat, onehot, place,
    resid, pieces, before, tang,
):
    def step(cols, lam, direc):
        total = mine[:, cols].astype(F32) + other[:, cols].astype(F32)
        return direc - alpha * (total / F32(TOTAL) + lam * direc)

    for k in range(NX):
        cols = slice(k * PART, (k + 1) * PART)
        left = step(cols, lamf[:, part_of(k, which)], lows[:, cols].astype(F32))
        pieces[:, cols] = left.astype(BF16)
    x = place[0, 3]
    own = part_of(x, which)
    cols = chunk(x, PART)
    lam = lamf[:, own]
    direc = rhs[...]
    left = step(cols, lam, direc)
    resid[...] = left
    pieces[:, cols] = left.astype(BF16)
    scalars = columns(
        [
            jnp.sum(left * left, axis=1, keepdims=True),
            jnp.sum(lam * left * left, axis=1, keepdims=True),
            jnp.sum(lam * left * direc, axis=1, keepdims=True),
        ]
    )
    hot = onehot[:, which * PART : (which + 1) * PART]
    blocks = block_sums(left, wfloat[:, own], hot)
    tangents(pieces, which, examples, before, tang)
    return scalars, blocks


def second_tangents(
    mine, other, rhs, lows, examples, lamf, wfloat, onehot, place,
    resid, tang, sums, kept, pieces,
):
    tile = mine[:, NX * PART :].astype(F32) + other[:, NX * PART :].astype(F32)
    tile = from_terms(tile)
    norm, scaled, curv = (column(tile, i) for i in range(3))
    alpha = norm / (curv / F32(TOTAL) + scaled)
    kept[...] = jnp.where(lane_ids() == 3, alpha, tile)
    scalars, blocks = second_part(
        0, alpha, mine, other, rhs, lows, examples, lamf, wfloat, onehot, place,
        resid, pieces, None, tang,
    )
    sums[:, :LANES] = scalars
    sums[:, LANES:] = blocks


def second_tangents_rest(
    mine, other, rhs, lows, examples, lamf, wfloat, onehot, before, sums, kept,
    place, resid, keep, send, tang, total, pieces,
):
    scalars, blocks = second_part(
        1, column(kept[...], 3), mine, other, rhs, lows, examples, lamf,
        wfloat, onehot, place, resid, pieces, before, tang,
    )
    total[...] = sums[:, LANES:] + blocks
    halves(tang, sums[:, :LANES] + scalars, total, place[0, 2], keep, send)


def curvature(arrived, curvew, tang_first, kept, place, out):
    tang, scalars, blocks = along_z(arrived)
    half = curvew[:, chunk(place[0, 2], HALF)]
    product = half * tang
    both = jnp.sum(product * tang, axis=1, keepdims=True)
    cross = jnp.sum(product * tang_first[...], axis=1, keepdims=True)
    tile = jnp.where(lane_ids() < 3, scalars, columns([both, cross], 3))
    lanes = lane_ids()
    shift = 4 * place[0, 1]
    now = pltpu.roll(blocks, (32 - shift + LANES) % LANES, 1)
    before = pltpu.roll(kept[:, LANES:], (36 - shift + LANES) % LANES, 1)
    tile = jnp.where((lanes >= 32) & (lanes < 36), now, tile)
    tile = jnp.where((lanes >= 36) & (lanes < 40), before, tile)
    for i in range(NC * NX):
        out[i] = tile


def finish(
    arrived, kept, rhs_a, rhs_b, resid_a, resid_b, strengths, place, solve, hyper
):
    core, x = place[0, 2], place[0, 3]
    mine = sum(arrived[core * NX + i] for i in range(NX))
    rest = sum(arrived[(1 - core) * NX + i] for i in range(NX))
    every = mine + rest
    tile = kept[...]
    norm, scaled_first, curv_first, alpha = (column(tile, i) for i in range(4))
    norm_next, scaled, mixed = (column(mine, i) for i in range(3))
    both, cross = column(every, 3), column(every, 4)
    beta = norm_next / norm
    curv = (both + 2.0 * beta * cross + beta * beta * curv_first) / F32(TOTAL)
    curv = curv + (scaled + 2.0 * beta * mixed + beta * beta * scaled_first)
    alpha_next = norm_next / curv
    for i, (rhs, resid) in enumerate(((rhs_a, resid_a), (rhs_b, resid_b))):
        first = rhs[...]
        solve[:, i * PART : (i + 1) * PART] = alpha * first + alpha_next * (
            resid[...] + beta * first
        )
    now, before = column(mine, 32 + x), column(mine, 36 + x)
    block = ((place[0, 0] * NZ + place[0, 1]) * NC + core) * NX + x
    kinds = lax.broadcasted_iota(jnp.int32, (1, NB), 1)
    strength = jnp.sum(jnp.where(kinds == block, strengths[...], 0.0), axis=1, keepdims=True)
    found = -strength * (alpha * before + alpha_next * (now + beta * before))
    hyper[...] = jnp.transpose(jnp.broadcast_to(found, (R, LANES)))[0:1]


def shift(array, axis, length, by):
    return lax.ppermute(array, axis, [(i, (i + by) % length) for i in range(length)])


def shifted(array, axis, length):
    return [shift(array, axis, length, s) for s in range(1, length)]


def traded(array, which, stage):
    return lax.ppermute(array, "x", [(i, partner(i, which, stage)) for i in range(NX)])


def swapped(array):
    return lax.ppermute(array, "c", [(0, 1), (1, 0)])


def summed(keep, send, place):
    wire = call(to_wire, shape(R, HALF + 3 * LANES, dtype=BF16), keep, swapped(send))
    arrived = shifted(wire, "y", NY)
    out = call(
        along_y, shape(NZ, R, HALF + LANES, dtype=BF16), wire, *arrived, place
    )
    return lax.all_to_all(out, "z", 0, 0, tiled=True)


def shards(examples, weights, labels, split, val_weight, strengths, block_ids):
    place = jnp.stack([lax.axis_index(axis) for axis in ("y", "z", "c", "x")])
    place = place.astype(jnp.int32).reshape(1, 4)
    strengths = strengths.reshape(1, NB)
    margin, examples, wfloat = call(
        margins,
        [shape(8, 128), pltpu.VMEM((N, W), BF16), shape(1, W)],
        examples,
        weights.reshape(W // LANES, LANES),
        place,
        scratch=[pltpu.VMEM((W // LANES, LANES), BF16), pltpu.SemaphoreType.DMA((9,))],
        hbm=(0, 1),
    )
    margin = margin + swapped(margin)
    margin_parts = lax.all_to_all(
        jnp.broadcast_to(margin[None], (NY * NZ, 8, 128)), ("y", "z"), 0, 0, tiled=True
    )
    work = 2 * R * N * W // 2
    whole = shape(R, NX * PART)
    part_a, wire_a, curvew, gradw = call(
        gradients,
        [
            whole,
            shape(R, (NX + 2) * PART, dtype=BF16),
            shape(1, N),
            shape(R, N, dtype=BF16),
        ],
        margin_parts,
        labels.reshape(1, N),
        split.reshape(1, N),
        val_weight,
        examples,
        place,
        flops=work,
    )
    arrived_a = traded(wire_a, 0, 0)
    part_b, wire_b = call(
        gradients_rest,
        [whole, shape(R, (NX + 2) * PART, dtype=BF16)],
        gradw,
        examples,
        place,
        flops=work,
    )
    arrived_b = traded(wire_b, 1, 0)
    lamf, onehot = call(
        prepare,
        [shape(1, W), shape(NB, OWN, dtype=BF16)],
        block_ids.reshape(1, W),
        strengths,
        place,
        gradw,
    )
    part_a, wire_a = call(
        functools.partial(rhs_pairs, 0),
        [whole, shape(R, (NX + 1) * PART, dtype=BF16)],
        part_a,
        arrived_a,
        place,
    )
    wire_a = traded(wire_a, 0, 1)
    part_b, wire_b = call(
        functools.partial(rhs_pairs, 1),
        [whole, shape(R, (NX + 1) * PART, dtype=BF16)],
        part_b,
        arrived_b,
        place,
    )
    wire_b = traded(wire_b, 1, 1)
    pair = [shape(R, HALF + 2 * LANES)] * 2
    low = shape(R, NX * PART, dtype=BF16)
    rhs_a, lows_a, tang, sums = call(
        first_tangents,
        [shape(R, PART), low, shape(R, N), shape(R, LANES + NB)],
        part_a,
        wire_a,
        examples,
        lamf,
        wfloat,
        onehot,
        place,
        flops=work,
    )
    rhs_b, lows_b, keep, send = call(
        first_tangents_rest,
        [shape(R, PART), low, *pair],
        part_b,
        wire_b,
        examples,
        lamf,
        wfloat,
        onehot,
        tang,
        sums,
        place,
        scratch=[pltpu.VMEM((R, N), F32), pltpu.VMEM((R, NB), F32)],
        flops=work,
    )
    arrived = summed(keep, send, place)
    tang_first, weighted, kept_first = call(
        weigh,
        [shape(R, HALF), shape(R, HALF + LANES, dtype=BF16), shape(R, 2 * LANES)],
        arrived,
        curvew,
        place,
    )
    other = swapped(weighted)
    part_a = call(
        products,
        shape(R, NX * PART + LANES, dtype=BF16),
        weighted,
        other,
        kept_first,
        examples,
        place,
        flops=work,
    )
    arrived_a = traded(part_a, 0, 0)
    part_b = call(
        products_rest,
        shape(R, NX * PART, dtype=BF16),
        weighted,
        other,
        examples,
        place,
        flops=work,
    )
    arrived_b = traded(part_b, 1, 0)
    mine_a = call(
        product_pairs, shape(R, NX * PART + LANES, dtype=BF16), part_a, arrived_a
    )
    other_a = traded(mine_a, 0, 1)
    mine_b = call(product_pairs, shape(R, NX * PART, dtype=BF16), part_b, arrived_b)
    other_b = traded(mine_b, 1, 1)
    resid_a, tang, sums, kept = call(
        second_tangents,
        [shape(R, PART), shape(R, N), shape(R, LANES + NB), shape(R, LANES)],
        mine_a,
        other_a,
        rhs_a,
        lows_a,
        examples,
        lamf,
        wfloat,
        onehot,
        place,
        scratch=[pltpu.VMEM((R, NX * PART), BF16)],
        flops=work,
    )
    resid_b, keep, send = call(
        second_tangents_rest,
        [shape(R, PART), *pair],
        mine_b,
        other_b,
        rhs_b,
        lows_b,
        examples,
        lamf,
        wfloat,
        onehot,
        tang,
        sums,
        kept,
        place,
        scratch=[
            pltpu.VMEM((R, N), F32),
            pltpu.VMEM((R, NB), F32),
            pltpu.VMEM((R, NX * PART), BF16),
        ],
        flops=work,
    )
    arrived = summed(keep, send, place)
    out = call(
        curvature,
        shape(NC * NX, R, LANES),
        arrived,
        curvew,
        tang_first,
        kept_first,
        place,
    )
    arrived = lax.all_to_all(out, ("c", "x"), 0, 0, tiled=True)
    solve, hyper = call(
        finish,
        [shape(R, OWN), shape(1, R)],
        arrived,
        kept,
        rhs_a,
        rhs_b,
        resid_a,
        resid_b,
        strengths,
        place,
    )
    return solve, hyper.reshape(R, 1)


def solution(mesh):
    fine = Mesh(mesh.devices.reshape(NY, NZ, NC, NX), ("y", "z", "c", "x"))
    feat = ("y", "z", "c")
    placed = (P("x", feat), P(feat), P("x"), P("x"), P(None, "x"), P(), P(feat))
    return jax.shard_map(
        shards,
        mesh=fine,
        in_specs=placed,
        out_specs=(P(None, (*feat, "x")), P(None, (*feat, "x"))),
        check_vma=False,
    )
```

time: 137 us -> 125 us (0.912)
  Pallas kernels: 26.3 us -> 16.5 us
  starting transfers between devices: 33.3 us -> 31.7 us
    ppermute x18 -> x6, starting transfers between devices: 21.2 us -> 6.89 us  [shift(): lax.ppermute(array, axis, [(i, (i + by) % length) for i in range(length)])]
    ppermute x0 -> x8, starting transfers between devices: none -> 10.2 us  [traded(): lax.ppermute(array, 'x', [(i, partner(i, which, stage)) for i in range(NX)])]
    pallas_call x17 -> x21, Pallas kernels: 26.3 us -> 16.5 us  [call(): pl.pallas_call(body, out_shape=outs, in_specs=specs, out_specs=jax.tree.m...]
    ppermute x18 -> x6, waiting for transfers between devices: 15.5 us -> 5.95 us  [shift(): lax.ppermute(array, axis, [(i, (i + by) % length) for i in range(length)])]
    ppermute x0 -> x8, waiting for transfers between devices: none -> 9.23 us  [traded(): lax.ppermute(array, 'x', [(i, partner(i, which, stage)) for i in range(NX)])]
    ppermute x4, starting transfers between devices: 12.1 us -> 14.6 us  [swapped(): return lax.ppermute(array, 'c', [(0, 1), (1, 0)])]
  transfers between devices with their start and end apart: 22 -> 18, of which waited for: 16 -> 15; matrix products, arithmetic and copies ran while one was open for 0% -> 0% of each run, Pallas kernels for 6% -> 5%
where the time goes in v4:
time: 125 us
  blocking collectives  56.7 us (45%)
  starting transfers between devices  31.7 us (25%)
  waiting for transfers between devices  18.8 us (15%)
  Pallas kernels  16.5 us (13%)
    all_to_all x2, blocking collectives, summed(): return lax.all_to_all(out, 'z', 0, 0, tiled=True)  26.2 us
    all_to_all x1, blocking collectives, shards(): lax.all_to_all(jnp.broadcast_to(margin[None], (NY * NZ, 8, 128)), ('y', '...  18.4 us
    pallas_call x21, Pallas kernels, call(): pl.pallas_call(body, out_shape=outs, in_specs=specs, out_specs=jax.tree.m...  16.5 us
    ppermute x4, starting transfers between devices, swapped(): return lax.ppermute(array, 'c', [(0, 1), (1, 0)])  14.6 us
    all_to_all x1, blocking collectives, shards(): arrived = lax.all_to_all(out, ('c', 'x'), 0, 0, tiled=True)  12.1 us
    ppermute x8, starting transfers between devices, traded(): lax.ppermute(array, 'x', [(i, partner(i, which, stage)) for i in range(NX)])  10.2 us
    ppermute x8, waiting for transfers between devices, traded(): lax.ppermute(array, 'x', [(i, partner(i, which, stage)) for i in range(NX)])  9.23 us
    ppermute x6, starting transfers between devices, shift(): lax.ppermute(array, axis, [(i, (i + by) % length) for i in range(length)])  6.89 us
  transfers between devices with their start and end apart: 18, of which 15 were waited for; matrix products, arithmetic and copies ran while one was open for 0% of the time, Pallas kernels for 5%

profile of v4, /device:TPU:1, one launch (start us, length us, event | category | flops | bytes accessed | tf_op | source)
XLA Modules:
  0.0 124.6 jit_solution(2126397636196733402)
XLA Ops:
  0.7 4.0 %shard_map.86 = (f32[8,128]{1,0:T(8,128)S(1)}, bf16[1024,4096]{1,0:T(8,128)(2,1)S(1)}, f32[1,4096]{1,0:T(1,128)S(1)}) custom-call(bf16[1024,4096]{1,0:T(8,128)(2,1)} %source.1, bf16[32,128]{1,0:T(8,128)(2,1)} %bitcast.17, s32[1,4]{1,0:T(1,128)S(1)} %add_bitcast_fusion.place), custom_call_target="tpu_custom_call" | custom-call | bytes 4194304 | tf_op jit(solution)/shard_map/pallas_call | solution.py:34
  4.7 3.3 %collective-permute-start = (f32[8,128]{1,0:T(8,128)S(1)}, f32[8,128]{1,0:T(8,128)S(1)}, u32[]{:S(2)}, u32[]{:S(2)}) collective-permute-start(f32[8,128]{1,0:T(8,128)S(1)} %get-tuple-element.37), channel_id=1, source_target_pairs={{0,4},{4,0},{1,5},{5,1},{2,6},{6,2},{3,7},{7,3},{8,12},{12,8},{9,1... | collective-permute-start | bytes 12296 | tf_op jit(solution)/shard_map/ppermute | solution.py:452
  8.0 0.8 collective-permute-done
  8.9 18.4 %all_to_all.20.margin_parts = f32[32,8,128]{2,1,0:T(8,128)S(1)} all-to-all(f32[32,8,128]{2,1,0:T(8,128)S(1)} %broadcast_in_dim.2), channel_id=1, replica_groups=mesh['y'=4,'z'=8,'c'=2,'x'=4] {'y','z'}, dimensions={0} | all-to-all | bytes 262144 | tf_op jit(solution)/shard_map/all_to_all | solution.py:478
  27.3 0.9 shard_map.87
  28.2 1.3 %collective-permute-start.3 = (bf16[32,3072]{1,0:T(8,128)(2,1)S(1)}, bf16[32,3072]{1,0:T(8,128)(2,1)S(1)}, u32[]{:S(2)}, u32[]{:S(2)}) collective-permute-start(bf16[32,3072]{1,0:T(8,128)(2,1)S(1)} %get-tuple-element.48), channel_id=1, source_target_pairs={{0,1},{1,0},{2,3},{3,2},{4,5},{5,4},{6,7},{7,6},{8,9},{9,8},{10,11... | collective-permute-start | bytes 589832 | tf_op jit(solution)/shard_map/ppermute | solution.py:448
  29.5 0.8 shard_map.88
  30.4 1.9 %collective-permute-start.1 = (bf16[32,3072]{1,0:T(8,128)(2,1)S(1)}, bf16[32,3072]{1,0:T(8,128)(2,1)S(1)}, u32[]{:S(2)}, u32[]{:S(2)}) collective-permute-start(bf16[32,3072]{1,0:T(8,128)(2,1)S(1)} %get-tuple-element.41), channel_id=1, source_target_pairs={{0,3},{1,2},{2,1},{3,0},{4,7},{5,6},{6,5},{7,4},{8,11},{9,10},{10,... | collective-permute-start | bytes 589832 | tf_op jit(solution)/shard_map/ppermute | solution.py:448
  32.3 0.5 collective-permute-done.3.arrived
  33.0 2.6 %collective-permute-start.4 = (bf16[32,2560]{1,0:T(8,128)(2,1)S(1)}, bf16[32,2560]{1,0:T(8,128)(2,1)S(1)}, u32[]{:S(2)}, u32[]{:S(2)}) collective-permute-start(bf16[32,2560]{1,0:T(8,128)(2,1)S(1)} %get-tuple-element.50), channel_id=1, source_target_pairs={{0,3},{1,2},{2,1},{3,0},{4,7},{5,6},{6,5},{7,4},{8,11},{9,10},{10,... | collective-permute-start | bytes 491528 | tf_op jit(solution)/shard_map/ppermute | solution.py:448
  35.5 0.7 collective-permute-done.1.arrived
  36.5 0.6 shard_map.90
  37.1 3.2 %collective-permute-done.4.wire = bf16[32,2560]{1,0:T(8,128)(2,1)S(1)} collective-permute-done((bf16[32,2560]{1,0:T(8,128)(2,1)S(1)}, bf16[32,2560]{1,0:T(8,128)(2,1)S(1)}, u32[]{:S(2)}, u32[]{:S(2)}) %collective-permute-start.4) | collective-permute-done | bytes 163872 | tf_op jit(solution)/shard_map/ppermute | solution.py:448
  40.2 1.4 %shard_map.92 = (f32[32,512]{1,0:T(8,128)S(1)}, bf16[32,2048]{1,0:T(8,128)(2,1)S(1)}, f32[32,1024]{1,0:T(8,128)S(1)}, f32[32,384]{1,0:T(8,128)S(1)}) custom-call(f32[32,2048]{1,0:T(8,128)S(1)} %get-tuple-element.49.part, bf16[32,2560]{1,0:T(8,128)(2,1)S(1)} %collective-permute-done.4.wire, bf16[1024,4096]{1,0:T(8,128)(2,1)S(1)} %get-tuple-element.38.examples, ...), custom_call_target="tpu_custom_call" | custom-call | flops 134217728 | bytes 4194304 | tf_op jit(solution)/shard_map/pallas_call | solution.py:34
  41.7 1.5 %shard_map.93 = (f32[32,512]{1,0:T(8,128)S(1)}, bf16[32,2048]{1,0:T(8,128)(2,1)S(1)}, f32[32,768]{1,0:T(8,128)S(1)}, f32[32,768]{1,0:T(8,128)S(1)}) custom-call(f32[32,2048]{1,0:T(8,128)S(1)} %get-tuple-element.42.part, bf16[32,2560]{1,0:T(8,128)(2,1)S(1)} %collective-permute-done.2.wire, bf16[1024,4096]{1,0:T(8,128)(2,1)S(1)} %get-tuple-element.38.examples, ...), custom_call_target="tpu_custom_call" | custom-call | flops 134217728 | bytes 4194304 | tf_op jit(solution)/shard_map/pallas_call | solution.py:34
  43.2 5.2 %collective-permute-start.5 = (f32[32,768]{1,0:T(8,128)S(1)}, f32[32,768]{1,0:T(8,128)S(1)}, u32[]{:S(2)}, u32[]{:S(2)}) collective-permute-start(f32[32,768]{1,0:T(8,128)S(1)} %get-tuple-element.54), channel_id=1, source_target_pairs={{0,4},{4,0},{1,5},{5,1},{2,6},{6,2},{3,7},{7,3},{8,12},{12,8},{9,1... | collective-permute-start | bytes 294920 | tf_op jit(solution)/shard_map/ppermute | solution.py:452
  48.4 0.9 collective-permute-done.5.arrived
  49.4 0.3 collective-permute-start.6
  49.7 1.7 %collective-permute-start.7 = (bf16[32,896]{1,0:T(8,128)(2,1)S(1)}, bf16[32,896]{1,0:T(8,128)(2,1)S(1)}, u32[]{:S(2)}, u32[]{:S(2)}) collective-permute-start(bf16[32,896]{1,0:T(8,128)(2,1)S(1)} %shard_map.94.wire0), channel_id=1, source_target_pairs={{0,128},{64,192},{128,0},{192,64},{1,129},{65,193},{129,1},{193,65... | collective-permute-start | bytes 172040 | tf_op jit(solution)/shard_map/ppermute | solution.py:440
  51.5 1.1 collective-permute-start.8
  52.6 1.0 collective-permute-done.6.wire1
  53.6 0.9 collective-permute-done.7.wire2
  54.6 0.7 collective-permute-done.8.wire3
  55.3 0.2 shard_map.95
  55.4 13.1 %all_to_all.21.arrived = bf16[8,32,640]{2,1,0:T(8,128)(2,1)S(1)} all-to-all(bf16[8,32,640]{2,1,0:T(8,128)(2,1)S(1)} %shard_map.95), channel_id=1, replica_groups=mesh['y'=4,'z'=8,'c'=2,'x'=4] {'z'}, dimensions={0} | all-to-all | bytes 655360 | tf_op jit(solution)/shard_map/all_to_all | solution.py:461
  68.6 0.3 shard_map.96
  68.8 3.7 %collective-permute-start.9 = (bf16[32,640]{1,0:T(8,128)(2,1)S(1)}, bf16[32,640]{1,0:T(8,128)(2,1)S(1)}, u32[]{:S(2)}, u32[]{:S(2)}) collective-permute-start(bf16[32,640]{1,0:T(8,128)(2,1)S(1)} %get-tuple-element.56.weighted), channel_id=1, source_target_pairs={{0,4},{4,0},{1,5},{5,1},{2,6},{6,2},{3,7},{7,3},{8,12},{12,8},{9,1... | collective-permute-start | bytes 122888 | tf_op jit(solution)/shard_map/ppermute | solution.py:452
  72.6 0.9 collective-permute-done.9.other
  73.4 0.9 shard_map.99.mine
  74.4 0.9 shard_map.97.mine
  75.3 2.1 %collective-permute-start.10 = (bf16[32,2048]{1,0:T(8,128)(2,1)S(1)}, bf16[32,2048]{1,0:T(8,128)(2,1)S(1)}, u32[]{:S(2)}, u32[]{:S(2)}) collective-permute-start(bf16[32,2048]{1,0:T(8,128)(2,1)S(1)} %shard_map.97.mine), channel_id=1, source_target_pairs={{0,3},{1,2},{2,1},{3,0},{4,7},{5,6},{6,5},{7,4},{8,11},{9,10},{10,... | collective-permute-start | bytes 393224 | tf_op jit(solution)/shard_map/ppermute | solution.py:448
  77.4 1.9 %collective-permute-done.12.other = bf16[32,2176]{1,0:T(8,128)(2,1)S(1)} collective-permute-done((bf16[32,2176]{1,0:T(8,128)(2,1)S(1)}, bf16[32,2176]{1,0:T(8,128)(2,1)S(1)}, u32[]{:S(2)}, u32[]{:S(2)}) %collective-permute-start.12) | collective-permute-done | bytes 139296 | tf_op jit(solution)/shard_map/ppermute | solution.py:448
  79.4 2.1 %collective-permute-start.13 = (bf16[32,2176]{1,0:T(8,128)(2,1)S(1)}, bf16[32,2176]{1,0:T(8,128)(2,1)S(1)}, u32[]{:S(2)}, u32[]{:S(2)}) collective-permute-start(bf16[32,2176]{1,0:T(8,128)(2,1)S(1)} %shard_map.100.mine), channel_id=1, source_target_pairs={{0,3},{1,2},{2,1},{3,0},{4,7},{5,6},{6,5},{7,4},{8,11},{9,10},{10,... | collective-permute-start | bytes 417800 | tf_op jit(solution)/shard_map/ppermute | solution.py:448
  81.7 2.9 %collective-permute-done.13.other = bf16[32,2176]{1,0:T(8,128)(2,1)S(1)} collective-permute-done((bf16[32,2176]{1,0:T(8,128)(2,1)S(1)}, bf16[32,2176]{1,0:T(8,128)(2,1)S(1)}, u32[]{:S(2)}, u32[]{:S(2)}) %collective-permute-start.13) | collective-permute-done | bytes 139296 | tf_op jit(solution)/shard_map/ppermute | solution.py:448
  84.6 1.6 %shard_map.101 = (f32[32,512]{1,0:T(8,128)S(1)}, f32[32,1024]{1,0:T(8,128)S(1)}, f32[32,384]{1,0:T(8,128)S(1)}, f32[32,128]{1,0:T(8,128)S(1)}) custom-call(bf16[32,2176]{1,0:T(8,128)(2,1)S(1)} %shard_map.100.mine, bf16[32,2176]{1,0:T(8,128)(2,1)S(1)} %collective-permute-done.13.other, f32[32,512]{1,0:T(8,128)S(1)} %get-tuple-element.60.rhs.rhs_a, ...), custom_call_target="tpu_custom_call" | custom-call | flops 134217728 | bytes 4194304 | tf_op jit(solution)/shard_map/pallas_call | solution.py:34
  86.2 1.5 %shard_map.102 = (f32[32,512]{1,0:T(8,128)S(1)}, f32[32,768]{1,0:T(8,128)S(1)}, f32[32,768]{1,0:T(8,128)S(1)}) custom-call(bf16[32,2048]{1,0:T(8,128)(2,1)S(1)} %shard_map.98.mine, bf16[32,2048]{1,0:T(8,128)(2,1)S(1)} %collective-permute-done.11.other, f32[32,512]{1,0:T(8,128)S(1)} %get-tuple-element.57.rhs.rhs_b, ...), custom_call_target="tpu_custom_call" | custom-call | flops 134217728 | bytes 4194304 | tf_op jit(solution)/shard_map/pallas_call | solution.py:34
  87.7 2.4 %collective-permute-start.14 = (f32[32,768]{1,0:T(8,128)S(1)}, f32[32,768]{1,0:T(8,128)S(1)}, u32[]{:S(2)}, u32[]{:S(2)}) collective-permute-start(f32[32,768]{1,0:T(8,128)S(1)} %get-tuple-element.66), channel_id=1, source_target_pairs={{0,4},{4,0},{1,5},{5,1},{2,6},{6,2},{3,7},{7,3},{8,12},{12,8},{9,1... | collective-permute-start | bytes 294920 | tf_op jit(solution)/shard_map/ppermute | solution.py:452
  90.1 0.9 collective-permute-done.14.arrived
  91.2 1.1 collective-permute-start.15
  92.2 2.6 %collective-permute-start.16 = (bf16[32,896]{1,0:T(8,128)(2,1)S(1)}, bf16[32,896]{1,0:T(8,128)(2,1)S(1)}, u32[]{:S(2)}, u32[]{:S(2)}) collective-permute-start(bf16[32,896]{1,0:T(8,128)(2,1)S(1)} %shard_map.103.wire0), channel_id=1, source_target_pairs={{0,128},{64,192},{128,0},{192,64},{1,129},{65,193},{129,1},{193,65... | collective-permute-start | bytes 172040 | tf_op jit(solution)/shard_map/ppermute | solution.py:440
  94.8 0.6 collective-permute-done.15.wire1
  95.4 2.0 %collective-permute-done.16.wire2 = bf16[32,896]{1,0:T(8,128)(2,1)S(1)} collective-permute-done((bf16[32,896]{1,0:T(8,128)(2,1)S(1)}, bf16[32,896]{1,0:T(8,128)(2,1)S(1)}, u32[]{:S(2)}, u32[]{:S(2)}) %collective-permute-start.16) | collective-permute-done | bytes 57376 | tf_op jit(solution)/shard_map/ppermute | solution.py:440
  97.4 0.7 collective-permute-done.17.wire3
  98.2 0.2 shard_map.104
  98.3 13.1 %all_to_all.22.arrived = bf16[8,32,640]{2,1,0:T(8,128)(2,1)S(1)} all-to-all(bf16[8,32,640]{2,1,0:T(8,128)(2,1)S(1)} %shard_map.104), channel_id=1, replica_groups=mesh['y'=4,'z'=8,'c'=2,'x'=4] {'z'}, dimensions={0} | all-to-all | bytes 655360 | tf_op jit(solution)/shard_map/all_to_all | solution.py:461
  111.5 0.2 shard_map.105
  111.7 12.1 %all_to_all.23.arrived = f32[8,32,128]{2,1,0:T(8,128)S(1)} all-to-all(f32[8,32,128]{2,1,0:T(8,128)S(1)} %shard_map.105), channel_id=1, replica_groups=mesh['y'=4,'z'=8,'c'=2,'x'=4] {'c','x'}, dimensions={0} | all-to-all | bytes 262144 | tf_op jit(solution)/shard_map/all_to_all | solution.py:645
  123.8 0.9 shard_map.106
  (26 shorter events, 1.0 us)
Async XLA Ops:
  0.6 26.7 %copy-start.2 = (s32[1024]{0:T(1024)S(1)}, s32[1024]{0:T(1024)}, u32[]{:S(2)}) copy-start(s32[1024]{0:T(1024)} %param.9) | copy-start | bytes 12292
  0.6 26.7 %copy-start.3 = (s32[1024]{0:T(1024)S(1)}, s32[1024]{0:T(1024)}, u32[]{:S(2)}) copy-start(s32[1024]{0:T(1024)} %param.10) | copy-start | bytes 12292
  0.7 26.7 %copy-start = (f32[32,1024]{1,0:T(8,128)S(1)}, f32[32,1024]{1,0:T(8,128)}, u32[]{:S(2)}) copy-start(f32[32,1024]{1,0:T(8,128)} %val_weight.1) | copy-start | bytes 393220
  4.7 4.2 %collective-permute-start = (f32[8,128]{1,0:T(8,128)S(1)}, f32[8,128]{1,0:T(8,128)S(1)}, u32[]{:S(2)}, u32[]{:S(2)}) collective-permute-start(f32[8,128]{1,0:T(8,128)S(1)} %get-tuple-element.37), channel_id=1, source_target_pairs={{0,4},{4,0},{1,5},{5,1},{2,6},{6,2},{3,7},{7,3},{8,12},{12,8},{9,1... | collective-permute-start | bytes 12296 | tf_op jit(solution)/shard_map/ppermute | solution.py:452
  27.3 9.1 %copy-start.1 = (s32[4096]{0:T(1024)S(1)}, s32[4096]{0:T(1024)}, u32[]{:S(2)}) copy-start(s32[4096]{0:T(1024)} %param.13) | copy-start | bytes 49156
  27.3 9.1 %copy-start.4 = (f32[256]{0:T(256)S(1)}, f32[256]{0:T(256)}, u32[]{:S(2)}) copy-start(f32[256]{0:T(256)} %param.12) | copy-start | bytes 3076
  28.2 4.6 %collective-permute-start.3 = (bf16[32,3072]{1,0:T(8,128)(2,1)S(1)}, bf16[32,3072]{1,0:T(8,128)(2,1)S(1)}, u32[]{:S(2)}, u32[]{:S(2)}) collective-permute-start(bf16[32,3072]{1,0:T(8,128)(2,1)S(1)} %get-tuple-element.48), channel_id=1, source_target_pairs={{0,1},{1,0},{2,3},{3,2},{4,5},{5,4},{6,7},{7,6},{8,9},{9,8},{10,11... | collective-permute-start | bytes 589832 | tf_op jit(solution)/shard_map/ppermute | solution.py:448
  30.4 5.8 %collective-permute-start.1 = (bf16[32,3072]{1,0:T(8,128)(2,1)S(1)}, bf16[32,3072]{1,0:T(8,128)(2,1)S(1)}, u32[]{:S(2)}, u32[]{:S(2)}) collective-permute-start(bf16[32,3072]{1,0:T(8,128)(2,1)S(1)} %get-tuple-element.41), channel_id=1, source_target_pairs={{0,3},{1,2},{2,1},{3,0},{4,7},{5,6},{6,5},{7,4},{8,11},{9,10},{10,... | collective-permute-start | bytes 589832 | tf_op jit(solution)/shard_map/ppermute | solution.py:448
  33.0 7.3 %collective-permute-start.4 = (bf16[32,2560]{1,0:T(8,128)(2,1)S(1)}, bf16[32,2560]{1,0:T(8,128)(2,1)S(1)}, u32[]{:S(2)}, u32[]{:S(2)}) collective-permute-start(bf16[32,2560]{1,0:T(8,128)(2,1)S(1)} %get-tuple-element.50), channel_id=1, source_target_pairs={{0,3},{1,2},{2,1},{3,0},{4,7},{5,6},{6,5},{7,4},{8,11},{9,10},{10,... | collective-permute-start | bytes 491528 | tf_op jit(solution)/shard_map/ppermute | solution.py:448
  36.3 5.4 %collective-permute-start.2 = (bf16[32,2560]{1,0:T(8,128)(2,1)S(1)}, bf16[32,2560]{1,0:T(8,128)(2,1)S(1)}, u32[]{:S(2)}, u32[]{:S(2)}) collective-permute-start(bf16[32,2560]{1,0:T(8,128)(2,1)S(1)} %get-tuple-element.43), channel_id=1, source_target_pairs={{0,1},{1,0},{2,3},{3,2},{4,5},{5,4},{6,7},{7,6},{8,9},{9,8},{10,11... | collective-permute-start | bytes 491528 | tf_op jit(solution)/shard_map/ppermute | solution.py:448
  43.2 6.1 %collective-permute-start.5 = (f32[32,768]{1,0:T(8,128)S(1)}, f32[32,768]{1,0:T(8,128)S(1)}, u32[]{:S(2)}, u32[]{:S(2)}) collective-permute-start(f32[32,768]{1,0:T(8,128)S(1)} %get-tuple-element.54), channel_id=1, source_target_pairs={{0,4},{4,0},{1,5},{5,1},{2,6},{6,2},{3,7},{7,3},{8,12},{12,8},{9,1... | collective-permute-start | bytes 294920 | tf_op jit(solution)/shard_map/ppermute | solution.py:452
  49.4 4.3 %collective-permute-start.6 = (bf16[32,896]{1,0:T(8,128)(2,1)S(1)}, bf16[32,896]{1,0:T(8,128)(2,1)S(1)}, u32[]{:S(2)}, u32[]{:S(2)}) collective-permute-start(bf16[32,896]{1,0:T(8,128)(2,1)S(1)} %shard_map.94.wire0), channel_id=1, source_target_pairs={{0,64},{64,128},{128,192},{192,0},{1,65},{65,129},{129,193},{193,1... | collective-permute-start | bytes 172040 | tf_op jit(solution)/shard_map/ppermute | solution.py:440
  49.7 4.8 %collective-permute-start.7 = (bf16[32,896]{1,0:T(8,128)(2,1)S(1)}, bf16[32,896]{1,0:T(8,128)(2,1)S(1)}, u32[]{:S(2)}, u32[]{:S(2)}) collective-permute-start(bf16[32,896]{1,0:T(8,128)(2,1)S(1)} %shard_map.94.wire0), channel_id=1, source_target_pairs={{0,128},{64,192},{128,0},{192,64},{1,129},{65,193},{129,1},{193,65... | collective-permute-start | bytes 172040 | tf_op jit(solution)/shard_map/ppermute | solution.py:440
  51.5 3.8 %collective-permute-start.8 = (bf16[32,896]{1,0:T(8,128)(2,1)S(1)}, bf16[32,896]{1,0:T(8,128)(2,1)S(1)}, u32[]{:S(2)}, u32[]{:S(2)}) collective-permute-start(bf16[32,896]{1,0:T(8,128)(2,1)S(1)} %shard_map.94.wire0), channel_id=1, source_target_pairs={{0,192},{64,0},{128,64},{192,128},{1,193},{65,1},{129,65},{193,129... | collective-permute-start | bytes 172040 | tf_op jit(solution)/shard_map/ppermute | solution.py:440
  68.8 4.6 %collective-permute-start.9 = (bf16[32,640]{1,0:T(8,128)(2,1)S(1)}, bf16[32,640]{1,0:T(8,128)(2,1)S(1)}, u32[]{:S(2)}, u32[]{:S(2)}) collective-permute-start(bf16[32,640]{1,0:T(8,128)(2,1)S(1)} %get-tuple-element.56.weighted), channel_id=1, source_target_pairs={{0,4},{4,0},{1,5},{5,1},{2,6},{6,2},{3,7},{7,3},{8,12},{12,8},{9,1... | collective-permute-start | bytes 122888 | tf_op jit(solution)/shard_map/ppermute | solution.py:452
  74.3 4.9 %collective-permute-start.12 = (bf16[32,2176]{1,0:T(8,128)(2,1)S(1)}, bf16[32,2176]{1,0:T(8,128)(2,1)S(1)}, u32[]{:S(2)}, u32[]{:S(2)}) collective-permute-start(bf16[32,2176]{1,0:T(8,128)(2,1)S(1)} %shard_map.99.mine), channel_id=1, source_target_pairs={{0,1},{1,0},{2,3},{3,2},{4,5},{5,4},{6,7},{7,6},{8,9},{9,8},{10,11... | collective-permute-start | bytes 417800 | tf_op jit(solution)/shard_map/ppermute | solution.py:448
  75.3 6.3 %collective-permute-start.10 = (bf16[32,2048]{1,0:T(8,128)(2,1)S(1)}, bf16[32,2048]{1,0:T(8,128)(2,1)S(1)}, u32[]{:S(2)}, u32[]{:S(2)}) collective-permute-start(bf16[32,2048]{1,0:T(8,128)(2,1)S(1)} %shard_map.97.mine), channel_id=1, source_target_pairs={{0,3},{1,2},{2,1},{3,0},{4,7},{5,6},{6,5},{7,4},{8,11},{9,10},{10,... | collective-permute-start | bytes 393224 | tf_op jit(solution)/shard_map/ppermute | solution.py:448
  79.4 5.2 %collective-permute-start.13 = (bf16[32,2176]{1,0:T(8,128)(2,1)S(1)}, bf16[32,2176]{1,0:T(8,128)(2,1)S(1)}, u32[]{:S(2)}, u32[]{:S(2)}) collective-permute-start(bf16[32,2176]{1,0:T(8,128)(2,1)S(1)} %shard_map.100.mine), channel_id=1, source_target_pairs={{0,3},{1,2},{2,1},{3,0},{4,7},{5,6},{6,5},{7,4},{8,11},{9,10},{10,... | collective-permute-start | bytes 417800 | tf_op jit(solution)/shard_map/ppermute | solution.py:448
  81.6 4.6 %collective-permute-start.11 = (bf16[32,2048]{1,0:T(8,128)(2,1)S(1)}, bf16[32,2048]{1,0:T(8,128)(2,1)S(1)}, u32[]{:S(2)}, u32[]{:S(2)}) collective-permute-start(bf16[32,2048]{1,0:T(8,128)(2,1)S(1)} %shard_map.98.mine), channel_id=1, source_target_pairs={{0,1},{1,0},{2,3},{3,2},{4,5},{5,4},{6,7},{7,6},{8,9},{9,8},{10,11... | collective-permute-start | bytes 393224 | tf_op jit(solution)/shard_map/ppermute | solution.py:448
  87.7 3.4 %collective-permute-start.14 = (f32[32,768]{1,0:T(8,128)S(1)}, f32[32,768]{1,0:T(8,128)S(1)}, u32[]{:S(2)}, u32[]{:S(2)}) collective-permute-start(f32[32,768]{1,0:T(8,128)S(1)} %get-tuple-element.66), channel_id=1, source_target_pairs={{0,4},{4,0},{1,5},{5,1},{2,6},{6,2},{3,7},{7,3},{8,12},{12,8},{9,1... | collective-permute-start | bytes 294920 | tf_op jit(solution)/shard_map/ppermute | solution.py:452
  91.2 4.3 %collective-permute-start.15 = (bf16[32,896]{1,0:T(8,128)(2,1)S(1)}, bf16[32,896]{1,0:T(8,128)(2,1)S(1)}, u32[]{:S(2)}, u32[]{:S(2)}) collective-permute-start(bf16[32,896]{1,0:T(8,128)(2,1)S(1)} %shard_map.103.wire0), channel_id=1, source_target_pairs={{0,64},{64,128},{128,192},{192,0},{1,65},{65,129},{129,193},{193,1... | collective-permute-start | bytes 172040 | tf_op jit(solution)/shard_map/ppermute | solution.py:440
  92.2 5.2 %collective-permute-start.16 = (bf16[32,896]{1,0:T(8,128)(2,1)S(1)}, bf16[32,896]{1,0:T(8,128)(2,1)S(1)}, u32[]{:S(2)}, u32[]{:S(2)}) collective-permute-start(bf16[32,896]{1,0:T(8,128)(2,1)S(1)} %shard_map.103.wire0), channel_id=1, source_target_pairs={{0,128},{64,192},{128,0},{192,64},{1,129},{65,193},{129,1},{193,65... | collective-permute-start | bytes 172040 | tf_op jit(solution)/shard_map/ppermute | solution.py:440
  94.8 3.3 %collective-permute-start.17 = (bf16[32,896]{1,0:T(8,128)(2,1)S(1)}, bf16[32,896]{1,0:T(8,128)(2,1)S(1)}, u32[]{:S(2)}, u32[]{:S(2)}) collective-permute-start(bf16[32,896]{1,0:T(8,128)(2,1)S(1)} %shard_map.103.wire0), channel_id=1, source_target_pairs={{0,192},{64,0},{128,64},{192,128},{1,193},{65,1},{129,65},{193,129... | collective-permute-start | bytes 172040 | tf_op jit(solution)/shard_map/ppermute | solution.py:440

commit v5 on v4

--- a/solution.py
+++ b/solution.py
@@ -189,9 +189,9 @@
     wire[:, NX * PART :] = (found - found.astype(BF16).astype(F32)).astype(BF16)
 
 
-def tangents(pieces, which, examples, before, tang):
-    for i in range(N // 256):
-        rows = slice(i * 256, (i + 1) * 256)
+def tangents(pieces, which, examples, before, tang, start, count):
+    for i in range(count // 256):
+        rows = pl.ds(pl.multiple_of(start + i * 256, 256), 256)
         total = None if before is None else before[:, rows]
         for k in range(NX):
             term = lax.dot_general(
@@ -201,19 +201,24 @@
                 preferred_element_type=F32,
             )
             total = term if total is None else total + term
-        tang[:, rows] = total
-
-
-def halves(tang, scalars, blocks, core, keep, send):
-    for out, which in ((keep, core), (send, 1 - core)):
-        out[:, :HALF] = tang[:, chunk(which, HALF)]
-        out[:, HALF : HALF + LANES] = scalars
-        out[:, HALF + LANES :] = blocks[:, chunk(which, LANES)]
-
-
-def first_part(
-    which, part, wire, examples, lamf, wfloat, onehot, place, rhs, lows, before, tang
-):
+        tang[:, i * 256 : (i + 1) * 256] = total
+
+
+def other_half(pieces, examples, before, scalars, blocks, total, place, send, rest):
+    core = place[0, 2]
+    tangents(pieces, 1, examples, before, send, (1 - core) * HALF, HALF)
+    total[...] = blocks
+    send[:, HALF : HALF + LANES] = scalars
+    send[:, HALF + LANES :] = total[:, chunk(1 - core, LANES)]
+    rest[:, :LANES] = scalars
+    rest[:, LANES:] = total[:, chunk(core, LANES)]
+
+
+def own_half(pieces, examples, before, place, keep):
+    tangents(pieces, 1, examples, before, keep, place[0, 2] * HALF, HALF)
+
+
+def first_part(which, part, wire, lamf, wfloat, onehot, place, rhs, lows):
     x = place[0, 3]
     lows[...] = (part[...] + wire[:, : NX * PART].astype(F32)).astype(BF16)
     cols = chunk(x, PART)
@@ -226,38 +231,35 @@
     scaled = jnp.sum(lamf[:, own] * square, axis=1, keepdims=True)
     hot = onehot[:, which * PART : (which + 1) * PART]
     blocks = block_sums(vec, wfloat[:, own], hot)
-    tangents(lows, which, examples, before, tang)
     return columns([norm, scaled]), blocks
 
 
 def first_tangents(
     part, wire, examples, lamf, wfloat, onehot, place, rhs, lows, tang, sums
 ):
-    scalars, blocks = first_part(
-        0, part, wire, examples, lamf, wfloat, onehot, place, rhs, lows, None, tang
-    )
+    scalars, blocks = first_part(0, part, wire, lamf, wfloat, onehot, place, rhs, lows)
+    tangents(lows, 0, examples, None, tang, 0, N)
     sums[:, :LANES] = scalars
     sums[:, LANES:] = blocks
 
 
 def first_tangents_rest(
     part, wire, examples, lamf, wfloat, onehot, before, sums, place,
-    rhs, lows, keep, send, tang, total,
+    rhs, lows, send, rest, total,
 ):
-    scalars, blocks = first_part(
-        1, part, wire, examples, lamf, wfloat, onehot, place, rhs, lows, before, tang
-    )
-    total[...] = sums[:, LANES:] + blocks
-    halves(tang, sums[:, :LANES] + scalars, total, place[0, 2], keep, send)
-
-
-def to_wire(keep, arrived, wire):
-    total = keep[...] + arrived[...]
-    wire[:, :HALF] = total[:, :HALF].astype(BF16)
-    wire[:, HALF : HALF + LANES] = to_terms(total[:, HALF : HALF + LANES]).astype(BF16)
-    high, rest = terms(total[:, HALF + LANES :], 2)
+    scalars, blocks = first_part(1, part, wire, lamf, wfloat, onehot, place, rhs, lows)
+    scalars = sums[:, :LANES] + scalars
+    blocks = sums[:, LANES:] + blocks
+    other_half(lows, examples, before, scalars, blocks, total, place, send, rest)
+
+
+def to_wire(keep, rest, arrived, wire):
+    wire[:, :HALF] = (keep[...] + arrived[:, :HALF]).astype(BF16)
+    scalars = rest[:, :LANES] + arrived[:, HALF : HALF + LANES]
+    wire[:, HALF : HALF + LANES] = to_terms(scalars).astype(BF16)
+    high, low = terms(rest[:, LANES:] + arrived[:, HALF + LANES :], 2)
     wire[:, HALF + LANES : HALF + 2 * LANES] = high.astype(BF16)
-    wire[:, HALF + 2 * LANES :] = rest.astype(BF16)
+    wire[:, HALF + 2 * LANES :] = low.astype(BF16)
 
 
 def along_y(wire0, wire1, wire2, wire3, place, out):
@@ -299,27 +301,35 @@
     kept[:, LANES:] = blocks
 
 
-def product_parts(which, weighted, other, examples, place, part):
-    core = place[0, 2]
+def own_products(weighted, examples, place, part_a, part_b):
+    rows = chunk(place[0, 2], HALF)
+    for which, part in enumerate((part_a, part_b)):
+        for k in range(NX):
+            part[:, k * PART : (k + 1) * PART] = jnp.dot(
+                weighted[:, :HALF],
+                examples[rows, part_of(k, which)],
+                preferred_element_type=F32,
+            )
+
+
+def product_parts(which, mine, other, examples, place, part):
+    rows = chunk(1 - place[0, 2], HALF)
     for k in range(NX):
-        cols = part_of(k, which)
-        mine = jnp.dot(
-            weighted[:, :HALF], examples[chunk(core, HALF), cols], preferred_element_type=F32
+        cols = slice(k * PART, (k + 1) * PART)
+        rest = jnp.dot(
+            other[:, :HALF], examples[rows, part_of(k, which)], preferred_element_type=F32
         )
-        rest = jnp.dot(
-            other[:, :HALF], examples[chunk(1 - core, HALF), cols], preferred_element_type=F32
-        )
-        part[:, k * PART : (k + 1) * PART] = (mine + rest).astype(BF16)
-
-
-def products(weighted, other, kept, examples, place, part):
+        part[:, cols] = (mine[:, cols] + rest).astype(BF16)
+
+
+def products(mine, other, kept, examples, place, part):
     scalars = kept[:, :LANES] + from_terms(other[:, HALF:].astype(F32))
     part[:, NX * PART :] = to_terms(scalars).astype(BF16)
-    product_parts(0, weighted, other, examples, place, part)
-
-
-def products_rest(weighted, other, examples, place, part):
-    product_parts(1, weighted, other, examples, place, part)
+    product_parts(0, mine, other, examples, place, part)
+
+
+def products_rest(mine, other, examples, place, part):
+    product_parts(1, mine, other, examples, place, part)
 
 
 def product_pairs(mine, other, wire):
@@ -330,8 +340,7 @@
 
 
 def second_part(
-    which, alpha, mine, other, rhs, lows, examples, lamf, wfloat, onehot, place,
-    resid, pieces, before, tang,
+    which, alpha, mine, other, rhs, lows, lamf, wfloat, onehot, place, resid, pieces
 ):
     def step(cols, lam, direc):
         total = mine[:, cols].astype(F32) + other[:, cols].astype(F32)
@@ -358,7 +367,6 @@
     )
     hot = onehot[:, which * PART : (which + 1) * PART]
     blocks = block_sums(left, wfloat[:, own], hot)
-    tangents(pieces, which, examples, before, tang)
     return scalars, blocks
 
 
@@ -372,23 +380,24 @@
     alpha = norm / (curv / F32(TOTAL) + scaled)
     kept[...] = jnp.where(lane_ids() == 3, alpha, tile)
     scalars, blocks = second_part(
-        0, alpha, mine, other, rhs, lows, examples, lamf, wfloat, onehot, place,
-        resid, pieces, None, tang,
-    )
+        0, alpha, mine, other, rhs, lows, lamf, wfloat, onehot, place, resid, pieces
+    )
+    tangents(pieces, 0, examples, None, tang, 0, N)
     sums[:, :LANES] = scalars
     sums[:, LANES:] = blocks
 
 
 def second_tangents_rest(
     mine, other, rhs, lows, examples, lamf, wfloat, onehot, before, sums, kept,
-    place, resid, keep, send, tang, total, pieces,
+    place, resid, pieces, send, rest, total,
 ):
     scalars, blocks = second_part(
-        1, column(kept[...], 3), mine, other, rhs, lows, examples, lamf,
-        wfloat, onehot, place, resid, pieces, before, tang,
-    )
-    total[...] = sums[:, LANES:] + blocks
-    halves(tang, sums[:, :LANES] + scalars, total, place[0, 2], keep, send)
+        1, column(kept[...], 3), mine, other, rhs, lows, lamf, wfloat, onehot, place,
+        resid, pieces,
+    )
+    scalars = sums[:, :LANES] + scalars
+    blocks = sums[:, LANES:] + blocks
+    other_half(pieces, examples, before, scalars, blocks, total, place, send, rest)
 
 
 def curvature(arrived, curvew, tang_first, kept, place, out):
@@ -440,10 +449,6 @@
     return lax.ppermute(array, axis, [(i, (i + by) % length) for i in range(length)])
 
 
-def shifted(array, axis, length):
-    return [shift(array, axis, length, s) for s in range(1, length)]
-
-
 def traded(array, which, stage):
     return lax.ppermute(array, "x", [(i, partner(i, which, stage)) for i in range(NX)])
 
@@ -452,11 +457,14 @@
     return lax.ppermute(array, "c", [(0, 1), (1, 0)])
 
 
-def summed(keep, send, place):
-    wire = call(to_wire, shape(R, HALF + 3 * LANES, dtype=BF16), keep, swapped(send))
-    arrived = shifted(wire, "y", NY)
+def summed(pieces, examples, before, send, rest, place, flops):
+    arrived = swapped(send)
+    keep = call(own_half, shape(R, HALF), pieces, examples, before, place, flops=flops)
+    wire = call(to_wire, shape(R, HALF + 3 * LANES, dtype=BF16), keep, rest, arrived)
+    far = shift(wire, "y", NY, 2)
+    near = [shift(wire, "y", NY, by) for by in (1, NY - 1)]
     out = call(
-        along_y, shape(NZ, R, HALF + LANES, dtype=BF16), wire, *arrived, place
+        along_y, shape(NZ, R, HALF + LANES, dtype=BF16), wire, *near, far, place
     )
     return lax.all_to_all(out, "z", 0, 0, tiled=True)
 
@@ -530,7 +538,7 @@
         place,
     )
     wire_b = traded(wire_b, 1, 1)
-    pair = [shape(R, HALF + 2 * LANES)] * 2
+    pair = [shape(R, HALF + 2 * LANES), shape(R, 2 * LANES)]
     low = shape(R, NX * PART, dtype=BF16)
     rhs_a, lows_a, tang, sums = call(
         first_tangents,
@@ -544,7 +552,7 @@
         place,
         flops=work,
     )
-    rhs_b, lows_b, keep, send = call(
+    rhs_b, lows_b, send, rest = call(
         first_tangents_rest,
         [shape(R, PART), low, *pair],
         part_b,
@@ -556,10 +564,10 @@
         tang,
         sums,
         place,
-        scratch=[pltpu.VMEM((R, N), F32), pltpu.VMEM((R, NB), F32)],
-        flops=work,
-    )
-    arrived = summed(keep, send, place)
+        scratch=[pltpu.VMEM((R, NB), F32)],
+        flops=work,
+    )
+    arrived = summed(lows_b, examples, tang, send, rest, place, work // 2)
     tang_first, weighted, kept_first = call(
         weigh,
         [shape(R, HALF), shape(R, HALF + LANES, dtype=BF16), shape(R, 2 * LANES)],
@@ -568,10 +576,11 @@
         place,
     )
     other = swapped(weighted)
+    own_a, own_b = call(own_products, [whole, whole], weighted, examples, place, flops=work)
     part_a = call(
         products,
         shape(R, NX * PART + LANES, dtype=BF16),
-        weighted,
+        own_a,
         other,
         kept_first,
         examples,
@@ -582,7 +591,7 @@
     part_b = call(
         products_rest,
         shape(R, NX * PART, dtype=BF16),
-        weighted,
+        own_b,
         other,
         examples,
         place,
@@ -610,9 +619,9 @@
         scratch=[pltpu.VMEM((R, NX * PART), BF16)],
         flops=work,
     )
-    resid_b, keep, send = call(
+    resid_b, pieces, send, rest = call(
         second_tangents_rest,
-        [shape(R, PART), *pair],
+        [shape(R, PART), low, *pair],
         mine_b,
         other_b,
         rhs_b,
@@ -625,14 +634,10 @@
         sums,
         kept,
         place,
-        scratch=[
-            pltpu.VMEM((R, N), F32),
-            pltpu.VMEM((R, NB), F32),
-            pltpu.VMEM((R, NX * PART), BF16),
-        ],
-        flops=work,
-    )
-    arrived = summed(keep, send, place)
+        scratch=[pltpu.VMEM((R, NB), F32)],
+        flops=work,
+    )
+    arrived = summed(pieces, examples, tang, send, rest, place, work // 2)
     out = call(
         curvature,
         shape(NC * NX, R, LANES),

time: 125 us -> 123 us (0.984)
  starting transfers between devices: 31.7 us -> 30 us
    ppermute x6, waiting for transfers between devices: 5.95 us -> 8.5 us  [shift(): lax.ppermute(array, axis, [(i, (i + by) % length) for i in range(length)])]
    ppermute x4, waiting for transfers between devices: 3.58 us -> 1.05 us  [swapped(): return lax.ppermute(array, 'c', [(0, 1), (1, 0)])]
    ppermute x6, starting transfers between devices: 6.89 us -> 4.47 us  [shift(): lax.ppermute(array, axis, [(i, (i + by) % length) for i in range(length)])]
    pallas_call x21 -> x24, Pallas kernels: 16.5 us -> 17.1 us  [call(): pl.pallas_call(body, out_shape=outs, in_specs=specs, out_specs=jax.tree.m...]
  transfers between devices with their start and end apart: 18 -> 18, of which waited for: 15 -> 13; matrix products, arithmetic and copies ran while one was open for 0% -> 0% of each run, Pallas kernels for 5% -> 7%
where the time goes in v5:
time: 123 us
  blocking collectives  55.9 us (45%)
  starting transfers between devices  30 us (24%)
  waiting for transfers between devices  19.2 us (16%)
  Pallas kernels  17.1 us (14%)
    all_to_all x2, blocking collectives, summed(): return lax.all_to_all(out, 'z', 0, 0, tiled=True)  25.3 us
    all_to_all x1, blocking collectives, shards(): lax.all_to_all(jnp.broadcast_to(margin[None], (NY * NZ, 8, 128)), ('y', '...  18.4 us
    pallas_call x24, Pallas kernels, call(): pl.pallas_call(body, out_shape=outs, in_specs=specs, out_specs=jax.tree.m...  17.1 us
    ppermute x4, starting transfers between devices, swapped(): return lax.ppermute(array, 'c', [(0, 1), (1, 0)])  15.4 us
    all_to_all x1, blocking collectives, shards(): arrived = lax.all_to_all(out, ('c', 'x'), 0, 0, tiled=True)  12.1 us
    ppermute x8, starting transfers between devices, traded(): lax.ppermute(array, 'x', [(i, partner(i, which, stage)) for i in range(NX)])  10.2 us
    ppermute x8, waiting for transfers between devices, traded(): lax.ppermute(array, 'x', [(i, partner(i, which, stage)) for i in range(NX)])  9.64 us
    ppermute x6, waiting for transfers between devices, shift(): lax.ppermute(array, axis, [(i, (i + by) % length) for i in range(length)])  8.5 us
  transfers between devices with their start and end apart: 18, of which 13 were waited for; matrix products, arithmetic and copies ran while one was open for 0% of the time, Pallas kernels for 7%

profile of v5, /device:TPU:1, one launch (start us, length us, event | category | flops | bytes accessed | tf_op | source)
XLA Modules:
  0.0 123.2 jit_solution(12686323546958388681)
XLA Ops:
  0.7 4.0 %shard_map.86 = (f32[8,128]{1,0:T(8,128)S(1)}, bf16[1024,4096]{1,0:T(8,128)(2,1)S(1)}, f32[1,4096]{1,0:T(1,128)S(1)}) custom-call(bf16[1024,4096]{1,0:T(8,128)(2,1)} %source.1, bf16[32,128]{1,0:T(8,128)(2,1)} %bitcast.17, s32[1,4]{1,0:T(1,128)S(1)} %add_bitcast_fusion.place), custom_call_target="tpu_custom_call" | custom-call | bytes 4194304 | tf_op jit(solution)/shard_map/pallas_call | solution.py:34
  4.7 3.3 %collective-permute-start = (f32[8,128]{1,0:T(8,128)S(1)}, f32[8,128]{1,0:T(8,128)S(1)}, u32[]{:S(2)}, u32[]{:S(2)}) collective-permute-start(f32[8,128]{1,0:T(8,128)S(1)} %get-tuple-element.40), channel_id=1, source_target_pairs={{0,4},{4,0},{1,5},{5,1},{2,6},{6,2},{3,7},{7,3},{8,12},{12,8},{9,1... | collective-permute-start | bytes 12296 | tf_op jit(solution)/shard_map/ppermute | solution.py:457
  8.0 0.8 collective-permute-done
  8.9 18.4 %all_to_all.20.margin_parts = f32[32,8,128]{2,1,0:T(8,128)S(1)} all-to-all(f32[32,8,128]{2,1,0:T(8,128)S(1)} %broadcast_in_dim.2), channel_id=1, replica_groups=mesh['y'=4,'z'=8,'c'=2,'x'=4] {'y','z'}, dimensions={0} | all-to-all | bytes 262144 | tf_op jit(solution)/shard_map/all_to_all | solution.py:486
  27.3 0.9 shard_map.87
  28.2 1.3 %collective-permute-start.3 = (bf16[32,3072]{1,0:T(8,128)(2,1)S(1)}, bf16[32,3072]{1,0:T(8,128)(2,1)S(1)}, u32[]{:S(2)}, u32[]{:S(2)}) collective-permute-start(bf16[32,3072]{1,0:T(8,128)(2,1)S(1)} %get-tuple-element.51), channel_id=1, source_target_pairs={{0,1},{1,0},{2,3},{3,2},{4,5},{5,4},{6,7},{7,6},{8,9},{9,8},{10,11... | collective-permute-start | bytes 589832 | tf_op jit(solution)/shard_map/ppermute | solution.py:453
  29.5 0.8 shard_map.88
  30.4 1.9 %collective-permute-start.1 = (bf16[32,3072]{1,0:T(8,128)(2,1)S(1)}, bf16[32,3072]{1,0:T(8,128)(2,1)S(1)}, u32[]{:S(2)}, u32[]{:S(2)}) collective-permute-start(bf16[32,3072]{1,0:T(8,128)(2,1)S(1)} %get-tuple-element.44), channel_id=1, source_target_pairs={{0,3},{1,2},{2,1},{3,0},{4,7},{5,6},{6,5},{7,4},{8,11},{9,10},{10,... | collective-permute-start | bytes 589832 | tf_op jit(solution)/shard_map/ppermute | solution.py:453
  32.3 0.5 collective-permute-done.3.arrived
  33.0 2.6 %collective-permute-start.4 = (bf16[32,2560]{1,0:T(8,128)(2,1)S(1)}, bf16[32,2560]{1,0:T(8,128)(2,1)S(1)}, u32[]{:S(2)}, u32[]{:S(2)}) collective-permute-start(bf16[32,2560]{1,0:T(8,128)(2,1)S(1)} %get-tuple-element.53), channel_id=1, source_target_pairs={{0,3},{1,2},{2,1},{3,0},{4,7},{5,6},{6,5},{7,4},{8,11},{9,10},{10,... | collective-permute-start | bytes 491528 | tf_op jit(solution)/shard_map/ppermute | solution.py:453
  35.5 0.7 collective-permute-done.1.arrived
  36.5 0.6 shard_map.90
  37.1 3.2 %collective-permute-done.4.wire = bf16[32,2560]{1,0:T(8,128)(2,1)S(1)} collective-permute-done((bf16[32,2560]{1,0:T(8,128)(2,1)S(1)}, bf16[32,2560]{1,0:T(8,128)(2,1)S(1)}, u32[]{:S(2)}, u32[]{:S(2)}) %collective-permute-start.4) | collective-permute-done | bytes 163872 | tf_op jit(solution)/shard_map/ppermute | solution.py:453
  40.2 1.4 %shard_map.92 = (f32[32,512]{1,0:T(8,128)S(1)}, bf16[32,2048]{1,0:T(8,128)(2,1)S(1)}, f32[32,1024]{1,0:T(8,128)S(1)}, f32[32,384]{1,0:T(8,128)S(1)}) custom-call(f32[32,2048]{1,0:T(8,128)S(1)} %get-tuple-element.52.part, bf16[32,2560]{1,0:T(8,128)(2,1)S(1)} %collective-permute-done.4.wire, bf16[1024,4096]{1,0:T(8,128)(2,1)S(1)} %get-tuple-element.41.examples, ...), custom_call_target="tpu_custom_call" | custom-call | flops 134217728 | bytes 4194304 | tf_op jit(solution)/shard_map/pallas_call | solution.py:34
  41.7 0.8 shard_map.93
  42.6 5.1 %collective-permute-start.5 = (f32[32,768]{1,0:T(8,128)S(1)}, f32[32,768]{1,0:T(8,128)S(1)}, u32[]{:S(2)}, u32[]{:S(2)}) collective-permute-start(f32[32,768]{1,0:T(8,128)S(1)} %get-tuple-element.58), channel_id=1, source_target_pairs={{0,4},{4,0},{1,5},{5,1},{2,6},{6,2},{3,7},{7,3},{8,12},{12,8},{9,1... | collective-permute-start | bytes 294920 | tf_op jit(solution)/shard_map/ppermute | solution.py:457
  47.7 0.8 shard_map.94.keep
  48.7 1.2 collective-permute-start.8
  49.9 1.6 %collective-permute-start.7 = (bf16[32,896]{1,0:T(8,128)(2,1)S(1)}, bf16[32,896]{1,0:T(8,128)(2,1)S(1)}, u32[]{:S(2)}, u32[]{:S(2)}) collective-permute-start(bf16[32,896]{1,0:T(8,128)(2,1)S(1)} %shard_map.95.wire0), channel_id=1, source_target_pairs={{0,192},{64,0},{128,64},{192,128},{1,193},{65,1},{129,65},{193,129... | collective-permute-start | bytes 172040 | tf_op jit(solution)/shard_map/ppermute | solution.py:449
  51.5 1.8 %collective-permute-done.8.wire3 = bf16[32,896]{1,0:T(8,128)(2,1)S(1)} collective-permute-done((bf16[32,896]{1,0:T(8,128)(2,1)S(1)}, bf16[32,896]{1,0:T(8,128)(2,1)S(1)}, u32[]{:S(2)}, u32[]{:S(2)}) %collective-permute-start.8) | collective-permute-done | bytes 57376 | tf_op jit(solution)/shard_map/ppermute | solution.py:449
  53.3 0.2 collective-permute-done.7.wire2
  53.5 2.2 %collective-permute-done.6.wire1 = bf16[32,896]{1,0:T(8,128)(2,1)S(1)} collective-permute-done((bf16[32,896]{1,0:T(8,128)(2,1)S(1)}, bf16[32,896]{1,0:T(8,128)(2,1)S(1)}, u32[]{:S(2)}, u32[]{:S(2)}) %collective-permute-start.6) | collective-permute-done | bytes 57376 | tf_op jit(solution)/shard_map/ppermute | solution.py:449
  55.7 0.2 shard_map.96
  55.9 12.2 %all_to_all.21.arrived = bf16[8,32,640]{2,1,0:T(8,128)(2,1)S(1)} all-to-all(bf16[8,32,640]{2,1,0:T(8,128)(2,1)S(1)} %shard_map.96), channel_id=1, replica_groups=mesh['y'=4,'z'=8,'c'=2,'x'=4] {'z'}, dimensions={0} | all-to-all | bytes 655360 | tf_op jit(solution)/shard_map/all_to_all | solution.py:469
  68.1 0.3 shard_map.97
  68.4 4.6 %collective-permute-start.9 = (bf16[32,640]{1,0:T(8,128)(2,1)S(1)}, bf16[32,640]{1,0:T(8,128)(2,1)S(1)}, u32[]{:S(2)}, u32[]{:S(2)}) collective-permute-start(bf16[32,640]{1,0:T(8,128)(2,1)S(1)} %get-tuple-element.60.weighted), channel_id=1, source_target_pairs={{0,4},{4,0},{1,5},{5,1},{2,6},{6,2},{3,7},{7,3},{8,12},{12,8},{9,1... | collective-permute-start | bytes 122888 | tf_op jit(solution)/shard_map/ppermute | solution.py:457
  73.0 0.9 shard_map.98
  73.9 0.6 shard_map.101.mine
  74.6 0.6 shard_map.99.mine
  75.1 2.1 %collective-permute-start.10 = (bf16[32,2048]{1,0:T(8,128)(2,1)S(1)}, bf16[32,2048]{1,0:T(8,128)(2,1)S(1)}, u32[]{:S(2)}, u32[]{:S(2)}) collective-permute-start(bf16[32,2048]{1,0:T(8,128)(2,1)S(1)} %shard_map.99.mine), channel_id=1, source_target_pairs={{0,3},{1,2},{2,1},{3,0},{4,7},{5,6},{6,5},{7,4},{8,11},{9,10},{10,... | collective-permute-start | bytes 393224 | tf_op jit(solution)/shard_map/ppermute | solution.py:453
  77.2 2.3 %collective-permute-done.12.other = bf16[32,2176]{1,0:T(8,128)(2,1)S(1)} collective-permute-done((bf16[32,2176]{1,0:T(8,128)(2,1)S(1)}, bf16[32,2176]{1,0:T(8,128)(2,1)S(1)}, u32[]{:S(2)}, u32[]{:S(2)}) %collective-permute-start.12) | collective-permute-done | bytes 139296 | tf_op jit(solution)/shard_map/ppermute | solution.py:453
  79.5 0.2 shard_map.102.mine
  79.7 2.1 %collective-permute-start.13 = (bf16[32,2176]{1,0:T(8,128)(2,1)S(1)}, bf16[32,2176]{1,0:T(8,128)(2,1)S(1)}, u32[]{:S(2)}, u32[]{:S(2)}) collective-permute-start(bf16[32,2176]{1,0:T(8,128)(2,1)S(1)} %shard_map.102.mine), channel_id=1, source_target_pairs={{0,3},{1,2},{2,1},{3,0},{4,7},{5,6},{6,5},{7,4},{8,11},{9,10},{10,... | collective-permute-start | bytes 417800 | tf_op jit(solution)/shard_map/ppermute | solution.py:453
  82.0 2.9 %collective-permute-done.13.other = bf16[32,2176]{1,0:T(8,128)(2,1)S(1)} collective-permute-done((bf16[32,2176]{1,0:T(8,128)(2,1)S(1)}, bf16[32,2176]{1,0:T(8,128)(2,1)S(1)}, u32[]{:S(2)}, u32[]{:S(2)}) %collective-permute-start.13) | collective-permute-done | bytes 139296 | tf_op jit(solution)/shard_map/ppermute | solution.py:453
  84.9 1.6 %shard_map.103 = (f32[32,512]{1,0:T(8,128)S(1)}, f32[32,1024]{1,0:T(8,128)S(1)}, f32[32,384]{1,0:T(8,128)S(1)}, f32[32,128]{1,0:T(8,128)S(1)}) custom-call(bf16[32,2176]{1,0:T(8,128)(2,1)S(1)} %shard_map.102.mine, bf16[32,2176]{1,0:T(8,128)(2,1)S(1)} %collective-permute-done.13.other, f32[32,512]{1,0:T(8,128)S(1)} %get-tuple-element.65.rhs.rhs_a, ...), custom_call_target="tpu_custom_call" | custom-call | flops 134217728 | bytes 4194304 | tf_op jit(solution)/shard_map/pallas_call | solution.py:34
  86.5 0.9 shard_map.104
  87.3 2.3 %collective-permute-start.14 = (f32[32,768]{1,0:T(8,128)S(1)}, f32[32,768]{1,0:T(8,128)S(1)}, u32[]{:S(2)}, u32[]{:S(2)}) collective-permute-start(f32[32,768]{1,0:T(8,128)S(1)} %get-tuple-element.72), channel_id=1, source_target_pairs={{0,4},{4,0},{1,5},{5,1},{2,6},{6,2},{3,7},{7,3},{8,12},{12,8},{9,1... | collective-permute-start | bytes 294920 | tf_op jit(solution)/shard_map/ppermute | solution.py:457
  89.6 0.8 shard_map.105.keep
  90.7 0.3 collective-permute-start.17
  90.9 1.2 %collective-permute-start.16 = (bf16[32,896]{1,0:T(8,128)(2,1)S(1)}, bf16[32,896]{1,0:T(8,128)(2,1)S(1)}, u32[]{:S(2)}, u32[]{:S(2)}) collective-permute-start(bf16[32,896]{1,0:T(8,128)(2,1)S(1)} %shard_map.106.wire0), channel_id=1, source_target_pairs={{0,192},{64,0},{128,64},{192,128},{1,193},{65,1},{129,65},{193,129... | collective-permute-start | bytes 172040 | tf_op jit(solution)/shard_map/ppermute | solution.py:449
  92.2 0.2 collective-permute-start.15
  92.4 2.8 %collective-permute-done.17.wire3 = bf16[32,896]{1,0:T(8,128)(2,1)S(1)} collective-permute-done((bf16[32,896]{1,0:T(8,128)(2,1)S(1)}, bf16[32,896]{1,0:T(8,128)(2,1)S(1)}, u32[]{:S(2)}, u32[]{:S(2)}) %collective-permute-start.17) | collective-permute-done | bytes 57376 | tf_op jit(solution)/shard_map/ppermute | solution.py:449
  95.2 1.4 %collective-permute-done.15.wire1 = bf16[32,896]{1,0:T(8,128)(2,1)S(1)} collective-permute-done((bf16[32,896]{1,0:T(8,128)(2,1)S(1)}, bf16[32,896]{1,0:T(8,128)(2,1)S(1)}, u32[]{:S(2)}, u32[]{:S(2)}) %collective-permute-start.15) | collective-permute-done | bytes 57376 | tf_op jit(solution)/shard_map/ppermute | solution.py:449
  96.7 0.2 shard_map.107
  96.9 13.1 %all_to_all.22.arrived = bf16[8,32,640]{2,1,0:T(8,128)(2,1)S(1)} all-to-all(bf16[8,32,640]{2,1,0:T(8,128)(2,1)S(1)} %shard_map.107), channel_id=1, replica_groups=mesh['y'=4,'z'=8,'c'=2,'x'=4] {'z'}, dimensions={0} | all-to-all | bytes 655360 | tf_op jit(solution)/shard_map/all_to_all | solution.py:469
  109.9 0.2 shard_map.108
  110.1 12.1 %all_to_all.23.arrived = f32[8,32,128]{2,1,0:T(8,128)S(1)} all-to-all(f32[8,32,128]{2,1,0:T(8,128)S(1)} %shard_map.108), channel_id=1, replica_groups=mesh['y'=4,'z'=8,'c'=2,'x'=4] {'c','x'}, dimensions={0} | all-to-all | bytes 262144 | tf_op jit(solution)/shard_map/all_to_all | solution.py:650
  122.3 0.9 shard_map.109
  (29 shorter events, 1.1 us)
Async XLA Ops:
  0.6 26.7 %copy-start = (f32[32,1024]{1,0:T(8,128)S(1)}, f32[32,1024]{1,0:T(8,128)}, u32[]{:S(2)}) copy-start(f32[32,1024]{1,0:T(8,128)} %val_weight.1) | copy-start | bytes 393220
  0.6 26.7 %copy-start.3 = (s32[1024]{0:T(1024)S(1)}, s32[1024]{0:T(1024)}, u32[]{:S(2)}) copy-start(s32[1024]{0:T(1024)} %param.10) | copy-start | bytes 12292
  0.7 26.7 %copy-start.2 = (s32[1024]{0:T(1024)S(1)}, s32[1024]{0:T(1024)}, u32[]{:S(2)}) copy-start(s32[1024]{0:T(1024)} %param.9) | copy-start | bytes 12292
  4.7 4.2 %collective-permute-start = (f32[8,128]{1,0:T(8,128)S(1)}, f32[8,128]{1,0:T(8,128)S(1)}, u32[]{:S(2)}, u32[]{:S(2)}) collective-permute-start(f32[8,128]{1,0:T(8,128)S(1)} %get-tuple-element.40), channel_id=1, source_target_pairs={{0,4},{4,0},{1,5},{5,1},{2,6},{6,2},{3,7},{7,3},{8,12},{12,8},{9,1... | collective-permute-start | bytes 12296 | tf_op jit(solution)/shard_map/ppermute | solution.py:457
  27.3 9.1 %copy-start.1 = (s32[4096]{0:T(1024)S(1)}, s32[4096]{0:T(1024)}, u32[]{:S(2)}) copy-start(s32[4096]{0:T(1024)} %param.13) | copy-start | bytes 49156
  27.3 9.1 %copy-start.4 = (f32[256]{0:T(256)S(1)}, f32[256]{0:T(256)}, u32[]{:S(2)}) copy-start(f32[256]{0:T(256)} %param.12) | copy-start | bytes 3076
  28.2 4.6 %collective-permute-start.3 = (bf16[32,3072]{1,0:T(8,128)(2,1)S(1)}, bf16[32,3072]{1,0:T(8,128)(2,1)S(1)}, u32[]{:S(2)}, u32[]{:S(2)}) collective-permute-start(bf16[32,3072]{1,0:T(8,128)(2,1)S(1)} %get-tuple-element.51), channel_id=1, source_target_pairs={{0,1},{1,0},{2,3},{3,2},{4,5},{5,4},{6,7},{7,6},{8,9},{9,8},{10,11... | collective-permute-start | bytes 589832 | tf_op jit(solution)/shard_map/ppermute | solution.py:453
  30.4 5.8 %collective-permute-start.1 = (bf16[32,3072]{1,0:T(8,128)(2,1)S(1)}, bf16[32,3072]{1,0:T(8,128)(2,1)S(1)}, u32[]{:S(2)}, u32[]{:S(2)}) collective-permute-start(bf16[32,3072]{1,0:T(8,128)(2,1)S(1)} %get-tuple-element.44), channel_id=1, source_target_pairs={{0,3},{1,2},{2,1},{3,0},{4,7},{5,6},{6,5},{7,4},{8,11},{9,10},{10,... | collective-permute-start | bytes 589832 | tf_op jit(solution)/shard_map/ppermute | solution.py:453
  33.0 7.3 %collective-permute-start.4 = (bf16[32,2560]{1,0:T(8,128)(2,1)S(1)}, bf16[32,2560]{1,0:T(8,128)(2,1)S(1)}, u32[]{:S(2)}, u32[]{:S(2)}) collective-permute-start(bf16[32,2560]{1,0:T(8,128)(2,1)S(1)} %get-tuple-element.53), channel_id=1, source_target_pairs={{0,3},{1,2},{2,1},{3,0},{4,7},{5,6},{6,5},{7,4},{8,11},{9,10},{10,... | collective-permute-start | bytes 491528 | tf_op jit(solution)/shard_map/ppermute | solution.py:453
  36.3 5.4 %collective-permute-start.2 = (bf16[32,2560]{1,0:T(8,128)(2,1)S(1)}, bf16[32,2560]{1,0:T(8,128)(2,1)S(1)}, u32[]{:S(2)}, u32[]{:S(2)}) collective-permute-start(bf16[32,2560]{1,0:T(8,128)(2,1)S(1)} %get-tuple-element.46), channel_id=1, source_target_pairs={{0,1},{1,0},{2,3},{3,2},{4,5},{5,4},{6,7},{7,6},{8,9},{9,8},{10,11... | collective-permute-start | bytes 491528 | tf_op jit(solution)/shard_map/ppermute | solution.py:453
  42.6 6.1 %collective-permute-start.5 = (f32[32,768]{1,0:T(8,128)S(1)}, f32[32,768]{1,0:T(8,128)S(1)}, u32[]{:S(2)}, u32[]{:S(2)}) collective-permute-start(f32[32,768]{1,0:T(8,128)S(1)} %get-tuple-element.58), channel_id=1, source_target_pairs={{0,4},{4,0},{1,5},{5,1},{2,6},{6,2},{3,7},{7,3},{8,12},{12,8},{9,1... | collective-permute-start | bytes 294920 | tf_op jit(solution)/shard_map/ppermute | solution.py:457
  48.7 4.6 %collective-permute-start.8 = (bf16[32,896]{1,0:T(8,128)(2,1)S(1)}, bf16[32,896]{1,0:T(8,128)(2,1)S(1)}, u32[]{:S(2)}, u32[]{:S(2)}) collective-permute-start(bf16[32,896]{1,0:T(8,128)(2,1)S(1)} %shard_map.95.wire0), channel_id=1, source_target_pairs={{0,128},{64,192},{128,0},{192,64},{1,129},{65,193},{129,1},{193,65... | collective-permute-start | bytes 172040 | tf_op jit(solution)/shard_map/ppermute | solution.py:449
  49.9 3.6 %collective-permute-start.7 = (bf16[32,896]{1,0:T(8,128)(2,1)S(1)}, bf16[32,896]{1,0:T(8,128)(2,1)S(1)}, u32[]{:S(2)}, u32[]{:S(2)}) collective-permute-start(bf16[32,896]{1,0:T(8,128)(2,1)S(1)} %shard_map.95.wire0), channel_id=1, source_target_pairs={{0,192},{64,0},{128,64},{192,128},{1,193},{65,1},{129,65},{193,129... | collective-permute-start | bytes 172040 | tf_op jit(solution)/shard_map/ppermute | solution.py:449
  51.5 4.2 %collective-permute-start.6 = (bf16[32,896]{1,0:T(8,128)(2,1)S(1)}, bf16[32,896]{1,0:T(8,128)(2,1)S(1)}, u32[]{:S(2)}, u32[]{:S(2)}) collective-permute-start(bf16[32,896]{1,0:T(8,128)(2,1)S(1)} %shard_map.95.wire0), channel_id=1, source_target_pairs={{0,64},{64,128},{128,192},{192,0},{1,65},{65,129},{129,193},{193,1... | collective-permute-start | bytes 172040 | tf_op jit(solution)/shard_map/ppermute | solution.py:449
  68.4 5.5 %collective-permute-start.9 = (bf16[32,640]{1,0:T(8,128)(2,1)S(1)}, bf16[32,640]{1,0:T(8,128)(2,1)S(1)}, u32[]{:S(2)}, u32[]{:S(2)}) collective-permute-start(bf16[32,640]{1,0:T(8,128)(2,1)S(1)} %get-tuple-element.60.weighted), channel_id=1, source_target_pairs={{0,4},{4,0},{1,5},{5,1},{2,6},{6,2},{3,7},{7,3},{8,12},{12,8},{9,1... | collective-permute-start | bytes 122888 | tf_op jit(solution)/shard_map/ppermute | solution.py:457
  74.5 5.0 %collective-permute-start.12 = (bf16[32,2176]{1,0:T(8,128)(2,1)S(1)}, bf16[32,2176]{1,0:T(8,128)(2,1)S(1)}, u32[]{:S(2)}, u32[]{:S(2)}) collective-permute-start(bf16[32,2176]{1,0:T(8,128)(2,1)S(1)} %shard_map.101.mine), channel_id=1, source_target_pairs={{0,1},{1,0},{2,3},{3,2},{4,5},{5,4},{6,7},{7,6},{8,9},{9,8},{10,11... | collective-permute-start | bytes 417800 | tf_op jit(solution)/shard_map/ppermute | solution.py:453
  75.1 6.7 %collective-permute-start.10 = (bf16[32,2048]{1,0:T(8,128)(2,1)S(1)}, bf16[32,2048]{1,0:T(8,128)(2,1)S(1)}, u32[]{:S(2)}, u32[]{:S(2)}) collective-permute-start(bf16[32,2048]{1,0:T(8,128)(2,1)S(1)} %shard_map.99.mine), channel_id=1, source_target_pairs={{0,3},{1,2},{2,1},{3,0},{4,7},{5,6},{6,5},{7,4},{8,11},{9,10},{10,... | collective-permute-start | bytes 393224 | tf_op jit(solution)/shard_map/ppermute | solution.py:453
  79.7 5.2 %collective-permute-start.13 = (bf16[32,2176]{1,0:T(8,128)(2,1)S(1)}, bf16[32,2176]{1,0:T(8,128)(2,1)S(1)}, u32[]{:S(2)}, u32[]{:S(2)}) collective-permute-start(bf16[32,2176]{1,0:T(8,128)(2,1)S(1)} %shard_map.102.mine), channel_id=1, source_target_pairs={{0,3},{1,2},{2,1},{3,0},{4,7},{5,6},{6,5},{7,4},{8,11},{9,10},{10,... | collective-permute-start | bytes 417800 | tf_op jit(solution)/shard_map/ppermute | solution.py:453
  81.9 4.6 %collective-permute-start.11 = (bf16[32,2048]{1,0:T(8,128)(2,1)S(1)}, bf16[32,2048]{1,0:T(8,128)(2,1)S(1)}, u32[]{:S(2)}, u32[]{:S(2)}) collective-permute-start(bf16[32,2048]{1,0:T(8,128)(2,1)S(1)} %shard_map.100.mine), channel_id=1, source_target_pairs={{0,1},{1,0},{2,3},{3,2},{4,5},{5,4},{6,7},{7,6},{8,9},{9,8},{10,11... | collective-permute-start | bytes 393224 | tf_op jit(solution)/shard_map/ppermute | solution.py:453
  87.3 3.3 %collective-permute-start.14 = (f32[32,768]{1,0:T(8,128)S(1)}, f32[32,768]{1,0:T(8,128)S(1)}, u32[]{:S(2)}, u32[]{:S(2)}) collective-permute-start(f32[32,768]{1,0:T(8,128)S(1)} %get-tuple-element.72), channel_id=1, source_target_pairs={{0,4},{4,0},{1,5},{5,1},{2,6},{6,2},{3,7},{7,3},{8,12},{12,8},{9,1... | collective-permute-start | bytes 294920 | tf_op jit(solution)/shard_map/ppermute | solution.py:457
  90.7 4.6 %collective-permute-start.17 = (bf16[32,896]{1,0:T(8,128)(2,1)S(1)}, bf16[32,896]{1,0:T(8,128)(2,1)S(1)}, u32[]{:S(2)}, u32[]{:S(2)}) collective-permute-start(bf16[32,896]{1,0:T(8,128)(2,1)S(1)} %shard_map.106.wire0), channel_id=1, source_target_pairs={{0,128},{64,192},{128,0},{192,64},{1,129},{65,193},{129,1},{193,65... | collective-permute-start | bytes 172040 | tf_op jit(solution)/shard_map/ppermute | solution.py:449
  90.9 4.3 %collective-permute-start.16 = (bf16[32,896]{1,0:T(8,128)(2,1)S(1)}, bf16[32,896]{1,0:T(8,128)(2,1)S(1)}, u32[]{:S(2)}, u32[]{:S(2)}) collective-permute-start(bf16[32,896]{1,0:T(8,128)(2,1)S(1)} %shard_map.106.wire0), channel_id=1, source_target_pairs={{0,192},{64,0},{128,64},{192,128},{1,193},{65,1},{129,65},{193,129... | collective-permute-start | bytes 172040 | tf_op jit(solution)/shard_map/ppermute | solution.py:449
  92.2 4.5 %collective-permute-start.15 = (bf16[32,896]{1,0:T(8,128)(2,1)S(1)}, bf16[32,896]{1,0:T(8,128)(2,1)S(1)}, u32[]{:S(2)}, u32[]{:S(2)}) collective-permute-start(bf16[32,896]{1,0:T(8,128)(2,1)S(1)} %shard_map.106.wire0), channel_id=1, source_target_pairs={{0,64},{64,128},{128,192},{192,0},{1,65},{65,129},{129,193},{193,1... | collective-permute-start | bytes 172040 | tf_op jit(solution)/shard_map/ppermute | solution.py:449

commit v6 on v5

--- a/solution.py
+++ b/solution.py
@@ -253,27 +253,31 @@
     other_half(lows, examples, before, scalars, blocks, total, place, send, rest)
 
 
-def to_wire(keep, rest, arrived, wire):
-    wire[:, :HALF] = (keep[...] + arrived[:, :HALF]).astype(BF16)
-    scalars = rest[:, :LANES] + arrived[:, HALF : HALF + LANES]
-    wire[:, HALF : HALF + LANES] = to_terms(scalars).astype(BF16)
+def to_wire(keep, rest, arrived, place, wire0, wire1, wire2, wire3):
+    tang = (keep[...] + arrived[:, :HALF]).astype(BF16)
+    scalars = to_terms(rest[:, :LANES] + arrived[:, HALF : HALF + LANES])
     high, low = terms(rest[:, LANES:] + arrived[:, HALF + LANES :], 2)
-    wire[:, HALF + LANES : HALF + 2 * LANES] = high.astype(BF16)
-    wire[:, HALF + 2 * LANES :] = low.astype(BF16)
-
-
-def along_y(wire0, wire1, wire2, wire3, place, out):
+    lanes = lane_ids()
+    for s, wire in enumerate((wire0, wire1, wire2, wire3)):
+        first = 32 * ((place[0, 0] + s) % NY)
+        at64 = pltpu.roll(high, (64 - first + LANES) % LANES, 1)
+        at96 = pltpu.roll(low, (96 - first + LANES) % LANES, 1)
+        tile = jnp.where(lanes >= 96, at96, jnp.where(lanes >= 64, at64, scalars))
+        wire[:, :HALF] = tang
+        wire[:, HALF:] = tile.astype(BF16)
+
+
+def along_y(wire0, wire1, wire2, wire3, out):
     total = wire0[...].astype(F32)
     for wire in (wire1, wire2, wire3):
         total = total + wire[...].astype(F32)
     tang = total[:, :HALF].astype(BF16)
-    tile = to_terms(from_terms(total[:, HALF : HALF + LANES]))
-    blocks = total[:, HALF + LANES : HALF + 2 * LANES] + total[:, HALF + 2 * LANES :]
-    high, rest = terms(blocks, 2)
+    tile = total[:, HALF:]
+    high, low = terms(tile + pltpu.roll(tile, LANES - 32, 1), 2)
     lanes = lane_ids()
-    at64 = pltpu.roll(high, (64 - 32 * place[0, 0] + LANES) % LANES, 1)
-    at96 = pltpu.roll(rest, (96 - 32 * place[0, 0] + LANES) % LANES, 1)
-    tile = jnp.where(lanes >= 96, at96, jnp.where(lanes >= 64, at64, tile)).astype(BF16)
+    tile = to_terms(from_terms(tile))
+    tile = jnp.where(lanes >= 64, high, tile)
+    tile = jnp.where(lanes >= 96, pltpu.roll(low, 32, 1), tile).astype(BF16)
     for i in range(NZ):
         out[i, :, :HALF] = tang
         out[i, :, HALF:] = tile
@@ -413,21 +417,25 @@
     before = pltpu.roll(kept[:, LANES:], (36 - shift + LANES) % LANES, 1)
     tile = jnp.where((lanes >= 32) & (lanes < 36), now, tile)
     tile = jnp.where((lanes >= 36) & (lanes < 40), before, tile)
-    for i in range(NC * NX):
-        out[i] = tile
+    out[...] = tile
+
+
+def join(tile, near, core, across, out):
+    lanes = lane_ids()
+    shared = (lanes == 3) | (lanes == 4)
+    total = tile[...] + near[...]
+    out[...] = total + jnp.where(shared, core[...] + across[...], 0.0)
 
 
 def finish(
-    arrived, kept, rhs_a, rhs_b, resid_a, resid_b, strengths, place, solve, hyper
+    tile, far, kept, rhs_a, rhs_b, resid_a, resid_b, strengths, place, solve, hyper
 ):
     core, x = place[0, 2], place[0, 3]
-    mine = sum(arrived[core * NX + i] for i in range(NX))
-    rest = sum(arrived[(1 - core) * NX + i] for i in range(NX))
-    every = mine + rest
-    tile = kept[...]
-    norm, scaled_first, curv_first, alpha = (column(tile, i) for i in range(4))
+    mine = tile[...] + far[...]
+    first_step = kept[...]
+    norm, scaled_first, curv_first, alpha = (column(first_step, i) for i in range(4))
     norm_next, scaled, mixed = (column(mine, i) for i in range(3))
-    both, cross = column(every, 3), column(every, 4)
+    both, cross = column(mine, 3), column(mine, 4)
     beta = norm_next / norm
     curv = (both + 2.0 * beta * cross + beta * beta * curv_first) / F32(TOTAL)
     curv = curv + (scaled + 2.0 * beta * mixed + beta * beta * scaled_first)
@@ -453,6 +461,11 @@
     return lax.ppermute(array, "x", [(i, partner(i, which, stage)) for i in range(NX)])
 
 
+def moved(array, core, flip):
+    pairs = [(c * NX + x, (c ^ core) * NX + (x ^ flip)) for c in range(NC) for x in range(NX)]
+    return lax.ppermute(array, ("c", "x"), pairs)
+
+
 def swapped(array):
     return lax.ppermute(array, "c", [(0, 1), (1, 0)])
 
@@ -460,12 +473,11 @@
 def summed(pieces, examples, before, send, rest, place, flops):
     arrived = swapped(send)
     keep = call(own_half, shape(R, HALF), pieces, examples, before, place, flops=flops)
-    wire = call(to_wire, shape(R, HALF + 3 * LANES, dtype=BF16), keep, rest, arrived)
-    far = shift(wire, "y", NY, 2)
-    near = [shift(wire, "y", NY, by) for by in (1, NY - 1)]
-    out = call(
-        along_y, shape(NZ, R, HALF + LANES, dtype=BF16), wire, *near, far, place
-    )
+    line = shape(R, HALF + LANES, dtype=BF16)
+    wires = call(to_wire, [line] * NY, keep, rest, arrived, place)
+    near = [shift(wires[by], "y", NY, by) for by in (1, NY - 1)]
+    far = shift(wires[2], "y", NY, 2)
+    out = call(along_y, shape(NZ, R, HALF + LANES, dtype=BF16), wires[0], *near, far)
     return lax.all_to_all(out, "z", 0, 0, tiled=True)
 
 
@@ -638,20 +650,23 @@
         flops=work,
     )
     arrived = summed(pieces, examples, tang, send, rest, place, work // 2)
-    out = call(
+    tile = call(
         curvature,
-        shape(NC * NX, R, LANES),
+        shape(R, LANES),
         arrived,
         curvew,
         tang_first,
         kept_first,
         place,
     )
-    arrived = lax.all_to_all(out, ("c", "x"), 0, 0, tiled=True)
+    others = [moved(tile, core, flip) for core, flip in ((0, 1), (1, 0), (1, 1))]
+    tile = call(join, shape(R, LANES), tile, *others)
+    far = moved(tile, 0, 3)
     solve, hyper = call(
         finish,
         [shape(R, OWN), shape(1, R)],
-        arrived,
+        tile,
+        far,
         kept,
         rhs_a,
         rhs_b,

time: 123 us -> 123 us (level)
  blocking collectives: 55.9 us -> 43.4 us
  starting transfers between devices: 30 us -> 38.5 us
  waiting for transfers between devices: 19.2 us -> 22.6 us
    all_to_all x1 -> x0, blocking collectives: 12.1 us -> none  [shards(): arrived = lax.all_to_all(out, ('c', 'x'), 0, 0, tiled=True)]
    ppermute x0 -> x4, starting transfers between devices: none -> 7.42 us  [moved(): return lax.ppermute(array, ('c', 'x'), pairs)]
    ppermute x0 -> x4, waiting for transfers between devices: none -> 3.14 us  [moved(): return lax.ppermute(array, ('c', 'x'), pairs)]
    pallas_call x24 -> x25, Pallas kernels: 17.1 us -> 17.2 us  [call(): pl.pallas_call(body, out_shape=outs, in_specs=specs, out_specs=jax.tree.m...]
  transfers between devices with their start and end apart: 18 -> 22, of which waited for: 13 -> 14; matrix products, arithmetic and copies ran while one was open for 0% -> 0% of each run, Pallas kernels for 7% -> 7%
where the time goes in v6:
time: 123 us
  blocking collectives  43.4 us (35%)
  starting transfers between devices  38.5 us (31%)
  waiting for transfers between devices  22.6 us (18%)
  Pallas kernels  17.2 us (14%)
    all_to_all x2, blocking collectives, summed(): return lax.all_to_all(out, 'z', 0, 0, tiled=True)  25 us
    all_to_all x1, blocking collectives, shards(): lax.all_to_all(jnp.broadcast_to(margin[None], (NY * NZ, 8, 128)), ('y', '...  18.4 us
    pallas_call x25, Pallas kernels, call(): pl.pallas_call(body, out_shape=outs, in_specs=specs, out_specs=jax.tree.m...  17.2 us
    ppermute x4, starting transfers between devices, swapped(): return lax.ppermute(array, 'c', [(0, 1), (1, 0)])  15.4 us
    ppermute x8, starting transfers between devices, traded(): lax.ppermute(array, 'x', [(i, partner(i, which, stage)) for i in range(NX)])  10.2 us
    ppermute x8, waiting for transfers between devices, traded(): lax.ppermute(array, 'x', [(i, partner(i, which, stage)) for i in range(NX)])  9.65 us
    ppermute x6, waiting for transfers between devices, shift(): lax.ppermute(array, axis, [(i, (i + by) % length) for i in range(length)])  8.71 us
    ppermute x4, starting transfers between devices, moved(): return lax.ppermute(array, ('c', 'x'), pairs)  7.42 us
  transfers between devices with their start and end apart: 22, of which 14 were waited for; matrix products, arithmetic and copies ran while one was open for 0% of the time, Pallas kernels for 7%

profile of v6, /device:TPU:1, one launch (start us, length us, event | category | flops | bytes accessed | tf_op | source)
XLA Modules:
  0.0 122.6 jit_solution(12973141788069255497)
XLA Ops:
  0.7 4.0 %shard_map.86 = (f32[8,128]{1,0:T(8,128)S(1)}, bf16[1024,4096]{1,0:T(8,128)(2,1)S(1)}, f32[1,4096]{1,0:T(1,128)S(1)}) custom-call(bf16[1024,4096]{1,0:T(8,128)(2,1)} %source.1, bf16[32,128]{1,0:T(8,128)(2,1)} %bitcast.17, s32[1,4]{1,0:T(1,128)S(1)} %add_bitcast_fusion.place), custom_call_target="tpu_custom_call" | custom-call | bytes 4194304 | tf_op jit(solution)/shard_map/pallas_call | solution.py:34
  4.7 3.3 %collective-permute-start = (f32[8,128]{1,0:T(8,128)S(1)}, f32[8,128]{1,0:T(8,128)S(1)}, u32[]{:S(2)}, u32[]{:S(2)}) collective-permute-start(f32[8,128]{1,0:T(8,128)S(1)} %get-tuple-element.48), channel_id=1, source_target_pairs={{0,4},{4,0},{1,5},{5,1},{2,6},{6,2},{3,7},{7,3},{8,12},{12,8},{9,1... | collective-permute-start | bytes 12296 | tf_op jit(solution)/shard_map/ppermute | solution.py:470
  8.0 0.8 collective-permute-done
  8.9 18.4 %all_to_all.15.margin_parts = f32[32,8,128]{2,1,0:T(8,128)S(1)} all-to-all(f32[32,8,128]{2,1,0:T(8,128)S(1)} %broadcast_in_dim.2), channel_id=1, replica_groups=mesh['y'=4,'z'=8,'c'=2,'x'=4] {'y','z'}, dimensions={0} | all-to-all | bytes 262144 | tf_op jit(solution)/shard_map/all_to_all | solution.py:498
  27.3 0.9 shard_map.87
  28.2 1.3 %collective-permute-start.3 = (bf16[32,3072]{1,0:T(8,128)(2,1)S(1)}, bf16[32,3072]{1,0:T(8,128)(2,1)S(1)}, u32[]{:S(2)}, u32[]{:S(2)}) collective-permute-start(bf16[32,3072]{1,0:T(8,128)(2,1)S(1)} %get-tuple-element.59), channel_id=1, source_target_pairs={{0,1},{1,0},{2,3},{3,2},{4,5},{5,4},{6,7},{7,6},{8,9},{9,8},{10,11... | collective-permute-start | bytes 589832 | tf_op jit(solution)/shard_map/ppermute | solution.py:461
  29.5 0.8 shard_map.88
  30.4 1.9 %collective-permute-start.1 = (bf16[32,3072]{1,0:T(8,128)(2,1)S(1)}, bf16[32,3072]{1,0:T(8,128)(2,1)S(1)}, u32[]{:S(2)}, u32[]{:S(2)}) collective-permute-start(bf16[32,3072]{1,0:T(8,128)(2,1)S(1)} %get-tuple-element.52), channel_id=1, source_target_pairs={{0,3},{1,2},{2,1},{3,0},{4,7},{5,6},{6,5},{7,4},{8,11},{9,10},{10,... | collective-permute-start | bytes 589832 | tf_op jit(solution)/shard_map/ppermute | solution.py:461
  32.3 0.5 collective-permute-done.3.arrived
  33.0 2.6 %collective-permute-start.4 = (bf16[32,2560]{1,0:T(8,128)(2,1)S(1)}, bf16[32,2560]{1,0:T(8,128)(2,1)S(1)}, u32[]{:S(2)}, u32[]{:S(2)}) collective-permute-start(bf16[32,2560]{1,0:T(8,128)(2,1)S(1)} %get-tuple-element.61), channel_id=1, source_target_pairs={{0,3},{1,2},{2,1},{3,0},{4,7},{5,6},{6,5},{7,4},{8,11},{9,10},{10,... | collective-permute-start | bytes 491528 | tf_op jit(solution)/shard_map/ppermute | solution.py:461
  35.5 0.7 collective-permute-done.1.arrived
  36.5 0.6 shard_map.90
  37.1 3.2 %collective-permute-done.4.wire = bf16[32,2560]{1,0:T(8,128)(2,1)S(1)} collective-permute-done((bf16[32,2560]{1,0:T(8,128)(2,1)S(1)}, bf16[32,2560]{1,0:T(8,128)(2,1)S(1)}, u32[]{:S(2)}, u32[]{:S(2)}) %collective-permute-start.4) | collective-permute-done | bytes 163872 | tf_op jit(solution)/shard_map/ppermute | solution.py:461
  40.2 1.4 %shard_map.92 = (f32[32,512]{1,0:T(8,128)S(1)}, bf16[32,2048]{1,0:T(8,128)(2,1)S(1)}, f32[32,1024]{1,0:T(8,128)S(1)}, f32[32,384]{1,0:T(8,128)S(1)}) custom-call(f32[32,2048]{1,0:T(8,128)S(1)} %get-tuple-element.60.part, bf16[32,2560]{1,0:T(8,128)(2,1)S(1)} %collective-permute-done.4.wire, bf16[1024,4096]{1,0:T(8,128)(2,1)S(1)} %get-tuple-element.49.examples, ...), custom_call_target="tpu_custom_call" | custom-call | flops 134217728 | bytes 4194304 | tf_op jit(solution)/shard_map/pallas_call | solution.py:34
  41.7 0.8 shard_map.93
  42.6 5.1 %collective-permute-start.5 = (f32[32,768]{1,0:T(8,128)S(1)}, f32[32,768]{1,0:T(8,128)S(1)}, u32[]{:S(2)}, u32[]{:S(2)}) collective-permute-start(f32[32,768]{1,0:T(8,128)S(1)} %get-tuple-element.66), channel_id=1, source_target_pairs={{0,4},{4,0},{1,5},{5,1},{2,6},{6,2},{3,7},{7,3},{8,12},{12,8},{9,1... | collective-permute-start | bytes 294920 | tf_op jit(solution)/shard_map/ppermute | solution.py:470
  47.7 0.8 shard_map.94.keep
  48.8 0.4 collective-permute-start.6
  49.2 2.4 %collective-permute-start.7 = (bf16[32,640]{1,0:T(8,128)(2,1)S(1)}, bf16[32,640]{1,0:T(8,128)(2,1)S(1)}, u32[]{:S(2)}, u32[]{:S(2)}) collective-permute-start(bf16[32,640]{1,0:T(8,128)(2,1)S(1)} %get-tuple-element.69), channel_id=1, source_target_pairs={{0,192},{64,0},{128,64},{192,128},{1,193},{65,1},{129,65},{193,129... | collective-permute-start | bytes 122888 | tf_op jit(solution)/shard_map/ppermute | solution.py:457
  51.5 1.4 %collective-permute-done.6.wire1 = bf16[32,640]{1,0:T(8,128)(2,1)S(1)} collective-permute-done((bf16[32,640]{1,0:T(8,128)(2,1)S(1)}, bf16[32,640]{1,0:T(8,128)(2,1)S(1)}, u32[]{:S(2)}, u32[]{:S(2)}) %collective-permute-start.6) | collective-permute-done | bytes 40992 | tf_op jit(solution)/shard_map/ppermute | solution.py:457
  52.9 3.0 %collective-permute-done.8.wire3 = bf16[32,640]{1,0:T(8,128)(2,1)S(1)} collective-permute-done((bf16[32,640]{1,0:T(8,128)(2,1)S(1)}, bf16[32,640]{1,0:T(8,128)(2,1)S(1)}, u32[]{:S(2)}, u32[]{:S(2)}) %collective-permute-start.8) | collective-permute-done | bytes 40992 | tf_op jit(solution)/shard_map/ppermute | solution.py:457
  55.9 0.2 shard_map.96
  56.1 12.2 %all_to_all.16.arrived = bf16[8,32,640]{2,1,0:T(8,128)(2,1)S(1)} all-to-all(bf16[8,32,640]{2,1,0:T(8,128)(2,1)S(1)} %shard_map.96), channel_id=1, replica_groups=mesh['y'=4,'z'=8,'c'=2,'x'=4] {'z'}, dimensions={0} | all-to-all | bytes 655360 | tf_op jit(solution)/shard_map/all_to_all | solution.py:481
  68.3 0.3 shard_map.97
  68.6 4.6 %collective-permute-start.9 = (bf16[32,640]{1,0:T(8,128)(2,1)S(1)}, bf16[32,640]{1,0:T(8,128)(2,1)S(1)}, u32[]{:S(2)}, u32[]{:S(2)}) collective-permute-start(bf16[32,640]{1,0:T(8,128)(2,1)S(1)} %get-tuple-element.72.weighted), channel_id=1, source_target_pairs={{0,4},{4,0},{1,5},{5,1},{2,6},{6,2},{3,7},{7,3},{8,12},{12,8},{9,1... | collective-permute-start | bytes 122888 | tf_op jit(solution)/shard_map/ppermute | solution.py:470
  73.2 0.9 shard_map.98
  74.1 0.6 shard_map.101.mine
  74.7 0.6 shard_map.99.mine
  75.3 2.1 %collective-permute-start.10 = (bf16[32,2048]{1,0:T(8,128)(2,1)S(1)}, bf16[32,2048]{1,0:T(8,128)(2,1)S(1)}, u32[]{:S(2)}, u32[]{:S(2)}) collective-permute-start(bf16[32,2048]{1,0:T(8,128)(2,1)S(1)} %shard_map.99.mine), channel_id=1, source_target_pairs={{0,3},{1,2},{2,1},{3,0},{4,7},{5,6},{6,5},{7,4},{8,11},{9,10},{10,... | collective-permute-start | bytes 393224 | tf_op jit(solution)/shard_map/ppermute | solution.py:461
  77.4 2.3 %collective-permute-done.12.other = bf16[32,2176]{1,0:T(8,128)(2,1)S(1)} collective-permute-done((bf16[32,2176]{1,0:T(8,128)(2,1)S(1)}, bf16[32,2176]{1,0:T(8,128)(2,1)S(1)}, u32[]{:S(2)}, u32[]{:S(2)}) %collective-permute-start.12) | collective-permute-done | bytes 139296 | tf_op jit(solution)/shard_map/ppermute | solution.py:461
  79.9 2.1 %collective-permute-start.13 = (bf16[32,2176]{1,0:T(8,128)(2,1)S(1)}, bf16[32,2176]{1,0:T(8,128)(2,1)S(1)}, u32[]{:S(2)}, u32[]{:S(2)}) collective-permute-start(bf16[32,2176]{1,0:T(8,128)(2,1)S(1)} %shard_map.102.mine), channel_id=1, source_target_pairs={{0,3},{1,2},{2,1},{3,0},{4,7},{5,6},{6,5},{7,4},{8,11},{9,10},{10,... | collective-permute-start | bytes 417800 | tf_op jit(solution)/shard_map/ppermute | solution.py:461
  82.1 2.9 %collective-permute-done.13.other = bf16[32,2176]{1,0:T(8,128)(2,1)S(1)} collective-permute-done((bf16[32,2176]{1,0:T(8,128)(2,1)S(1)}, bf16[32,2176]{1,0:T(8,128)(2,1)S(1)}, u32[]{:S(2)}, u32[]{:S(2)}) %collective-permute-start.13) | collective-permute-done | bytes 139296 | tf_op jit(solution)/shard_map/ppermute | solution.py:461
  85.0 1.6 %shard_map.103 = (f32[32,512]{1,0:T(8,128)S(1)}, f32[32,1024]{1,0:T(8,128)S(1)}, f32[32,384]{1,0:T(8,128)S(1)}, f32[32,128]{1,0:T(8,128)S(1)}) custom-call(bf16[32,2176]{1,0:T(8,128)(2,1)S(1)} %shard_map.102.mine, bf16[32,2176]{1,0:T(8,128)(2,1)S(1)} %collective-permute-done.13.other, f32[32,512]{1,0:T(8,128)S(1)} %get-tuple-element.77.rhs.rhs_a, ...), custom_call_target="tpu_custom_call" | custom-call | flops 134217728 | bytes 4194304 | tf_op jit(solution)/shard_map/pallas_call | solution.py:34
  86.6 0.9 shard_map.104
  87.5 2.3 %collective-permute-start.14 = (f32[32,768]{1,0:T(8,128)S(1)}, f32[32,768]{1,0:T(8,128)S(1)}, u32[]{:S(2)}, u32[]{:S(2)}) collective-permute-start(f32[32,768]{1,0:T(8,128)S(1)} %get-tuple-element.84), channel_id=1, source_target_pairs={{0,4},{4,0},{1,5},{5,1},{2,6},{6,2},{3,7},{7,3},{8,12},{12,8},{9,1... | collective-permute-start | bytes 294920 | tf_op jit(solution)/shard_map/ppermute | solution.py:470
  89.8 0.8 shard_map.105.keep
  91.0 2.7 %collective-permute-start.16 = (bf16[32,640]{1,0:T(8,128)(2,1)S(1)}, bf16[32,640]{1,0:T(8,128)(2,1)S(1)}, u32[]{:S(2)}, u32[]{:S(2)}) collective-permute-start(bf16[32,640]{1,0:T(8,128)(2,1)S(1)} %get-tuple-element.87), channel_id=1, source_target_pairs={{0,192},{64,0},{128,64},{192,128},{1,193},{65,1},{129,65},{193,129... | collective-permute-start | bytes 122888 | tf_op jit(solution)/shard_map/ppermute | solution.py:457
  93.7 1.4 %collective-permute-done.15.wire1 = bf16[32,640]{1,0:T(8,128)(2,1)S(1)} collective-permute-done((bf16[32,640]{1,0:T(8,128)(2,1)S(1)}, bf16[32,640]{1,0:T(8,128)(2,1)S(1)}, u32[]{:S(2)}, u32[]{:S(2)}) %collective-permute-start.15) | collective-permute-done | bytes 40992 | tf_op jit(solution)/shard_map/ppermute | solution.py:457
  95.0 3.0 %collective-permute-done.17.wire3 = bf16[32,640]{1,0:T(8,128)(2,1)S(1)} collective-permute-done((bf16[32,640]{1,0:T(8,128)(2,1)S(1)}, bf16[32,640]{1,0:T(8,128)(2,1)S(1)}, u32[]{:S(2)}, u32[]{:S(2)}) %collective-permute-start.17) | collective-permute-done | bytes 40992 | tf_op jit(solution)/shard_map/ppermute | solution.py:457
  98.2 12.8 %all_to_all.17.arrived = bf16[8,32,640]{2,1,0:T(8,128)(2,1)S(1)} all-to-all(bf16[8,32,640]{2,1,0:T(8,128)(2,1)S(1)} %shard_map.107), channel_id=1, replica_groups=mesh['y'=4,'z'=8,'c'=2,'x'=4] {'z'}, dimensions={0} | all-to-all | bytes 655360 | tf_op jit(solution)/shard_map/all_to_all | solution.py:481
  111.0 0.2 shard_map.108.tile
  111.2 3.1 %collective-permute-start.20 = (f32[32,128]{1,0:T(8,128)S(1)}, f32[32,128]{1,0:T(8,128)S(1)}, u32[]{:S(2)}, u32[]{:S(2)}) collective-permute-start(f32[32,128]{1,0:T(8,128)S(1)} %shard_map.108.tile), channel_id=1, source_target_pairs={{0,5},{1,4},{2,7},{3,6},{4,1},{5,0},{6,3},{7,2},{8,13},{9,12},{10,... | collective-permute-start | bytes 49160 | tf_op jit(solution)/shard_map/ppermute | solution.py:466
  114.3 0.9 collective-permute-start.19
  115.2 1.3 %collective-permute-start.18 = (f32[32,128]{1,0:T(8,128)S(1)}, f32[32,128]{1,0:T(8,128)S(1)}, u32[]{:S(2)}, u32[]{:S(2)}) collective-permute-start(f32[32,128]{1,0:T(8,128)S(1)} %shard_map.108.tile), channel_id=1, source_target_pairs={{0,1},{1,0},{2,3},{3,2},{4,5},{5,4},{6,7},{7,6},{8,9},{9,8},{10,11... | collective-permute-start | bytes 49160 | tf_op jit(solution)/shard_map/ppermute | solution.py:466
  116.5 1.4 %collective-permute-done.18.near = f32[32,128]{1,0:T(8,128)S(1)} collective-permute-done((f32[32,128]{1,0:T(8,128)S(1)}, f32[32,128]{1,0:T(8,128)S(1)}, u32[]{:S(2)}, u32[]{:S(2)}) %collective-permute-start.18) | collective-permute-done | bytes 16416 | tf_op jit(solution)/shard_map/ppermute | solution.py:466
  117.9 2.2 %collective-permute-start.21 = (f32[32,128]{1,0:T(8,128)S(1)}, f32[32,128]{1,0:T(8,128)S(1)}, u32[]{:S(2)}, u32[]{:S(2)}) collective-permute-start(f32[32,128]{1,0:T(8,128)S(1)} %shard_map.109.tile), channel_id=1, source_target_pairs={{0,3},{1,2},{2,1},{3,0},{4,7},{5,6},{6,5},{7,4},{8,11},{9,10},{10,... | collective-permute-start | bytes 49160 | tf_op jit(solution)/shard_map/ppermute | solution.py:466
  120.0 1.7 %collective-permute-done.21.far = f32[32,128]{1,0:T(8,128)S(1)} collective-permute-done((f32[32,128]{1,0:T(8,128)S(1)}, f32[32,128]{1,0:T(8,128)S(1)}, u32[]{:S(2)}, u32[]{:S(2)}) %collective-permute-start.21) | collective-permute-done | bytes 16416 | tf_op jit(solution)/shard_map/ppermute | solution.py:466
  121.8 0.9 shard_map.110
  (37 shorter events, 1.6 us)
Async XLA Ops:
  0.6 26.7 %copy-start = (f32[32,1024]{1,0:T(8,128)S(1)}, f32[32,1024]{1,0:T(8,128)}, u32[]{:S(2)}) copy-start(f32[32,1024]{1,0:T(8,128)} %val_weight.1) | copy-start | bytes 393220
  0.6 26.7 %copy-start.3 = (s32[1024]{0:T(1024)S(1)}, s32[1024]{0:T(1024)}, u32[]{:S(2)}) copy-start(s32[1024]{0:T(1024)} %param.10) | copy-start | bytes 12292
  0.7 26.7 %copy-start.2 = (s32[1024]{0:T(1024)S(1)}, s32[1024]{0:T(1024)}, u32[]{:S(2)}) copy-start(s32[1024]{0:T(1024)} %param.9) | copy-start | bytes 12292
  4.7 4.2 %collective-permute-start = (f32[8,128]{1,0:T(8,128)S(1)}, f32[8,128]{1,0:T(8,128)S(1)}, u32[]{:S(2)}, u32[]{:S(2)}) collective-permute-start(f32[8,128]{1,0:T(8,128)S(1)} %get-tuple-element.48), channel_id=1, source_target_pairs={{0,4},{4,0},{1,5},{5,1},{2,6},{6,2},{3,7},{7,3},{8,12},{12,8},{9,1... | collective-permute-start | bytes 12296 | tf_op jit(solution)/shard_map/ppermute | solution.py:470
  27.3 9.1 %copy-start.1 = (s32[4096]{0:T(1024)S(1)}, s32[4096]{0:T(1024)}, u32[]{:S(2)}) copy-start(s32[4096]{0:T(1024)} %param.13) | copy-start | bytes 49156
  27.3 9.1 %copy-start.4 = (f32[256]{0:T(256)S(1)}, f32[256]{0:T(256)}, u32[]{:S(2)}) copy-start(f32[256]{0:T(256)} %param.12) | copy-start | bytes 3076
  28.2 4.6 %collective-permute-start.3 = (bf16[32,3072]{1,0:T(8,128)(2,1)S(1)}, bf16[32,3072]{1,0:T(8,128)(2,1)S(1)}, u32[]{:S(2)}, u32[]{:S(2)}) collective-permute-start(bf16[32,3072]{1,0:T(8,128)(2,1)S(1)} %get-tuple-element.59), channel_id=1, source_target_pairs={{0,1},{1,0},{2,3},{3,2},{4,5},{5,4},{6,7},{7,6},{8,9},{9,8},{10,11... | collective-permute-start | bytes 589832 | tf_op jit(solution)/shard_map/ppermute | solution.py:461
  30.4 5.8 %collective-permute-start.1 = (bf16[32,3072]{1,0:T(8,128)(2,1)S(1)}, bf16[32,3072]{1,0:T(8,128)(2,1)S(1)}, u32[]{:S(2)}, u32[]{:S(2)}) collective-permute-start(bf16[32,3072]{1,0:T(8,128)(2,1)S(1)} %get-tuple-element.52), channel_id=1, source_target_pairs={{0,3},{1,2},{2,1},{3,0},{4,7},{5,6},{6,5},{7,4},{8,11},{9,10},{10,... | collective-permute-start | bytes 589832 | tf_op jit(solution)/shard_map/ppermute | solution.py:461
  33.0 7.3 %collective-permute-start.4 = (bf16[32,2560]{1,0:T(8,128)(2,1)S(1)}, bf16[32,2560]{1,0:T(8,128)(2,1)S(1)}, u32[]{:S(2)}, u32[]{:S(2)}) collective-permute-start(bf16[32,2560]{1,0:T(8,128)(2,1)S(1)} %get-tuple-element.61), channel_id=1, source_target_pairs={{0,3},{1,2},{2,1},{3,0},{4,7},{5,6},{6,5},{7,4},{8,11},{9,10},{10,... | collective-permute-start | bytes 491528 | tf_op jit(solution)/shard_map/ppermute | solution.py:461
  36.3 5.4 %collective-permute-start.2 = (bf16[32,2560]{1,0:T(8,128)(2,1)S(1)}, bf16[32,2560]{1,0:T(8,128)(2,1)S(1)}, u32[]{:S(2)}, u32[]{:S(2)}) collective-permute-start(bf16[32,2560]{1,0:T(8,128)(2,1)S(1)} %get-tuple-element.54), channel_id=1, source_target_pairs={{0,1},{1,0},{2,3},{3,2},{4,5},{5,4},{6,7},{7,6},{8,9},{9,8},{10,11... | collective-permute-start | bytes 491528 | tf_op jit(solution)/shard_map/ppermute | solution.py:461
  42.6 6.1 %collective-permute-start.5 = (f32[32,768]{1,0:T(8,128)S(1)}, f32[32,768]{1,0:T(8,128)S(1)}, u32[]{:S(2)}, u32[]{:S(2)}) collective-permute-start(f32[32,768]{1,0:T(8,128)S(1)} %get-tuple-element.66), channel_id=1, source_target_pairs={{0,4},{4,0},{1,5},{5,1},{2,6},{6,2},{3,7},{7,3},{8,12},{12,8},{9,1... | collective-permute-start | bytes 294920 | tf_op jit(solution)/shard_map/ppermute | solution.py:470
  48.8 4.1 %collective-permute-start.6 = (bf16[32,640]{1,0:T(8,128)(2,1)S(1)}, bf16[32,640]{1,0:T(8,128)(2,1)S(1)}, u32[]{:S(2)}, u32[]{:S(2)}) collective-permute-start(bf16[32,640]{1,0:T(8,128)(2,1)S(1)} %get-tuple-element.68), channel_id=1, source_target_pairs={{0,64},{64,128},{128,192},{192,0},{1,65},{65,129},{129,193},{193,1... | collective-permute-start | bytes 122888 | tf_op jit(solution)/shard_map/ppermute | solution.py:457
  49.2 3.7 %collective-permute-start.7 = (bf16[32,640]{1,0:T(8,128)(2,1)S(1)}, bf16[32,640]{1,0:T(8,128)(2,1)S(1)}, u32[]{:S(2)}, u32[]{:S(2)}) collective-permute-start(bf16[32,640]{1,0:T(8,128)(2,1)S(1)} %get-tuple-element.69), channel_id=1, source_target_pairs={{0,192},{64,0},{128,64},{192,128},{1,193},{65,1},{129,65},{193,129... | collective-permute-start | bytes 122888 | tf_op jit(solution)/shard_map/ppermute | solution.py:457
  51.5 4.4 %collective-permute-start.8 = (bf16[32,640]{1,0:T(8,128)(2,1)S(1)}, bf16[32,640]{1,0:T(8,128)(2,1)S(1)}, u32[]{:S(2)}, u32[]{:S(2)}) collective-permute-start(bf16[32,640]{1,0:T(8,128)(2,1)S(1)} %get-tuple-element.70), channel_id=1, source_target_pairs={{0,128},{64,192},{128,0},{192,64},{1,129},{65,193},{129,1},{193,65... | collective-permute-start | bytes 122888 | tf_op jit(solution)/shard_map/ppermute | solution.py:457
  68.6 5.5 %collective-permute-start.9 = (bf16[32,640]{1,0:T(8,128)(2,1)S(1)}, bf16[32,640]{1,0:T(8,128)(2,1)S(1)}, u32[]{:S(2)}, u32[]{:S(2)}) collective-permute-start(bf16[32,640]{1,0:T(8,128)(2,1)S(1)} %get-tuple-element.72.weighted), channel_id=1, source_target_pairs={{0,4},{4,0},{1,5},{5,1},{2,6},{6,2},{3,7},{7,3},{8,12},{12,8},{9,1... | collective-permute-start | bytes 122888 | tf_op jit(solution)/shard_map/ppermute | solution.py:470
  74.7 5.0 %collective-permute-start.12 = (bf16[32,2176]{1,0:T(8,128)(2,1)S(1)}, bf16[32,2176]{1,0:T(8,128)(2,1)S(1)}, u32[]{:S(2)}, u32[]{:S(2)}) collective-permute-start(bf16[32,2176]{1,0:T(8,128)(2,1)S(1)} %shard_map.101.mine), channel_id=1, source_target_pairs={{0,1},{1,0},{2,3},{3,2},{4,5},{5,4},{6,7},{7,6},{8,9},{9,8},{10,11... | collective-permute-start | bytes 417800 | tf_op jit(solution)/shard_map/ppermute | solution.py:461
  75.3 6.7 %collective-permute-start.10 = (bf16[32,2048]{1,0:T(8,128)(2,1)S(1)}, bf16[32,2048]{1,0:T(8,128)(2,1)S(1)}, u32[]{:S(2)}, u32[]{:S(2)}) collective-permute-start(bf16[32,2048]{1,0:T(8,128)(2,1)S(1)} %shard_map.99.mine), channel_id=1, source_target_pairs={{0,3},{1,2},{2,1},{3,0},{4,7},{5,6},{6,5},{7,4},{8,11},{9,10},{10,... | collective-permute-start | bytes 393224 | tf_op jit(solution)/shard_map/ppermute | solution.py:461
  79.9 5.2 %collective-permute-start.13 = (bf16[32,2176]{1,0:T(8,128)(2,1)S(1)}, bf16[32,2176]{1,0:T(8,128)(2,1)S(1)}, u32[]{:S(2)}, u32[]{:S(2)}) collective-permute-start(bf16[32,2176]{1,0:T(8,128)(2,1)S(1)} %shard_map.102.mine), channel_id=1, source_target_pairs={{0,3},{1,2},{2,1},{3,0},{4,7},{5,6},{6,5},{7,4},{8,11},{9,10},{10,... | collective-permute-start | bytes 417800 | tf_op jit(solution)/shard_map/ppermute | solution.py:461
  82.0 4.6 %collective-permute-start.11 = (bf16[32,2048]{1,0:T(8,128)(2,1)S(1)}, bf16[32,2048]{1,0:T(8,128)(2,1)S(1)}, u32[]{:S(2)}, u32[]{:S(2)}) collective-permute-start(bf16[32,2048]{1,0:T(8,128)(2,1)S(1)} %shard_map.100.mine), channel_id=1, source_target_pairs={{0,1},{1,0},{2,3},{3,2},{4,5},{5,4},{6,7},{7,6},{8,9},{9,8},{10,11... | collective-permute-start | bytes 393224 | tf_op jit(solution)/shard_map/ppermute | solution.py:461
  87.5 3.3 %collective-permute-start.14 = (f32[32,768]{1,0:T(8,128)S(1)}, f32[32,768]{1,0:T(8,128)S(1)}, u32[]{:S(2)}, u32[]{:S(2)}) collective-permute-start(f32[32,768]{1,0:T(8,128)S(1)} %get-tuple-element.84), channel_id=1, source_target_pairs={{0,4},{4,0},{1,5},{5,1},{2,6},{6,2},{3,7},{7,3},{8,12},{12,8},{9,1... | collective-permute-start | bytes 294920 | tf_op jit(solution)/shard_map/ppermute | solution.py:470
  90.9 4.1 %collective-permute-start.15 = (bf16[32,640]{1,0:T(8,128)(2,1)S(1)}, bf16[32,640]{1,0:T(8,128)(2,1)S(1)}, u32[]{:S(2)}, u32[]{:S(2)}) collective-permute-start(bf16[32,640]{1,0:T(8,128)(2,1)S(1)} %get-tuple-element.86), channel_id=1, source_target_pairs={{0,64},{64,128},{128,192},{192,0},{1,65},{65,129},{129,193},{193,1... | collective-permute-start | bytes 122888 | tf_op jit(solution)/shard_map/ppermute | solution.py:457
  91.0 4.1 %collective-permute-start.16 = (bf16[32,640]{1,0:T(8,128)(2,1)S(1)}, bf16[32,640]{1,0:T(8,128)(2,1)S(1)}, u32[]{:S(2)}, u32[]{:S(2)}) collective-permute-start(bf16[32,640]{1,0:T(8,128)(2,1)S(1)} %get-tuple-element.87), channel_id=1, source_target_pairs={{0,192},{64,0},{128,64},{192,128},{1,193},{65,1},{129,65},{193,129... | collective-permute-start | bytes 122888 | tf_op jit(solution)/shard_map/ppermute | solution.py:457
  93.6 4.4 %collective-permute-start.17 = (bf16[32,640]{1,0:T(8,128)(2,1)S(1)}, bf16[32,640]{1,0:T(8,128)(2,1)S(1)}, u32[]{:S(2)}, u32[]{:S(2)}) collective-permute-start(bf16[32,640]{1,0:T(8,128)(2,1)S(1)} %get-tuple-element.88), channel_id=1, source_target_pairs={{0,128},{64,192},{128,0},{192,64},{1,129},{65,193},{129,1},{193,65... | collective-permute-start | bytes 122888 | tf_op jit(solution)/shard_map/ppermute | solution.py:457
  111.2 5.3 %collective-permute-start.20 = (f32[32,128]{1,0:T(8,128)S(1)}, f32[32,128]{1,0:T(8,128)S(1)}, u32[]{:S(2)}, u32[]{:S(2)}) collective-permute-start(f32[32,128]{1,0:T(8,128)S(1)} %shard_map.108.tile), channel_id=1, source_target_pairs={{0,5},{1,4},{2,7},{3,6},{4,1},{5,0},{6,3},{7,2},{8,13},{9,12},{10,... | collective-permute-start | bytes 49160 | tf_op jit(solution)/shard_map/ppermute | solution.py:466
  114.3 2.2 %collective-permute-start.19 = (f32[32,128]{1,0:T(8,128)S(1)}, f32[32,128]{1,0:T(8,128)S(1)}, u32[]{:S(2)}, u32[]{:S(2)}) collective-permute-start(f32[32,128]{1,0:T(8,128)S(1)} %shard_map.108.tile), channel_id=1, source_target_pairs={{0,4},{1,5},{2,6},{3,7},{4,0},{5,1},{6,2},{7,3},{8,12},{9,13},{10,... | collective-permute-start | bytes 49160 | tf_op jit(solution)/shard_map/ppermute | solution.py:466
  115.2 2.7 %collective-permute-start.18 = (f32[32,128]{1,0:T(8,128)S(1)}, f32[32,128]{1,0:T(8,128)S(1)}, u32[]{:S(2)}, u32[]{:S(2)}) collective-permute-start(f32[32,128]{1,0:T(8,128)S(1)} %shard_map.108.tile), channel_id=1, source_target_pairs={{0,1},{1,0},{2,3},{3,2},{4,5},{5,4},{6,7},{7,6},{8,9},{9,8},{10,11... | collective-permute-start | bytes 49160 | tf_op jit(solution)/shard_map/ppermute | solution.py:466
  117.9 3.9 %collective-permute-start.21 = (f32[32,128]{1,0:T(8,128)S(1)}, f32[32,128]{1,0:T(8,128)S(1)}, u32[]{:S(2)}, u32[]{:S(2)}) collective-permute-start(f32[32,128]{1,0:T(8,128)S(1)} %shard_map.109.tile), channel_id=1, source_target_pairs={{0,3},{1,2},{2,1},{3,0},{4,7},{5,6},{6,5},{7,4},{8,11},{9,10},{10,... | collective-permute-start | bytes 49160 | tf_op jit(solution)/shard_map/ppermute | solution.py:466

commit v7 on v6

--- a/solution.py
+++ b/solution.py
@@ -477,7 +477,7 @@
     wires = call(to_wire, [line] * NY, keep, rest, arrived, place)
     near = [shift(wires[by], "y", NY, by) for by in (1, NY - 1)]
     far = shift(wires[2], "y", NY, 2)
-    out = call(along_y, shape(NZ, R, HALF + LANES, dtype=BF16), wires[0], *near, far)
+    out = call(along_y, shape(NZ, R, HALF + LANES, dtype=BF16), wires[0], far, *near)
     return lax.all_to_all(out, "z", 0, 0, tiled=True)
 
 

time: 123 us -> 121 us (0.984)
  waiting for transfers between devices: 22.6 us -> 17.8 us
  blocking collectives: 43.4 us -> 45.1 us
    ppermute x6, waiting for transfers between devices: 8.71 us -> 3.9 us  [shift(): lax.ppermute(array, axis, [(i, (i + by) % length) for i in range(length)])]
    ppermute x6, starting transfers between devices: 5.51 us -> 7.91 us  [shift(): lax.ppermute(array, axis, [(i, (i + by) % length) for i in range(length)])]
    all_to_all x2, blocking collectives: 25 us -> 26.7 us  [summed(): return lax.all_to_all(out, 'z', 0, 0, tiled=True)]
    ppermute x4, starting transfers between devices: 15.4 us -> 14.1 us  [swapped(): return lax.ppermute(array, 'c', [(0, 1), (1, 0)])]
where the time goes in v7:
time: 121 us; the launch traced here: 120 us
  blocking collectives  45.1 us (37%)
  starting transfers between devices  39.2 us (32%)
  waiting for transfers between devices  17.8 us (15%)
  Pallas kernels  17.2 us (14%)
    all_to_all x2, blocking collectives, summed(): return lax.all_to_all(out, 'z', 0, 0, tiled=True)  26.7 us
    all_to_all x1, blocking collectives, shards(): lax.all_to_all(jnp.broadcast_to(margin[None], (NY * NZ, 8, 128)), ('y', '...  18.4 us
    pallas_call x25, Pallas kernels, call(): pl.pallas_call(body, out_shape=outs, in_specs=specs, out_specs=jax.tree.m...  17.2 us
    ppermute x4, starting transfers between devices, swapped(): return lax.ppermute(array, 'c', [(0, 1), (1, 0)])  14.1 us
    ppermute x8, starting transfers between devices, traded(): lax.ppermute(array, 'x', [(i, partner(i, which, stage)) for i in range(NX)])  10.2 us
    ppermute x8, waiting for transfers between devices, traded(): lax.ppermute(array, 'x', [(i, partner(i, which, stage)) for i in range(NX)])  9.69 us
    ppermute x6, starting transfers between devices, shift(): lax.ppermute(array, axis, [(i, (i + by) % length) for i in range(length)])  7.91 us
    ppermute x4, starting transfers between devices, moved(): return lax.ppermute(array, ('c', 'x'), pairs)  7.07 us
  transfers between devices with their start and end apart: 22, of which 14 were waited for; matrix products, arithmetic and copies ran while one was open for 0% of the time, Pallas kernels for 7%

profile of v7, /device:TPU:1, one launch (start us, length us, event | category | flops | bytes accessed | tf_op | source)
XLA Modules:
  0.0 120.2 jit_solution(14741116251220427560)
XLA Ops:
  0.7 4.0 %shard_map.86 = (f32[8,128]{1,0:T(8,128)S(1)}, bf16[1024,4096]{1,0:T(8,128)(2,1)S(1)}, f32[1,4096]{1,0:T(1,128)S(1)}) custom-call(bf16[1024,4096]{1,0:T(8,128)(2,1)} %source.1, bf16[32,128]{1,0:T(8,128)(2,1)} %bitcast.17, s32[1,4]{1,0:T(1,128)S(1)} %add_bitcast_fusion.place), custom_call_target="tpu_custom_call" | custom-call | bytes 4194304 | tf_op jit(solution)/shard_map/pallas_call | solution.py:34
  4.7 3.3 %collective-permute-start = (f32[8,128]{1,0:T(8,128)S(1)}, f32[8,128]{1,0:T(8,128)S(1)}, u32[]{:S(2)}, u32[]{:S(2)}) collective-permute-start(f32[8,128]{1,0:T(8,128)S(1)} %get-tuple-element.48), channel_id=1, source_target_pairs={{0,4},{4,0},{1,5},{5,1},{2,6},{6,2},{3,7},{7,3},{8,12},{12,8},{9,1... | collective-permute-start | bytes 12296 | tf_op jit(solution)/shard_map/ppermute | solution.py:470
  8.0 0.8 collective-permute-done
  8.9 18.4 %all_to_all.15.margin_parts = f32[32,8,128]{2,1,0:T(8,128)S(1)} all-to-all(f32[32,8,128]{2,1,0:T(8,128)S(1)} %broadcast_in_dim.2), channel_id=1, replica_groups=mesh['y'=4,'z'=8,'c'=2,'x'=4] {'y','z'}, dimensions={0} | all-to-all | bytes 262144 | tf_op jit(solution)/shard_map/all_to_all | solution.py:498
  27.3 0.9 shard_map.87
  28.2 1.3 %collective-permute-start.3 = (bf16[32,3072]{1,0:T(8,128)(2,1)S(1)}, bf16[32,3072]{1,0:T(8,128)(2,1)S(1)}, u32[]{:S(2)}, u32[]{:S(2)}) collective-permute-start(bf16[32,3072]{1,0:T(8,128)(2,1)S(1)} %get-tuple-element.59), channel_id=1, source_target_pairs={{0,1},{1,0},{2,3},{3,2},{4,5},{5,4},{6,7},{7,6},{8,9},{9,8},{10,11... | collective-permute-start | bytes 589832 | tf_op jit(solution)/shard_map/ppermute | solution.py:461
  29.5 0.8 shard_map.88
  30.4 1.9 %collective-permute-start.1 = (bf16[32,3072]{1,0:T(8,128)(2,1)S(1)}, bf16[32,3072]{1,0:T(8,128)(2,1)S(1)}, u32[]{:S(2)}, u32[]{:S(2)}) collective-permute-start(bf16[32,3072]{1,0:T(8,128)(2,1)S(1)} %get-tuple-element.52), channel_id=1, source_target_pairs={{0,3},{1,2},{2,1},{3,0},{4,7},{5,6},{6,5},{7,4},{8,11},{9,10},{10,... | collective-permute-start | bytes 589832 | tf_op jit(solution)/shard_map/ppermute | solution.py:461
  32.3 0.5 collective-permute-done.3.arrived
  33.0 2.6 %collective-permute-start.4 = (bf16[32,2560]{1,0:T(8,128)(2,1)S(1)}, bf16[32,2560]{1,0:T(8,128)(2,1)S(1)}, u32[]{:S(2)}, u32[]{:S(2)}) collective-permute-start(bf16[32,2560]{1,0:T(8,128)(2,1)S(1)} %get-tuple-element.61), channel_id=1, source_target_pairs={{0,3},{1,2},{2,1},{3,0},{4,7},{5,6},{6,5},{7,4},{8,11},{9,10},{10,... | collective-permute-start | bytes 491528 | tf_op jit(solution)/shard_map/ppermute | solution.py:461
  35.5 0.7 collective-permute-done.1.arrived
  36.5 0.6 shard_map.90
  37.1 3.2 %collective-permute-done.4.wire = bf16[32,2560]{1,0:T(8,128)(2,1)S(1)} collective-permute-done((bf16[32,2560]{1,0:T(8,128)(2,1)S(1)}, bf16[32,2560]{1,0:T(8,128)(2,1)S(1)}, u32[]{:S(2)}, u32[]{:S(2)}) %collective-permute-start.4) | collective-permute-done | bytes 163872 | tf_op jit(solution)/shard_map/ppermute | solution.py:461
  40.2 1.4 %shard_map.92 = (f32[32,512]{1,0:T(8,128)S(1)}, bf16[32,2048]{1,0:T(8,128)(2,1)S(1)}, f32[32,1024]{1,0:T(8,128)S(1)}, f32[32,384]{1,0:T(8,128)S(1)}) custom-call(f32[32,2048]{1,0:T(8,128)S(1)} %get-tuple-element.60.part, bf16[32,2560]{1,0:T(8,128)(2,1)S(1)} %collective-permute-done.4.wire, bf16[1024,4096]{1,0:T(8,128)(2,1)S(1)} %get-tuple-element.49.examples, ...), custom_call_target="tpu_custom_call" | custom-call | flops 134217728 | bytes 4194304 | tf_op jit(solution)/shard_map/pallas_call | solution.py:34
  41.7 0.8 shard_map.93
  42.6 5.1 %collective-permute-start.5 = (f32[32,768]{1,0:T(8,128)S(1)}, f32[32,768]{1,0:T(8,128)S(1)}, u32[]{:S(2)}, u32[]{:S(2)}) collective-permute-start(f32[32,768]{1,0:T(8,128)S(1)} %get-tuple-element.66), channel_id=1, source_target_pairs={{0,4},{4,0},{1,5},{5,1},{2,6},{6,2},{3,7},{7,3},{8,12},{12,8},{9,1... | collective-permute-start | bytes 294920 | tf_op jit(solution)/shard_map/ppermute | solution.py:470
  47.7 0.8 shard_map.94.keep
  48.8 1.2 %collective-permute-start.6 = (bf16[32,640]{1,0:T(8,128)(2,1)S(1)}, bf16[32,640]{1,0:T(8,128)(2,1)S(1)}, u32[]{:S(2)}, u32[]{:S(2)}) collective-permute-start(bf16[32,640]{1,0:T(8,128)(2,1)S(1)} %get-tuple-element.68), channel_id=1, source_target_pairs={{0,128},{64,192},{128,0},{192,64},{1,129},{65,193},{129,1},{193,65... | collective-permute-start | bytes 122888 | tf_op jit(solution)/shard_map/ppermute | solution.py:457
  50.0 0.3 collective-permute-start.7
  50.3 2.4 %collective-permute-start.8 = (bf16[32,640]{1,0:T(8,128)(2,1)S(1)}, bf16[32,640]{1,0:T(8,128)(2,1)S(1)}, u32[]{:S(2)}, u32[]{:S(2)}) collective-permute-start(bf16[32,640]{1,0:T(8,128)(2,1)S(1)} %get-tuple-element.70), channel_id=1, source_target_pairs={{0,192},{64,0},{128,64},{192,128},{1,193},{65,1},{129,65},{193,129... | collective-permute-start | bytes 122888 | tf_op jit(solution)/shard_map/ppermute | solution.py:457
  52.7 0.5 collective-permute-done.6.wire1
  53.2 1.4 %collective-permute-done.7.wire2 = bf16[32,640]{1,0:T(8,128)(2,1)S(1)} collective-permute-done((bf16[32,640]{1,0:T(8,128)(2,1)S(1)}, bf16[32,640]{1,0:T(8,128)(2,1)S(1)}, u32[]{:S(2)}, u32[]{:S(2)}) %collective-permute-start.7) | collective-permute-done | bytes 40992 | tf_op jit(solution)/shard_map/ppermute | solution.py:457
  54.8 13.6 %all_to_all.16.arrived = bf16[8,32,640]{2,1,0:T(8,128)(2,1)S(1)} all-to-all(bf16[8,32,640]{2,1,0:T(8,128)(2,1)S(1)} %shard_map.96), channel_id=1, replica_groups=mesh['y'=4,'z'=8,'c'=2,'x'=4] {'z'}, dimensions={0} | all-to-all | bytes 655360 | tf_op jit(solution)/shard_map/all_to_all | solution.py:481
  68.7 3.3 %collective-permute-start.9 = (bf16[32,640]{1,0:T(8,128)(2,1)S(1)}, bf16[32,640]{1,0:T(8,128)(2,1)S(1)}, u32[]{:S(2)}, u32[]{:S(2)}) collective-permute-start(bf16[32,640]{1,0:T(8,128)(2,1)S(1)} %get-tuple-element.72.weighted), channel_id=1, source_target_pairs={{0,4},{4,0},{1,5},{5,1},{2,6},{6,2},{3,7},{7,3},{8,12},{12,8},{9,1... | collective-permute-start | bytes 122888 | tf_op jit(solution)/shard_map/ppermute | solution.py:470
  71.9 0.9 shard_map.98
  72.9 0.6 shard_map.101.mine
  73.5 0.6 shard_map.99.mine
  74.1 2.1 %collective-permute-start.10 = (bf16[32,2048]{1,0:T(8,128)(2,1)S(1)}, bf16[32,2048]{1,0:T(8,128)(2,1)S(1)}, u32[]{:S(2)}, u32[]{:S(2)}) collective-permute-start(bf16[32,2048]{1,0:T(8,128)(2,1)S(1)} %shard_map.99.mine), channel_id=1, source_target_pairs={{0,3},{1,2},{2,1},{3,0},{4,7},{5,6},{6,5},{7,4},{8,11},{9,10},{10,... | collective-permute-start | bytes 393224 | tf_op jit(solution)/shard_map/ppermute | solution.py:461
  76.1 2.3 %collective-permute-done.12.other = bf16[32,2176]{1,0:T(8,128)(2,1)S(1)} collective-permute-done((bf16[32,2176]{1,0:T(8,128)(2,1)S(1)}, bf16[32,2176]{1,0:T(8,128)(2,1)S(1)}, u32[]{:S(2)}, u32[]{:S(2)}) %collective-permute-start.12) | collective-permute-done | bytes 139296 | tf_op jit(solution)/shard_map/ppermute | solution.py:461
  78.6 2.1 %collective-permute-start.13 = (bf16[32,2176]{1,0:T(8,128)(2,1)S(1)}, bf16[32,2176]{1,0:T(8,128)(2,1)S(1)}, u32[]{:S(2)}, u32[]{:S(2)}) collective-permute-start(bf16[32,2176]{1,0:T(8,128)(2,1)S(1)} %shard_map.102.mine), channel_id=1, source_target_pairs={{0,3},{1,2},{2,1},{3,0},{4,7},{5,6},{6,5},{7,4},{8,11},{9,10},{10,... | collective-permute-start | bytes 417800 | tf_op jit(solution)/shard_map/ppermute | solution.py:461
  80.9 2.9 %collective-permute-done.13.other = bf16[32,2176]{1,0:T(8,128)(2,1)S(1)} collective-permute-done((bf16[32,2176]{1,0:T(8,128)(2,1)S(1)}, bf16[32,2176]{1,0:T(8,128)(2,1)S(1)}, u32[]{:S(2)}, u32[]{:S(2)}) %collective-permute-start.13) | collective-permute-done | bytes 139296 | tf_op jit(solution)/shard_map/ppermute | solution.py:461
  83.8 1.6 %shard_map.103 = (f32[32,512]{1,0:T(8,128)S(1)}, f32[32,1024]{1,0:T(8,128)S(1)}, f32[32,384]{1,0:T(8,128)S(1)}, f32[32,128]{1,0:T(8,128)S(1)}) custom-call(bf16[32,2176]{1,0:T(8,128)(2,1)S(1)} %shard_map.102.mine, bf16[32,2176]{1,0:T(8,128)(2,1)S(1)} %collective-permute-done.13.other, f32[32,512]{1,0:T(8,128)S(1)} %get-tuple-element.77.rhs.rhs_a, ...), custom_call_target="tpu_custom_call" | custom-call | flops 134217728 | bytes 4194304 | tf_op jit(solution)/shard_map/pallas_call | solution.py:34
  85.4 0.9 shard_map.104
  86.3 2.3 %collective-permute-start.14 = (f32[32,768]{1,0:T(8,128)S(1)}, f32[32,768]{1,0:T(8,128)S(1)}, u32[]{:S(2)}, u32[]{:S(2)}) collective-permute-start(f32[32,768]{1,0:T(8,128)S(1)} %get-tuple-element.84), channel_id=1, source_target_pairs={{0,4},{4,0},{1,5},{5,1},{2,6},{6,2},{3,7},{7,3},{8,12},{12,8},{9,1... | collective-permute-start | bytes 294920 | tf_op jit(solution)/shard_map/ppermute | solution.py:470
  88.6 0.8 shard_map.105.keep
  89.7 1.3 %collective-permute-start.15 = (bf16[32,640]{1,0:T(8,128)(2,1)S(1)}, bf16[32,640]{1,0:T(8,128)(2,1)S(1)}, u32[]{:S(2)}, u32[]{:S(2)}) collective-permute-start(bf16[32,640]{1,0:T(8,128)(2,1)S(1)} %get-tuple-element.86), channel_id=1, source_target_pairs={{0,128},{64,192},{128,0},{192,64},{1,129},{65,193},{129,1},{193,65... | collective-permute-start | bytes 122888 | tf_op jit(solution)/shard_map/ppermute | solution.py:457
  91.0 1.4 %collective-permute-start.16 = (bf16[32,640]{1,0:T(8,128)(2,1)S(1)}, bf16[32,640]{1,0:T(8,128)(2,1)S(1)}, u32[]{:S(2)}, u32[]{:S(2)}) collective-permute-start(bf16[32,640]{1,0:T(8,128)(2,1)S(1)} %get-tuple-element.87), channel_id=1, source_target_pairs={{0,64},{64,128},{128,192},{192,0},{1,65},{65,129},{129,193},{193,1... | collective-permute-start | bytes 122888 | tf_op jit(solution)/shard_map/ppermute | solution.py:457
  92.4 1.3 %collective-permute-start.17 = (bf16[32,640]{1,0:T(8,128)(2,1)S(1)}, bf16[32,640]{1,0:T(8,128)(2,1)S(1)}, u32[]{:S(2)}, u32[]{:S(2)}) collective-permute-start(bf16[32,640]{1,0:T(8,128)(2,1)S(1)} %get-tuple-element.88), channel_id=1, source_target_pairs={{0,192},{64,0},{128,64},{192,128},{1,193},{65,1},{129,65},{193,129... | collective-permute-start | bytes 122888 | tf_op jit(solution)/shard_map/ppermute | solution.py:457
  93.7 0.4 collective-permute-done.15.wire1
  94.1 1.5 %collective-permute-done.16.wire2 = bf16[32,640]{1,0:T(8,128)(2,1)S(1)} collective-permute-done((bf16[32,640]{1,0:T(8,128)(2,1)S(1)}, bf16[32,640]{1,0:T(8,128)(2,1)S(1)}, u32[]{:S(2)}, u32[]{:S(2)}) %collective-permute-start.16) | collective-permute-done | bytes 40992 | tf_op jit(solution)/shard_map/ppermute | solution.py:457
  95.8 13.1 %all_to_all.17.arrived = bf16[8,32,640]{2,1,0:T(8,128)(2,1)S(1)} all-to-all(bf16[8,32,640]{2,1,0:T(8,128)(2,1)S(1)} %shard_map.107), channel_id=1, replica_groups=mesh['y'=4,'z'=8,'c'=2,'x'=4] {'z'}, dimensions={0} | all-to-all | bytes 655360 | tf_op jit(solution)/shard_map/all_to_all | solution.py:481
  109.1 2.8 %collective-permute-start.20 = (f32[32,128]{1,0:T(8,128)S(1)}, f32[32,128]{1,0:T(8,128)S(1)}, u32[]{:S(2)}, u32[]{:S(2)}) collective-permute-start(f32[32,128]{1,0:T(8,128)S(1)} %shard_map.108.tile), channel_id=1, source_target_pairs={{0,5},{1,4},{2,7},{3,6},{4,1},{5,0},{6,3},{7,2},{8,13},{9,12},{10,... | collective-permute-start | bytes 49160 | tf_op jit(solution)/shard_map/ppermute | solution.py:466
  111.9 0.9 collective-permute-start.19
  112.8 1.3 %collective-permute-start.18 = (f32[32,128]{1,0:T(8,128)S(1)}, f32[32,128]{1,0:T(8,128)S(1)}, u32[]{:S(2)}, u32[]{:S(2)}) collective-permute-start(f32[32,128]{1,0:T(8,128)S(1)} %shard_map.108.tile), channel_id=1, source_target_pairs={{0,1},{1,0},{2,3},{3,2},{4,5},{5,4},{6,7},{7,6},{8,9},{9,8},{10,11... | collective-permute-start | bytes 49160 | tf_op jit(solution)/shard_map/ppermute | solution.py:466
  114.1 1.4 %collective-permute-done.18.near = f32[32,128]{1,0:T(8,128)S(1)} collective-permute-done((f32[32,128]{1,0:T(8,128)S(1)}, f32[32,128]{1,0:T(8,128)S(1)}, u32[]{:S(2)}, u32[]{:S(2)}) %collective-permute-start.18) | collective-permute-done | bytes 16416 | tf_op jit(solution)/shard_map/ppermute | solution.py:466
  115.5 2.2 %collective-permute-start.21 = (f32[32,128]{1,0:T(8,128)S(1)}, f32[32,128]{1,0:T(8,128)S(1)}, u32[]{:S(2)}, u32[]{:S(2)}) collective-permute-start(f32[32,128]{1,0:T(8,128)S(1)} %shard_map.109.tile), channel_id=1, source_target_pairs={{0,3},{1,2},{2,1},{3,0},{4,7},{5,6},{6,5},{7,4},{8,11},{9,10},{10,... | collective-permute-start | bytes 49160 | tf_op jit(solution)/shard_map/ppermute | solution.py:466
  117.6 1.7 %collective-permute-done.21.far = f32[32,128]{1,0:T(8,128)S(1)} collective-permute-done((f32[32,128]{1,0:T(8,128)S(1)}, f32[32,128]{1,0:T(8,128)S(1)}, u32[]{:S(2)}, u32[]{:S(2)}) %collective-permute-start.21) | collective-permute-done | bytes 16416 | tf_op jit(solution)/shard_map/ppermute | solution.py:466
  119.4 0.9 shard_map.110
  (37 shorter events, 2.2 us)
Async XLA Ops:
  0.6 26.7 %copy-start = (f32[32,1024]{1,0:T(8,128)S(1)}, f32[32,1024]{1,0:T(8,128)}, u32[]{:S(2)}) copy-start(f32[32,1024]{1,0:T(8,128)} %val_weight.1) | copy-start | bytes 393220
  0.6 26.7 %copy-start.3 = (s32[1024]{0:T(1024)S(1)}, s32[1024]{0:T(1024)}, u32[]{:S(2)}) copy-start(s32[1024]{0:T(1024)} %param.10) | copy-start | bytes 12292
  0.7 26.7 %copy-start.2 = (s32[1024]{0:T(1024)S(1)}, s32[1024]{0:T(1024)}, u32[]{:S(2)}) copy-start(s32[1024]{0:T(1024)} %param.9) | copy-start | bytes 12292
  4.7 4.2 %collective-permute-start = (f32[8,128]{1,0:T(8,128)S(1)}, f32[8,128]{1,0:T(8,128)S(1)}, u32[]{:S(2)}, u32[]{:S(2)}) collective-permute-start(f32[8,128]{1,0:T(8,128)S(1)} %get-tuple-element.48), channel_id=1, source_target_pairs={{0,4},{4,0},{1,5},{5,1},{2,6},{6,2},{3,7},{7,3},{8,12},{12,8},{9,1... | collective-permute-start | bytes 12296 | tf_op jit(solution)/shard_map/ppermute | solution.py:470
  27.3 9.1 %copy-start.1 = (s32[4096]{0:T(1024)S(1)}, s32[4096]{0:T(1024)}, u32[]{:S(2)}) copy-start(s32[4096]{0:T(1024)} %param.13) | copy-start | bytes 49156
  27.3 9.1 %copy-start.4 = (f32[256]{0:T(256)S(1)}, f32[256]{0:T(256)}, u32[]{:S(2)}) copy-start(f32[256]{0:T(256)} %param.12) | copy-start | bytes 3076
  28.2 4.6 %collective-permute-start.3 = (bf16[32,3072]{1,0:T(8,128)(2,1)S(1)}, bf16[32,3072]{1,0:T(8,128)(2,1)S(1)}, u32[]{:S(2)}, u32[]{:S(2)}) collective-permute-start(bf16[32,3072]{1,0:T(8,128)(2,1)S(1)} %get-tuple-element.59), channel_id=1, source_target_pairs={{0,1},{1,0},{2,3},{3,2},{4,5},{5,4},{6,7},{7,6},{8,9},{9,8},{10,11... | collective-permute-start | bytes 589832 | tf_op jit(solution)/shard_map/ppermute | solution.py:461
  30.4 5.8 %collective-permute-start.1 = (bf16[32,3072]{1,0:T(8,128)(2,1)S(1)}, bf16[32,3072]{1,0:T(8,128)(2,1)S(1)}, u32[]{:S(2)}, u32[]{:S(2)}) collective-permute-start(bf16[32,3072]{1,0:T(8,128)(2,1)S(1)} %get-tuple-element.52), channel_id=1, source_target_pairs={{0,3},{1,2},{2,1},{3,0},{4,7},{5,6},{6,5},{7,4},{8,11},{9,10},{10,... | collective-permute-start | bytes 589832 | tf_op jit(solution)/shard_map/ppermute | solution.py:461
  33.0 7.3 %collective-permute-start.4 = (bf16[32,2560]{1,0:T(8,128)(2,1)S(1)}, bf16[32,2560]{1,0:T(8,128)(2,1)S(1)}, u32[]{:S(2)}, u32[]{:S(2)}) collective-permute-start(bf16[32,2560]{1,0:T(8,128)(2,1)S(1)} %get-tuple-element.61), channel_id=1, source_target_pairs={{0,3},{1,2},{2,1},{3,0},{4,7},{5,6},{6,5},{7,4},{8,11},{9,10},{10,... | collective-permute-start | bytes 491528 | tf_op jit(solution)/shard_map/ppermute | solution.py:461
  36.3 5.4 %collective-permute-start.2 = (bf16[32,2560]{1,0:T(8,128)(2,1)S(1)}, bf16[32,2560]{1,0:T(8,128)(2,1)S(1)}, u32[]{:S(2)}, u32[]{:S(2)}) collective-permute-start(bf16[32,2560]{1,0:T(8,128)(2,1)S(1)} %get-tuple-element.54), channel_id=1, source_target_pairs={{0,1},{1,0},{2,3},{3,2},{4,5},{5,4},{6,7},{7,6},{8,9},{9,8},{10,11... | collective-permute-start | bytes 491528 | tf_op jit(solution)/shard_map/ppermute | solution.py:461
  42.6 6.1 %collective-permute-start.5 = (f32[32,768]{1,0:T(8,128)S(1)}, f32[32,768]{1,0:T(8,128)S(1)}, u32[]{:S(2)}, u32[]{:S(2)}) collective-permute-start(f32[32,768]{1,0:T(8,128)S(1)} %get-tuple-element.66), channel_id=1, source_target_pairs={{0,4},{4,0},{1,5},{5,1},{2,6},{6,2},{3,7},{7,3},{8,12},{12,8},{9,1... | collective-permute-start | bytes 294920 | tf_op jit(solution)/shard_map/ppermute | solution.py:470
  48.8 4.4 %collective-permute-start.6 = (bf16[32,640]{1,0:T(8,128)(2,1)S(1)}, bf16[32,640]{1,0:T(8,128)(2,1)S(1)}, u32[]{:S(2)}, u32[]{:S(2)}) collective-permute-start(bf16[32,640]{1,0:T(8,128)(2,1)S(1)} %get-tuple-element.68), channel_id=1, source_target_pairs={{0,128},{64,192},{128,0},{192,64},{1,129},{65,193},{129,1},{193,65... | collective-permute-start | bytes 122888 | tf_op jit(solution)/shard_map/ppermute | solution.py:457
  50.0 4.7 %collective-permute-start.7 = (bf16[32,640]{1,0:T(8,128)(2,1)S(1)}, bf16[32,640]{1,0:T(8,128)(2,1)S(1)}, u32[]{:S(2)}, u32[]{:S(2)}) collective-permute-start(bf16[32,640]{1,0:T(8,128)(2,1)S(1)} %get-tuple-element.69), channel_id=1, source_target_pairs={{0,64},{64,128},{128,192},{192,0},{1,65},{65,129},{129,193},{193,1... | collective-permute-start | bytes 122888 | tf_op jit(solution)/shard_map/ppermute | solution.py:457
  50.3 4.3 %collective-permute-start.8 = (bf16[32,640]{1,0:T(8,128)(2,1)S(1)}, bf16[32,640]{1,0:T(8,128)(2,1)S(1)}, u32[]{:S(2)}, u32[]{:S(2)}) collective-permute-start(bf16[32,640]{1,0:T(8,128)(2,1)S(1)} %get-tuple-element.70), channel_id=1, source_target_pairs={{0,192},{64,0},{128,64},{192,128},{1,193},{65,1},{129,65},{193,129... | collective-permute-start | bytes 122888 | tf_op jit(solution)/shard_map/ppermute | solution.py:457
  68.7 4.2 %collective-permute-start.9 = (bf16[32,640]{1,0:T(8,128)(2,1)S(1)}, bf16[32,640]{1,0:T(8,128)(2,1)S(1)}, u32[]{:S(2)}, u32[]{:S(2)}) collective-permute-start(bf16[32,640]{1,0:T(8,128)(2,1)S(1)} %get-tuple-element.72.weighted), channel_id=1, source_target_pairs={{0,4},{4,0},{1,5},{5,1},{2,6},{6,2},{3,7},{7,3},{8,12},{12,8},{9,1... | collective-permute-start | bytes 122888 | tf_op jit(solution)/shard_map/ppermute | solution.py:470
  73.5 5.0 %collective-permute-start.12 = (bf16[32,2176]{1,0:T(8,128)(2,1)S(1)}, bf16[32,2176]{1,0:T(8,128)(2,1)S(1)}, u32[]{:S(2)}, u32[]{:S(2)}) collective-permute-start(bf16[32,2176]{1,0:T(8,128)(2,1)S(1)} %shard_map.101.mine), channel_id=1, source_target_pairs={{0,1},{1,0},{2,3},{3,2},{4,5},{5,4},{6,7},{7,6},{8,9},{9,8},{10,11... | collective-permute-start | bytes 417800 | tf_op jit(solution)/shard_map/ppermute | solution.py:461
  74.1 6.7 %collective-permute-start.10 = (bf16[32,2048]{1,0:T(8,128)(2,1)S(1)}, bf16[32,2048]{1,0:T(8,128)(2,1)S(1)}, u32[]{:S(2)}, u32[]{:S(2)}) collective-permute-start(bf16[32,2048]{1,0:T(8,128)(2,1)S(1)} %shard_map.99.mine), channel_id=1, source_target_pairs={{0,3},{1,2},{2,1},{3,0},{4,7},{5,6},{6,5},{7,4},{8,11},{9,10},{10,... | collective-permute-start | bytes 393224 | tf_op jit(solution)/shard_map/ppermute | solution.py:461
  78.6 5.2 %collective-permute-start.13 = (bf16[32,2176]{1,0:T(8,128)(2,1)S(1)}, bf16[32,2176]{1,0:T(8,128)(2,1)S(1)}, u32[]{:S(2)}, u32[]{:S(2)}) collective-permute-start(bf16[32,2176]{1,0:T(8,128)(2,1)S(1)} %shard_map.102.mine), channel_id=1, source_target_pairs={{0,3},{1,2},{2,1},{3,0},{4,7},{5,6},{6,5},{7,4},{8,11},{9,10},{10,... | collective-permute-start | bytes 417800 | tf_op jit(solution)/shard_map/ppermute | solution.py:461
  80.8 4.6 %collective-permute-start.11 = (bf16[32,2048]{1,0:T(8,128)(2,1)S(1)}, bf16[32,2048]{1,0:T(8,128)(2,1)S(1)}, u32[]{:S(2)}, u32[]{:S(2)}) collective-permute-start(bf16[32,2048]{1,0:T(8,128)(2,1)S(1)} %shard_map.100.mine), channel_id=1, source_target_pairs={{0,1},{1,0},{2,3},{3,2},{4,5},{5,4},{6,7},{7,6},{8,9},{9,8},{10,11... | collective-permute-start | bytes 393224 | tf_op jit(solution)/shard_map/ppermute | solution.py:461
  86.3 3.3 %collective-permute-start.14 = (f32[32,768]{1,0:T(8,128)S(1)}, f32[32,768]{1,0:T(8,128)S(1)}, u32[]{:S(2)}, u32[]{:S(2)}) collective-permute-start(f32[32,768]{1,0:T(8,128)S(1)} %get-tuple-element.84), channel_id=1, source_target_pairs={{0,4},{4,0},{1,5},{5,1},{2,6},{6,2},{3,7},{7,3},{8,12},{12,8},{9,1... | collective-permute-start | bytes 294920 | tf_op jit(solution)/shard_map/ppermute | solution.py:470
  89.7 4.4 %collective-permute-start.15 = (bf16[32,640]{1,0:T(8,128)(2,1)S(1)}, bf16[32,640]{1,0:T(8,128)(2,1)S(1)}, u32[]{:S(2)}, u32[]{:S(2)}) collective-permute-start(bf16[32,640]{1,0:T(8,128)(2,1)S(1)} %get-tuple-element.86), channel_id=1, source_target_pairs={{0,128},{64,192},{128,0},{192,64},{1,129},{65,193},{129,1},{193,65... | collective-permute-start | bytes 122888 | tf_op jit(solution)/shard_map/ppermute | solution.py:457
  91.0 4.6 %collective-permute-start.16 = (bf16[32,640]{1,0:T(8,128)(2,1)S(1)}, bf16[32,640]{1,0:T(8,128)(2,1)S(1)}, u32[]{:S(2)}, u32[]{:S(2)}) collective-permute-start(bf16[32,640]{1,0:T(8,128)(2,1)S(1)} %get-tuple-element.87), channel_id=1, source_target_pairs={{0,64},{64,128},{128,192},{192,0},{1,65},{65,129},{129,193},{193,1... | collective-permute-start | bytes 122888 | tf_op jit(solution)/shard_map/ppermute | solution.py:457
  92.4 3.2 %collective-permute-start.17 = (bf16[32,640]{1,0:T(8,128)(2,1)S(1)}, bf16[32,640]{1,0:T(8,128)(2,1)S(1)}, u32[]{:S(2)}, u32[]{:S(2)}) collective-permute-start(bf16[32,640]{1,0:T(8,128)(2,1)S(1)} %get-tuple-element.88), channel_id=1, source_target_pairs={{0,192},{64,0},{128,64},{192,128},{1,193},{65,1},{129,65},{193,129... | collective-permute-start | bytes 122888 | tf_op jit(solution)/shard_map/ppermute | solution.py:457
  109.1 4.9 %collective-permute-start.20 = (f32[32,128]{1,0:T(8,128)S(1)}, f32[32,128]{1,0:T(8,128)S(1)}, u32[]{:S(2)}, u32[]{:S(2)}) collective-permute-start(f32[32,128]{1,0:T(8,128)S(1)} %shard_map.108.tile), channel_id=1, source_target_pairs={{0,5},{1,4},{2,7},{3,6},{4,1},{5,0},{6,3},{7,2},{8,13},{9,12},{10,... | collective-permute-start | bytes 49160 | tf_op jit(solution)/shard_map/ppermute | solution.py:466
  111.9 2.2 %collective-permute-start.19 = (f32[32,128]{1,0:T(8,128)S(1)}, f32[32,128]{1,0:T(8,128)S(1)}, u32[]{:S(2)}, u32[]{:S(2)}) collective-permute-start(f32[32,128]{1,0:T(8,128)S(1)} %shard_map.108.tile), channel_id=1, source_target_pairs={{0,4},{1,5},{2,6},{3,7},{4,0},{5,1},{6,2},{7,3},{8,12},{9,13},{10,... | collective-permute-start | bytes 49160 | tf_op jit(solution)/shard_map/ppermute | solution.py:466
  112.8 2.7 %collective-permute-start.18 = (f32[32,128]{1,0:T(8,128)S(1)}, f32[32,128]{1,0:T(8,128)S(1)}, u32[]{:S(2)}, u32[]{:S(2)}) collective-permute-start(f32[32,128]{1,0:T(8,128)S(1)} %shard_map.108.tile), channel_id=1, source_target_pairs={{0,1},{1,0},{2,3},{3,2},{4,5},{5,4},{6,7},{7,6},{8,9},{9,8},{10,11... | collective-permute-start | bytes 49160 | tf_op jit(solution)/shard_map/ppermute | solution.py:466
  115.5 3.9 %collective-permute-start.21 = (f32[32,128]{1,0:T(8,128)S(1)}, f32[32,128]{1,0:T(8,128)S(1)}, u32[]{:S(2)}, u32[]{:S(2)}) collective-permute-start(f32[32,128]{1,0:T(8,128)S(1)} %shard_map.109.tile), channel_id=1, source_target_pairs={{0,3},{1,2},{2,1},{3,0},{4,7},{5,6},{6,5},{7,4},{8,11},{9,10},{10,... | collective-permute-start | bytes 49160 | tf_op jit(solution)/shard_map/ppermute | solution.py:466
